TPU v7x, 512 devices: a whole 4x8x8 slice. The times are simulated.
512 devices in a mesh: dp: 128 (over z, y, core), grp: 4 (over x).
Axes of the slice: x: 4, y: 8, z: 8, core: 2. Of those that a mesh axis runs over, the one named last changes fastest.
Arguments:
- embeddings: bfloat16 [65536, 768], P(('dp', 'grp')), may hold values from -6 to 6
- inv_temp: bfloat16 [65536], P(('dp', 'grp')), may hold values from 4 to 16
- cluster: int32 [65536, 1], P(('dp', 'grp')), may hold values from 0 to 127; in each aligned block of 128 rows (0 to 127, 128 to 255, ...) at most 2 rows name the same one
Outputs:
- neighbour: bfloat16 [65536, 768], P(('dp', 'grp'))
- duplicate_mass: bfloat16 [65536], P(('dp', 'grp'))
Inputs may be any that keep to these rules, and one draw needn't show every extreme that they name: Among the 128 rows of one device no cluster is named more than 2 times, a bound that some block reaches.
All inputs are finite; a program needn't handle non-finite values.
Results may differ from a plain program's by a relative error of at most 0.011.
Values may be sent and summed in bfloat16 or wider, within the bound.
No kernel may reach another device: no remote copies, remote signals or barrier semaphores. Data moves between devices by JAX's collectives and lax.ppermute only.
A program may use at most 64 MiB of HBM per device.

v0:
```python
import math

import jax
import jax.numpy as jnp
from jax import lax
from jax.sharding import PartitionSpec as P

NEIGH_SCALE = 8.0


def normalize(embeddings):
    values = embeddings.astype(jnp.float32)
    square_mean = jnp.mean(values * values, axis=1, keepdims=True)
    return (
        values * lax.rsqrt(square_mean + 1e-06) * (1.0 / math.sqrt(embeddings.shape[1]))
    ).astype(jnp.bfloat16)


def weigh_tile(query_unit, query_temp, query_start, key_unit, key_temp):
    cosine = lax.dot_general(
        query_unit, key_unit, (((1,), (1,)), ((), ())), preferred_element_type=jnp.float32
    )
    key_float = key_temp.astype(jnp.float32)
    query_float = query_temp.astype(jnp.float32)
    temper = (query_float[:, None] + key_float[None, :]) * 0.5
    query_index = query_start + jnp.arange(query_unit.shape[0], dtype=jnp.int32)
    key_index = jnp.arange(key_unit.shape[0], dtype=jnp.int32)
    allowed = (
        (key_float[None, :] > 0.0)
        & (query_float[:, None] > 0.0)
        & (query_index[:, None] != key_index[None, :])
    )
    return jnp.where(allowed, jnp.exp((cosine - 1.0) * temper), 0.0)


def shards(embeddings, inv_temp, cluster):
    row_count, feat_width = embeddings.shape
    dp_count = lax.axis_size("dp")
    capacity = max(2, 2 * row_count // dp_count)
    slot_count = dp_count * capacity
    unit_rows = normalize(embeddings)
    target = cluster[:, 0]
    matches = (target[:, None] == jnp.arange(dp_count, dtype=jnp.int32)[None, :]).astype(jnp.int32)
    earlier = jnp.cumsum(matches, axis=0) - matches
    slot_rank = jnp.sum(earlier * matches, axis=1)
    position = target * capacity + slot_rank
    send_unit = jnp.zeros((slot_count, feat_width), jnp.bfloat16).at[position].set(unit_rows)
    send_temp = jnp.zeros((slot_count,), jnp.bfloat16).at[position].set(inv_temp)
    recv_unit, recv_temp = (
        lax.all_to_all(
            send_unit.reshape(dp_count, capacity, feat_width),
            "dp",
            split_axis=0,
            concat_axis=0,
            tiled=True,
        ),
        lax.all_to_all(
            send_temp.reshape(dp_count, capacity), "dp", split_axis=0, concat_axis=0, tiled=True
        ),
    )
    query_unit = recv_unit.reshape(slot_count, feat_width)
    query_temp = recv_temp.reshape(slot_count)
    group_index = lax.axis_index("grp")
    own_start = group_index * slot_count
    piece = (
        lax.all_gather(query_unit, "grp", axis=0, tiled=True),
        lax.all_gather(query_temp, "grp", axis=0, tiled=True),
    )
    tile_weight = weigh_tile(query_unit, query_temp, own_start, piece[0], piece[1])
    mass_part = jnp.sum(tile_weight, axis=1)
    sum_part = jnp.dot(
        tile_weight.astype(jnp.bfloat16), piece[0], preferred_element_type=jnp.float32
    )
    neigh = (NEIGH_SCALE * math.sqrt(feat_width) * sum_part / (1.0 + mass_part)[:, None]).astype(
        jnp.bfloat16
    )
    mass_rounded = mass_part.astype(jnp.bfloat16)
    back_neigh, back_dup = (
        lax.all_to_all(
            neigh.reshape(dp_count, capacity, feat_width),
            "dp",
            split_axis=0,
            concat_axis=0,
            tiled=True,
        ),
        lax.all_to_all(
            mass_rounded.reshape(dp_count, capacity), "dp", split_axis=0, concat_axis=0, tiled=True
        ),
    )
    neighbour = back_neigh.reshape(slot_count, feat_width)[position]
    duplicate_mass = back_dup.reshape(slot_count)[position]
    return (neighbour, duplicate_mass)


def solution(mesh):
    placed = (P(("dp", "grp"), None), P(("dp", "grp")), P(("dp", "grp"), None))
    return jax.shard_map(
        shards,
        mesh=mesh,
        in_specs=placed,
        out_specs=(P(("dp", "grp"), None), P(("dp", "grp"))),
        check_vma=False,
    )
```

profile of v0, /device:TPU:1, one launch (start us, length us, event | category | flops | bytes accessed | tf_op | source)
XLA Modules:
  0.0 135.3 jit_solution(2277095667952706912)
XLA Ops:
  7.2 0.0 all-gather.3.cloned.1.call-start
  7.2 0.7 fusion.15
  8.0 0.2 reduce_window_sum.11
  8.1 0.8 select_reduce_fusion
  9.0 0.7 fusion.16
  9.6 1.0 fusion.7
  10.7 1.7 %scatter_custom_fusion.1 = bf16[256,768]{1,0:T(8,128)(2,1)S(1)} fusion(s32[128]{0:T(128)S(1)} %fusion.16, bf16[128,768]{1,0:T(8,128)(2,1)} %param.3, f32[]{:T(128)} %constant.7.clone.1, f32[128]{0:T(128)S(1)} %add_rsqrt_fusion, bf16[]{:T(256)} %constant.13.clone.1), kind=kCustom, calls=%fused_computation.19 | custom fusion | flops 393216 | bytes 590342 | tf_op jit(solution)/shard_map/scatter | solution.py:47
  12.4 0.1 reshape.75
  12.6 36.1 %all_to_all.26 = bf16[128,2,768]{2,1,0:T(2,128)(2,1)S(1)} all-to-all(bf16[128,2,768]{2,1,0:T(2,128)(2,1)S(1)} %reshape.75), channel_id=1, replica_groups=mesh['dp'=128,'grp'=4] {'dp'}, dimensions={0} | all-to-all | bytes 786432 | tf_op jit(solution)/shard_map/all_to_all | solution.py:50
  48.7 0.9 reshape.76
  49.6 1.5 %scatter_custom_fusion = bf16[256]{0:T(256)(128)(2,1)S(1)} fusion(s32[128]{0:T(128)S(1)} %fusion.16, bf16[128]{0:T(256)(128)(2,1)} %param.4, bf16[]{:T(256)} %constant.13.clone.1), kind=kCustom, calls=%fused_computation.36 | custom fusion | bytes 1024 | tf_op jit(solution)/shard_map/scatter | solution.py:48
  51.1 0.8 all_to_all.21
  51.9 5.3 %all-to-all-start = ((bf16[128,1,2]{2,1,0:T(2,128)(2,1)}), bf16[128,1,2]{2,1,0:T(2,128)(2,1)S(1)}, u32[]{:S(2)}, u32[]{:S(2)}) async-start(bf16[128,1,2]{2,1,0:T(2,128)(2,1)} %all_to_all.21), calls=%async_computation | async-start | bytes 131072 | tf_op jit(solution)/shard_map/all_to_all | solution.py:57
  57.2 11.5 %all-to-all-done = bf16[128,1,2]{2,1,0:T(2,128)(2,1)S(1)} async-done(((bf16[128,1,2]{2,1,0:T(2,128)(2,1)}), bf16[128,1,2]{2,1,0:T(2,128)(2,1)S(1)}, u32[]{:S(2)}, u32[]{:S(2)}) %all-to-all-start) | async-done | bytes 544 | tf_op jit(solution)/shard_map/all_to_all | solution.py:57
  68.7 0.2 convert_reduce_fusion
  68.9 0.1 reshape.116
  69.0 0.2 reduce
  69.2 0.1 reshape.112
  69.4 7.7 %all-gather = bf16[4,1,256]{2,1,0:T(2,128)(2,1)S(1)} all-gather(bf16[1,1,256]{2,1,0:T(2,128)(2,1)S(1)} %reshape.112), channel_id=1, replica_groups=mesh['dp'=128,'grp'=4] {'grp'}, dimensions={0}, use_global_device_ids=true | all-gather | bytes 2560 | tf_op jit(solution)/shard_map/all_gather | solution.py:67
  77.1 2.5 %fusion.20 = (f32[256]{0:T(256)S(1)}, bf16[256,1024]{1,0:T(8,128)(2,1)S(1)}) fusion(f32[1024]{0:T(1024)S(1)} %bitcast.13, f32[256]{0:T(256)S(1)} %reshape.116, bf16[256,768]{1,0:T(8,128)(2,1)} %reshape.76, bf16[1024,768]{1,0:T(8,128)(2,1)} %all-gather.3.cloned.1.call-done, s32[256]{0:T(256)S(1)} %iota_add_fusion, ...), kind=kOutput, calls=%fused_computation.39 | convolution fusion | flops 405274368 | bytes 2498816 | tf_op jit(solution)/shard_map/dot_general | solution.py:20
  79.7 0.8 convert_element_type.53
  80.5 11.1 %all-to-all-start.3 = ((bf16[128,1,2]{2,1,0:T(2,128)(2,1)}), bf16[128,1,2]{2,1,0:T(2,128)(2,1)S(1)}, u32[]{:S(2)}, u32[]{:S(2)}) async-start(bf16[128,1,2]{2,1,0:T(2,128)(2,1)} %convert_element_type.53), calls=%async_computation.3 | async-start | bytes 131072 | tf_op jit(solution)/shard_map/all_to_all | solution.py:86
  91.6 0.6 fusion.4
  92.2 0.9 reshape.77
  93.1 9.9 %all-to-all-done.3 = bf16[128,1,2]{2,1,0:T(2,128)(2,1)S(1)} async-done(((bf16[128,1,2]{2,1,0:T(2,128)(2,1)}), bf16[128,1,2]{2,1,0:T(2,128)(2,1)S(1)}, u32[]{:S(2)}, u32[]{:S(2)}) %all-to-all-start.3) | async-done | bytes 544 | tf_op jit(solution)/shard_map/all_to_all | solution.py:86
  103.0 5.8 %all-to-all-start.2 = ((bf16[128,2,768]{2,1,0:T(2,128)(2,1)}), bf16[128,2,768]{2,1,0:T(2,128)(2,1)S(1)}, u32[]{:S(2)}, u32[]{:S(2)}) async-start(bf16[128,2,768]{2,1,0:T(2,128)(2,1)} %reshape.77), calls=%async_computation.2 | async-start | bytes 786432 | tf_op jit(solution)/shard_map/all_to_all | solution.py:79
  108.8 0.2 reduce.2
  109.0 0.1 reshape.79
  109.1 1.7 %gather_fusion.1 = bf16[128]{0:T(256)(128)(2,1)} fusion(bf16[256]{0:T(256)(128)(2,1)S(1)} %reshape.79, s32[1024]{0:T(1024)S(1)} %pad_clamp_fusion), kind=kCustom, calls=%fused_computation.1 | custom fusion | bytes 1024 | tf_op jit(solution)/shard_map/gather | solution.py:91
  110.9 15.9 %all-to-all-done.2 = bf16[128,2,768]{2,1,0:T(2,128)(2,1)S(1)} async-done(((bf16[128,2,768]{2,1,0:T(2,128)(2,1)}), bf16[128,2,768]{2,1,0:T(2,128)(2,1)S(1)}, u32[]{:S(2)}, u32[]{:S(2)}) %all-to-all-start.2) | async-done | bytes 393248 | tf_op jit(solution)/shard_map/all_to_all | solution.py:79
  126.8 0.1 reshape.78
  126.9 1.5 %gather_fusion = bf16[128,768]{1,0:T(8,128)(2,1)} fusion(bf16[256,768]{1,0:T(8,128)(2,1)S(1)} %reshape.78, s32[1024]{0:T(1024)S(1)} %pad_clamp_fusion), kind=kCustom, calls=%fused_computation | custom fusion | bytes 393728 | tf_op jit(solution)/shard_map/gather | solution.py:90
  (11 shorter events, 0.1 us)
Async XLA Ops:
  7.2 70.0 %all-gather.3.cloned.1.call-start = ((), (), s32[]{:S(2)}) async-start(), calls=%async_computation.4 | async-start | bytes 1966080 | tf_op jit(solution)/shard_map/all_gather | solution.py:66
  51.9 16.8 %all-to-all-start = ((bf16[128,1,2]{2,1,0:T(2,128)(2,1)}), bf16[128,1,2]{2,1,0:T(2,128)(2,1)S(1)}, u32[]{:S(2)}, u32[]{:S(2)}) async-start(bf16[128,1,2]{2,1,0:T(2,128)(2,1)} %all_to_all.21), calls=%async_computation | async-start | bytes 131072 | tf_op jit(solution)/shard_map/all_to_all | solution.py:57
  77.1 14.5 %copy-start = (bf16[1024,768]{1,0:T(8,128)(2,1)S(1)}, bf16[1024,768]{1,0:T(8,128)(2,1)}, u32[]{:S(2)}) copy-start(bf16[1024,768]{1,0:T(8,128)(2,1)} %all-gather.3.cloned.1.call-done) | copy-start | bytes 4718596
  80.5 22.5 %all-to-all-start.3 = ((bf16[128,1,2]{2,1,0:T(2,128)(2,1)}), bf16[128,1,2]{2,1,0:T(2,128)(2,1)S(1)}, u32[]{:S(2)}, u32[]{:S(2)}) async-start(bf16[128,1,2]{2,1,0:T(2,128)(2,1)} %convert_element_type.53), calls=%async_computation.3 | async-start | bytes 131072 | tf_op jit(solution)/shard_map/all_to_all | solution.py:86
  103.0 23.8 %all-to-all-start.2 = ((bf16[128,2,768]{2,1,0:T(2,128)(2,1)}), bf16[128,2,768]{2,1,0:T(2,128)(2,1)S(1)}, u32[]{:S(2)}, u32[]{:S(2)}) async-start(bf16[128,2,768]{2,1,0:T(2,128)(2,1)} %reshape.77), calls=%async_computation.2 | async-start | bytes 786432 | tf_op jit(solution)/shard_map/all_to_all | solution.py:79
Sparse Core Ops, SparseCore 0:
  49.7 24.1 all-gather.2
where the time goes:
time: 136 us; the launch traced here: 135 us
  blocking collectives  43.8 us (32%)
  waiting for transfers between devices  37.3 us (27%)
  starting transfers between devices  22.3 us (16%)
  between operations  14.2 us (10%)
  local copies, waits for them, and re-layouts  8.86 us (7%)
  other arithmetic  5.76 us (4%)
  matrix products  3.11 us (2%)
    all_to_all x1, blocking collectives, shards(): lax.all_to_all(send_unit.reshape(dp_count, capacity, feat_width), 'dp', s...  36.1 us
    all_to_all x1, waiting for transfers between devices, shards(): lax.all_to_all(neigh.reshape(dp_count, capacity, feat_width), 'dp', split...  15.9 us
    all_to_all x1, waiting for transfers between devices, shards(): lax.all_to_all(send_temp.reshape(dp_count, capacity), 'dp', split_axis=0,...  11.5 us
    all_to_all x1, starting transfers between devices, shards(): lax.all_to_all(mass_rounded.reshape(dp_count, capacity), 'dp', split_axis...  11.1 us
    all_to_all x1, waiting for transfers between devices, shards(): lax.all_to_all(mass_rounded.reshape(dp_count, capacity), 'dp', split_axis...  9.9 us
    all_gather x1, blocking collectives, shards(): lax.all_gather(query_temp, 'grp', axis=0, tiled=True)  7.71 us
    all_to_all x1, starting transfers between devices, shards(): lax.all_to_all(neigh.reshape(dp_count, capacity, feat_width), 'dp', split...  5.75 us
    all_to_all x1, starting transfers between devices, shards(): lax.all_to_all(send_temp.reshape(dp_count, capacity), 'dp', split_axis=0,...  5.32 us
  transfers between devices with their start and end apart: 4, of which 3 were waited for; matrix products, arithmetic and copies ran while one was open for 4% of the time, Pallas kernels for 0%

commit v1 on v0

v1 whole, which is shorter than its diff:
```python
import functools
import math

import jax
import jax.numpy as jnp
from jax import lax
from jax.experimental import pallas as pl
from jax.experimental.pallas import tpu as pltpu
from jax.sharding import Mesh
from jax.sharding import PartitionSpec as P

NEIGH_SCALE = 8.0
EXT = 128
NT = (((1,), (1,)), ((), ()))

AXES = ("z", "y", "core", "xhi", "xlo")
SPREAD = ("z", "y", "xhi")


def params():
    return pltpu.CompilerParams(vmem_limit_bytes=32 * 1024 * 1024)


def lane_to_row(ext):
    first = (lax.broadcasted_iota(jnp.int32, (16, EXT), 1) == 0).astype(jnp.bfloat16)
    return lax.dot_general(first, ext, NT, preferred_element_type=jnp.float32)[:1]


def pack_kernel(emb_ref, temp_ref, cluster_ref, send_ref, pick_ref):
    rows, width = emb_ref.shape
    slots = send_ref.shape[0]
    values = emb_ref[...].astype(jnp.float32)
    square_mean = jnp.mean(values * values, axis=1, keepdims=True)
    unit = (values * lax.rsqrt(square_mean + 1e-06) * (1.0 / math.sqrt(width))).astype(jnp.bfloat16)

    cluster_row = cluster_ref[...].astype(jnp.float32)
    row = lax.broadcasted_iota(jnp.int32, (rows, rows), 0)
    col = lax.broadcasted_iota(jnp.int32, (rows, rows), 1)
    cluster_col = jnp.sum(jnp.where(row == col, cluster_row, 0.0), axis=1, keepdims=True)
    same = cluster_row == cluster_col
    rank_row = jnp.sum(jnp.where(same & (row < col), 1.0, 0.0), axis=0, keepdims=True)
    rank_col = jnp.sum(jnp.where(same & (col < row), 1.0, 0.0), axis=1, keepdims=True)
    slot_row = (2.0 * cluster_row + rank_row).astype(jnp.int32)
    slot_col = (2.0 * cluster_col + rank_col).astype(jnp.int32)

    put = lax.broadcasted_iota(jnp.int32, (slots, rows), 0) == slot_row
    placed = jnp.dot(
        jnp.where(put, 1.0, 0.0).astype(jnp.bfloat16), unit, preferred_element_type=jnp.float32
    )
    temp = jnp.sum(jnp.where(put, temp_ref[...].astype(jnp.float32), 0.0), axis=1, keepdims=True)
    send_ref[:, :width] = placed.astype(jnp.bfloat16)
    send_ref[:, width:] = jnp.broadcast_to(temp, (slots, EXT)).astype(jnp.bfloat16)
    pick = lax.broadcasted_iota(jnp.int32, (rows, slots), 1) == slot_col
    pick_ref[...] = jnp.where(pick, 1.0, 0.0).astype(jnp.bfloat16)


def weigh(query_ref, key_ref, own_start):
    width = query_ref.shape[1] - EXT
    unit = key_ref[:, :width]
    cosine = lax.dot_general(
        query_ref[:, :width], unit, NT, preferred_element_type=jnp.float32
    )
    key_temp = lane_to_row(key_ref[:, width:])
    query_temp = query_ref[:, width : width + 1].astype(jnp.float32)
    weight = jnp.exp((cosine - 1.0) * ((query_temp + key_temp) * 0.5))
    allowed = key_temp > 0.0
    if own_start is not None:
        query_index = lax.broadcasted_iota(jnp.int32, cosine.shape, 0) + own_start
        allowed = allowed & (query_index != lax.broadcasted_iota(jnp.int32, cosine.shape, 1))
    weight = jnp.where(allowed, weight, 0.0)
    near = jnp.dot(weight.astype(jnp.bfloat16), unit, preferred_element_type=jnp.float32)
    return jnp.sum(weight, axis=1, keepdims=True), near


def first_kernel(core_ref, query_ref, key_ref, mass_ref, near_ref):
    mass, near = weigh(query_ref, key_ref, core_ref[0] * query_ref.shape[0])
    mass_ref[...] = jnp.broadcast_to(mass, mass_ref.shape)
    near_ref[...] = near


def second_kernel(query_ref, key_ref, mass_ref, near_ref, out_ref):
    width = near_ref.shape[1]
    mass, near = weigh(query_ref, key_ref, None)
    mass = mass + mass_ref[:, :1]
    near = near + near_ref[...]
    neigh = NEIGH_SCALE * math.sqrt(width) * near / (1.0 + mass)
    out_ref[:, :width] = neigh.astype(jnp.bfloat16)
    out_ref[:, width:] = jnp.broadcast_to(mass, (mass.shape[0], EXT)).astype(jnp.bfloat16)


def unpack_kernel(pick_ref, back_ref, neigh_ref, mass_ref):
    width = neigh_ref.shape[1]
    rows = jnp.dot(pick_ref[...], back_ref[...], preferred_element_type=jnp.float32)
    rows = rows.astype(jnp.bfloat16)
    neigh_ref[...] = rows[:, :width]
    mass_ref[...] = lane_to_row(rows[:, width:]).astype(jnp.bfloat16)


def call(kernel, outs, flops, *args, scalars=0):
    shapes = [jax.ShapeDtypeStruct(shape, dtype) for shape, dtype in outs]
    specs = [pl.BlockSpec(memory_space=pltpu.SMEM)] * scalars
    specs += [pl.BlockSpec(memory_space=pltpu.VMEM)] * (len(args) - scalars)
    moved = sum(a.size * a.dtype.itemsize for a in args)
    moved += sum(math.prod(s.shape) * s.dtype.itemsize for s in shapes)
    return pl.pallas_call(
        kernel,
        out_shape=shapes,
        in_specs=specs,
        out_specs=[pl.BlockSpec(memory_space=pltpu.VMEM)] * len(shapes),
        compiler_params=params(),
        cost_estimate=pl.CostEstimate(flops=flops, bytes_accessed=moved, transcendentals=0),
    )(*args)


def spread(slots, parts):
    count, wide = slots.shape
    moved = lax.all_to_all(
        slots.reshape(parts, count // parts, wide), SPREAD, split_axis=0, concat_axis=0, tiled=True
    )
    return moved.reshape(count, wide)


def shards(embeddings, inv_temp, cluster):
    rows, width = embeddings.shape
    parts = lax.axis_size("z") * lax.axis_size("y") * lax.axis_size("xhi")
    slots = 2 * parts
    wide = width + EXT
    bf16, f32 = jnp.bfloat16, jnp.float32

    send, pick = call(
        pack_kernel,
        [((slots, wide), bf16), ((rows, slots), bf16)],
        2 * slots * rows * width,
        embeddings,
        inv_temp.reshape(1, rows),
        cluster.reshape(1, rows),
    )
    query = spread(send, parts)

    pairs = [(0, 1), (1, 0)]
    far = lax.ppermute(query, "xlo", pairs)
    near_keys = lax.all_gather(query, "core", axis=0, tiled=True)
    core = lax.axis_index("core").astype(jnp.int32).reshape(1)
    work = 4 * slots * 2 * slots * width
    mass, near = call(
        first_kernel, [((slots, EXT), f32), ((slots, width), f32)], work, core, query, near_keys, scalars=1
    )
    far_keys = lax.all_gather(far, "core", axis=0, tiled=True)
    (result,) = call(second_kernel, [((slots, wide), bf16)], work, query, far_keys, mass, near)

    back = spread(result, parts)
    neigh, dup = call(
        unpack_kernel,
        [((rows, width), bf16), ((1, rows), bf16)],
        2 * slots * rows * wide,
        pick,
        back,
    )
    return neigh, dup.reshape(rows)


def solution(mesh):
    dp, grp = mesh.devices.shape
    z = y = math.isqrt(dp // 2)
    split = Mesh(mesh.devices.reshape(z, y, 2, grp // 2, 2), AXES)
    return jax.shard_map(
        shards,
        mesh=split,
        in_specs=(P(AXES, None), P(AXES), P(AXES, None)),
        out_specs=(P(AXES, None), P(AXES)),
        check_vma=False,
    )
```

time: 136 us -> 87.4 us (0.64)
  waiting for transfers between devices: 37.3 us -> 0.99 us
  blocking collectives: 43.8 us -> 76.4 us
  starting transfers between devices: 22.3 us -> 2.25 us
  between operations: 14.2 us -> 0.71 us
  local copies, waits for them, and re-layouts: 8.86 us -> 2.27 us
  other arithmetic: 5.76 us -> 0 us
  Pallas kernels: 0 us -> 3.12 us
  matrix products: 3.11 us -> 0 us
    all_to_all x3 -> x0, waiting for transfers between devices: 37.3 us -> none  [the longest x1 15.9 us: shards(): lax.all_to_all(neigh.reshape(dp_count, capacity, feat_width), 'dp', split...]
    all_to_all x1 -> x2, blocking collectives: 36.1 us -> 63.6 us  [spread(): lax.all_to_all(slots.reshape(parts, count // parts, wide), SPREAD, split_...]
    all_to_all x3 -> x0, starting transfers between devices: 22.2 us -> none  [the longest x1 11.1 us: shards(): lax.all_to_all(mass_rounded.reshape(dp_count, capacity), 'dp', split_axis...]
    all_gather x1 -> x2, blocking collectives: 7.71 us -> 12.7 us  [the longest x1 6.7 us: shards(): far_keys = lax.all_gather(far, 'core', axis=0, tiled=True)]
    gather x2 -> x0, local copies, waits for them, and re-layouts: 3.28 us -> none  [the longest x1 1.73 us: shards(): duplicate_mass = back_dup.reshape(slot_count)[position]]
    pallas_call x0 -> x4, Pallas kernels: none -> 3.12 us  [call(): pl.pallas_call(kernel, out_shape=shapes, in_specs=specs, out_specs=[pl.Bl...]
    dot_general x2 -> x0, matrix products: 3.11 us -> none  [the longest x1 2.53 us: weigh_tile(): lax.dot_general(query_unit, key_unit, (((1,), (1,)), ((), ())), preferred...]
    ppermute x0 -> x1, starting transfers between devices: none -> 2.25 us  [shards(): far = lax.ppermute(query, 'xlo', pairs)]
  transfers between devices with their start and end apart: 4 -> 1, of which waited for: 3 -> 1; matrix products, arithmetic and copies ran while one was open for 4% -> 0% of each run, Pallas kernels for 0% -> 1%
where the time goes in v1:
time: 87.4 us; the launch traced here: 85.7 us
  blocking collectives  76.4 us (87%)
  Pallas kernels  3.12 us (4%)
  local copies, waits for them, and re-layouts  2.27 us (3%)
  starting transfers between devices  2.25 us (3%)
  waiting for transfers between devices  0.99 us (1%)
    all_to_all x2, blocking collectives, spread(): lax.all_to_all(slots.reshape(parts, count // parts, wide), SPREAD, split_...  63.6 us
    all_gather x1, blocking collectives, shards(): far_keys = lax.all_gather(far, 'core', axis=0, tiled=True)  6.7 us
    all_gather x1, blocking collectives, shards(): near_keys = lax.all_gather(query, 'core', axis=0, tiled=True)  6.05 us
    pallas_call x4, Pallas kernels, call(): pl.pallas_call(kernel, out_shape=shapes, in_specs=specs, out_specs=[pl.Bl...  3.12 us
    ppermute x1, starting transfers between devices, shards(): far = lax.ppermute(query, 'xlo', pairs)  2.25 us
  transfers between devices with their start and end apart: 1, of which 1 were waited for; matrix products, arithmetic and copies ran while one was open for 0% of the time, Pallas kernels for 1%

profile of v1, /device:TPU:1, one launch (start us, length us, event | category | flops | bytes accessed | tf_op | source)
XLA Modules:
  0.0 85.7 jit_solution(11572350475607440152)
XLA Ops:
  0.6 0.0 copy-start.1
  0.6 0.0 copy-start.2
  0.6 0.6 copy-done.1
  1.3 0.0 copy-done.2
  1.3 0.0 copy-start
  1.3 0.9 %copy-done = bf16[128,768]{1,0:T(8,128)(2,1)S(1)} copy-done((bf16[128,768]{1,0:T(8,128)(2,1)S(1)}, bf16[128,768]{1,0:T(8,128)(2,1)}, u32[]{:S(2)}) %copy-start) | copy-done | bytes 196632
  2.2 0.4 shard_map.50
  2.6 0.2 reshape.30
  2.8 37.7 %all_to_all.10 = bf16[128,2,896]{2,1,0:T(2,128)(2,1)S(1)} all-to-all(bf16[128,2,896]{2,1,0:T(2,128)(2,1)S(1)} %reshape.30), channel_id=1, replica_groups=mesh['z'=8,'y'=8,'core'=2,'xhi'=2,'xlo'=2] {'z','y','xhi'}, dimensions={0} | all-to-all | bytes 917504 | tf_op jit(solution)/shard_map/all_to_all | solution.py:117
  40.5 0.2 reshape.31.query_ref
  40.7 2.2 %collective-permute-start = (bf16[256,896]{1,0:T(8,128)(2,1)S(1)}, bf16[256,896]{1,0:T(8,128)(2,1)S(1)}, u32[]{:S(2)}, u32[]{:S(2)}) collective-permute-start(bf16[256,896]{1,0:T(8,128)(2,1)S(1)} %reshape.31.query_ref), channel_id=1, source_target_pairs={{0,1},{1,0},{2,3},{3,2},{4,5},{5,4},{6,7},{7,6},{8,9},{9,8},{10,11... | collective-permute-start | bytes 1376264 | tf_op jit(solution)/shard_map/ppermute | solution.py:141
  42.9 6.0 %all_gather.7.key_ref = bf16[512,896]{1,0:T(8,128)(2,1)S(1)} all-gather(bf16[256,896]{1,0:T(8,128)(2,1)S(1)} %reshape.31.query_ref), channel_id=1, replica_groups=mesh['z'=8,'y'=8,'core'=2,'xhi'=2,'xlo'=2] {'core'}, dimensions={0}, use_global_device_ids=true | all-gather | bytes 1376256 | tf_op jit(solution)/shard_map/all_gather | solution.py:142
  49.0 0.9 %shard_map.51 = (f32[256,128]{1,0:T(8,128)S(1)}, f32[256,768]{1,0:T(8,128)S(1)}) custom-call(s32[1]{0:T(128)} %bitcast.2.core_ref, bf16[256,896]{1,0:T(8,128)(2,1)S(1)} %reshape.31.query_ref, bf16[512,896]{1,0:T(8,128)(2,1)S(1)} %all_gather.7.key_ref), custom_call_target="tpu_custom_call" | custom-call | flops 402653184 | bytes 2293764 | tf_op jit(solution)/shard_map/pallas_call | solution.py:105
  49.9 1.0 %collective-permute-done = bf16[256,896]{1,0:T(8,128)(2,1)S(1)} collective-permute-done((bf16[256,896]{1,0:T(8,128)(2,1)S(1)}, bf16[256,896]{1,0:T(8,128)(2,1)S(1)}, u32[]{:S(2)}, u32[]{:S(2)}) %collective-permute-start) | collective-permute-done | bytes 458784 | tf_op jit(solution)/shard_map/ppermute | solution.py:141
  50.9 6.7 %all_gather.6.key_ref = bf16[512,896]{1,0:T(8,128)(2,1)S(1)} all-gather(bf16[256,896]{1,0:T(8,128)(2,1)S(1)} %collective-permute-done), channel_id=1, replica_groups=mesh['z'=8,'y'=8,'core'=2,'xhi'=2,'xlo'=2] {'core'}, dimensions={0}, use_global_device_ids=true | all-gather | bytes 1376256 | tf_op jit(solution)/shard_map/all_gather | solution.py:148
  57.6 0.9 %shard_map.52 = bf16[256,896]{1,0:T(8,128)(2,1)S(1)} custom-call(bf16[256,896]{1,0:T(8,128)(2,1)S(1)} %reshape.31.query_ref, bf16[512,896]{1,0:T(8,128)(2,1)S(1)} %all_gather.6.key_ref, f32[256,128]{1,0:T(8,128)S(1)} %get-tuple-element.10.mass_ref, f32[256,768]{1,0:T(8,128)S(1)} %get-tuple-element.11.near_ref), custom_call_target="tpu_custom_call" | custom-call | flops 402653184 | bytes 2752512 | tf_op jit(solution)/shard_map/pallas_call | solution.py:105
  58.5 0.2 reshape.33
  58.7 25.9 %all_to_all.11 = bf16[128,2,896]{2,1,0:T(2,128)(2,1)S(1)} all-to-all(bf16[128,2,896]{2,1,0:T(2,128)(2,1)S(1)} %reshape.33), channel_id=1, replica_groups=mesh['z'=8,'y'=8,'core'=2,'xhi'=2,'xlo'=2] {'z','y','xhi'}, dimensions={0} | all-to-all | bytes 917504 | tf_op jit(solution)/shard_map/all_to_all | solution.py:117
  84.6 0.2 reshape.34.back_ref
  84.8 0.9 %shard_map.53 = (bf16[128,768]{1,0:T(8,128)(2,1)}, bf16[1,128]{1,0:T(2,128)(2,1)}) custom-call(bf16[128,256]{1,0:T(8,128)(2,1)S(1)} %get-tuple-element.8.pick_ref, bf16[256,896]{1,0:T(8,128)(2,1)S(1)} %reshape.34.back_ref), custom_call_target="tpu_custom_call" | custom-call | flops 58720256 | bytes 721152 | tf_op jit(solution)/shard_map/pallas_call | solution.py:105
Async XLA Ops:
  0.6 0.7 copy-start.1
  0.6 0.7 copy-start.2
  1.3 0.9 %copy-start = (bf16[128,768]{1,0:T(8,128)(2,1)S(1)}, bf16[128,768]{1,0:T(8,128)(2,1)}, u32[]{:S(2)}) copy-start(bf16[128,768]{1,0:T(8,128)(2,1)} %emb_ref.1) | copy-start | bytes 589828
  40.7 10.2 %collective-permute-start = (bf16[256,896]{1,0:T(8,128)(2,1)S(1)}, bf16[256,896]{1,0:T(8,128)(2,1)S(1)}, u32[]{:S(2)}, u32[]{:S(2)}) collective-permute-start(bf16[256,896]{1,0:T(8,128)(2,1)S(1)} %reshape.31.query_ref), channel_id=1, source_target_pairs={{0,1},{1,0},{2,3},{3,2},{4,5},{5,4},{6,7},{7,6},{8,9},{9,8},{10,11... | collective-permute-start | bytes 1376264 | tf_op jit(solution)/shard_map/ppermute | solution.py:141

commit v2 on v1

v2 whole, which is shorter than its diff:
```python
import math

import jax
import jax.numpy as jnp
from jax import lax
from jax.experimental import pallas as pl
from jax.experimental.pallas import tpu as pltpu
from jax.sharding import Mesh
from jax.sharding import PartitionSpec as P

NEIGH_SCALE = 8.0
EXT = 128
NT = (((1,), (1,)), ((), ()))

AXES = ("z", "y", "core", "xhi", "xlo")
SPREAD = ("z", "y", "xhi")


def params():
    return pltpu.CompilerParams(vmem_limit_bytes=32 * 1024 * 1024)


def lane_to_row(ext):
    first = (lax.broadcasted_iota(jnp.int32, (16, EXT), 1) == 0).astype(jnp.bfloat16)
    return lax.dot_general(first, ext, NT, preferred_element_type=jnp.float32)[:1]


def pack_kernel(emb_hbm, temp_hbm, cluster_hbm, send_ref, pick_ref, emb_ref, temp_ref, cluster_ref, sems):
    copies = [
        pltpu.make_async_copy(source, target, sems.at[i])
        for i, (source, target) in enumerate(
            ((cluster_hbm, cluster_ref), (temp_hbm, temp_ref), (emb_hbm, emb_ref))
        )
    ]
    for copy in copies:
        copy.start()
    rows, width = emb_ref.shape
    places = send_ref.shape[0]
    slots = pick_ref.shape[1]
    copies[0].wait()
    copies[1].wait()

    cluster_row = cluster_ref[...].astype(jnp.float32)
    row = lax.broadcasted_iota(jnp.int32, (rows, rows), 0)
    col = lax.broadcasted_iota(jnp.int32, (rows, rows), 1)
    cluster_col = jnp.sum(jnp.where(row == col, cluster_row, 0.0), axis=1, keepdims=True)
    same = cluster_row == cluster_col
    rank_row = jnp.sum(jnp.where(same & (row < col), 1.0, 0.0), axis=0, keepdims=True)
    rank_col = jnp.sum(jnp.where(same & (col < row), 1.0, 0.0), axis=1, keepdims=True)
    slot_row = (2.0 * cluster_row + rank_row).astype(jnp.int32)
    slot_col = (2.0 * cluster_col + rank_col).astype(jnp.int32)
    pick = lax.broadcasted_iota(jnp.int32, (rows, slots), 1) == slot_col
    pick_ref[...] = jnp.where(pick, 1.0, 0.0).astype(jnp.bfloat16)

    place = lax.broadcasted_iota(jnp.int32, (places, rows), 0)
    put = 2 * (place >> 2) + (place & 1) == slot_row
    temp = jnp.sum(jnp.where(put, temp_ref[...].astype(jnp.float32), 0.0), axis=1, keepdims=True)
    send_ref[:, width:] = jnp.broadcast_to(temp, (places, EXT)).astype(jnp.bfloat16)

    copies[2].wait()
    values = emb_ref[...].astype(jnp.float32)
    square_mean = jnp.mean(values * values, axis=1, keepdims=True)
    unit = (values * lax.rsqrt(square_mean + 1e-06) * (1.0 / math.sqrt(width))).astype(jnp.bfloat16)
    placed = jnp.dot(
        jnp.where(put, 1.0, 0.0).astype(jnp.bfloat16), unit, preferred_element_type=jnp.float32
    )
    send_ref[:, :width] = placed.astype(jnp.bfloat16)


def weigh(query, key_ref, skipped):
    width = key_ref.shape[1] - EXT
    unit = key_ref[:, :width]
    cosine = lax.dot_general(query[:, :width], unit, NT, preferred_element_type=jnp.float32)
    key_temp = lane_to_row(key_ref[:, width:])
    query_temp = query[:, width : width + 1].astype(jnp.float32)
    weight = jnp.exp((cosine - 1.0) * ((query_temp + key_temp) * 0.5))
    allowed = key_temp > 0.0
    if skipped is not None:
        allowed = allowed & ~skipped
    weight = jnp.where(allowed, weight, 0.0)
    near = jnp.dot(weight.astype(jnp.bfloat16), unit, preferred_element_type=jnp.float32)
    return jnp.sum(weight, axis=1, keepdims=True), near


def first_kernel(xlo_ref, mine_ref, query_ref, mass_ref, near_ref):
    shape = (query_ref.shape[0], mine_ref.shape[0])
    index = lax.broadcasted_iota(jnp.int32, shape, 0)
    place = 4 * (index >> 1) + (index & 1) + 2 * xlo_ref[0]
    own = lax.broadcasted_iota(jnp.int32, shape, 1) == place
    query = jnp.dot(
        jnp.where(own, 1.0, 0.0).astype(jnp.bfloat16),
        mine_ref[...],
        preferred_element_type=jnp.float32,
    ).astype(jnp.bfloat16)
    query_ref[...] = query
    mass, near = weigh(query, mine_ref, own)
    mass_ref[...] = jnp.broadcast_to(mass, mass_ref.shape)
    near_ref[...] = near


def second_kernel(query_ref, key_ref, mass_ref, near_ref, out_ref):
    width = near_ref.shape[1]
    mass, near = weigh(query_ref[...], key_ref, None)
    mass = mass + mass_ref[:, :1]
    near = near + near_ref[...]
    neigh = NEIGH_SCALE * math.sqrt(width) * near / (1.0 + mass)
    out_ref[:, :width] = neigh.astype(jnp.bfloat16)
    out_ref[:, width:] = jnp.broadcast_to(mass, (mass.shape[0], EXT)).astype(jnp.bfloat16)


def unpack_kernel(pick_ref, back_ref, neigh_ref, mass_ref):
    width = neigh_ref.shape[1]
    rows = jnp.dot(pick_ref[...], back_ref[...], preferred_element_type=jnp.float32)
    rows = rows.astype(jnp.bfloat16)
    neigh_ref[...] = rows[:, :width]
    mass_ref[...] = lane_to_row(rows[:, width:]).astype(jnp.bfloat16)


def call(kernel, outs, flops, *args, spaces=None, scratch=()):
    shapes = [jax.ShapeDtypeStruct(shape, dtype) for shape, dtype in outs]
    spaces = spaces or [pltpu.VMEM] * len(args)
    moved = sum(a.size * a.dtype.itemsize for a in args)
    moved += sum(math.prod(s.shape) * s.dtype.itemsize for s in shapes)
    return pl.pallas_call(
        kernel,
        out_shape=shapes,
        in_specs=[pl.BlockSpec(memory_space=space) for space in spaces],
        out_specs=[pl.BlockSpec(memory_space=pltpu.VMEM)] * len(shapes),
        scratch_shapes=scratch,
        compiler_params=params(),
        cost_estimate=pl.CostEstimate(flops=flops, bytes_accessed=moved, transcendentals=0),
    )(*args)


def exchange(slots, axes):
    count, wide = slots.shape
    moved = lax.all_to_all(
        slots.reshape(count // 2, 2, wide), axes, split_axis=0, concat_axis=0, tiled=True
    )
    return moved.reshape(count, wide)


def shards(embeddings, inv_temp, cluster):
    rows, width = embeddings.shape
    slots = 2 * math.prod(lax.axis_size(axis) for axis in SPREAD)
    places = 2 * slots
    wide = width + EXT
    bf16, f32, i32 = jnp.bfloat16, jnp.float32, jnp.int32

    send, pick = call(
        pack_kernel,
        [((places, wide), bf16), ((rows, slots), bf16)],
        2 * places * rows * width,
        embeddings,
        inv_temp.reshape(1, rows),
        cluster.reshape(1, rows),
        spaces=[pltpu.HBM] * 3,
        scratch=[
            pltpu.VMEM((rows, width), bf16),
            pltpu.VMEM((1, rows), bf16),
            pltpu.VMEM((1, rows), i32),
            pltpu.SemaphoreType.DMA((3,)),
        ],
    )
    mine = exchange(send, SPREAD + ("xlo",))
    other = lax.ppermute(mine, "core", [(0, 1), (1, 0)])
    xlo = lax.axis_index("xlo").astype(i32).reshape(1)
    work = 4 * slots * places * width
    query, mass, near = call(
        first_kernel,
        [((slots, wide), bf16), ((slots, EXT), f32), ((slots, width), f32)],
        work,
        xlo,
        mine,
        spaces=[pltpu.SMEM, pltpu.VMEM],
    )
    (result,) = call(second_kernel, [((slots, wide), bf16)], work, query, other, mass, near)
    back = exchange(result, SPREAD)
    neigh, dup = call(
        unpack_kernel,
        [((rows, width), bf16), ((1, rows), bf16)],
        2 * slots * rows * wide,
        pick,
        back,
    )
    return neigh, dup.reshape(rows)


def solution(mesh):
    dp, grp = mesh.devices.shape
    z = y = math.isqrt(dp // 2)
    split = Mesh(mesh.devices.reshape(z, y, 2, grp // 2, 2), AXES)
    return jax.shard_map(
        shards,
        mesh=split,
        in_specs=(P(AXES, None), P(AXES), P(AXES, None)),
        out_specs=(P(AXES, None), P(AXES)),
        check_vma=False,
    )
```

time: 87.4 us -> 88.6 us (1.014)
  starting transfers between devices: 2.25 us -> 4.59 us
  blocking collectives: 76.4 us -> 74.1 us
    all_gather x2 -> x0, blocking collectives: 12.7 us -> none  [the longest x1 6.7 us: shards(): far_keys = lax.all_gather(far, 'core', axis=0, tiled=True)]
    all_to_all x2, blocking collectives: 63.6 us -> 74.1 us  [exchange(): lax.all_to_all(slots.reshape(count // 2, 2, wide), axes, split_axis=0, co...]
    ppermute x1, starting transfers between devices: 2.25 us -> 4.59 us  [shards(): other = lax.ppermute(mine, 'core', [(0, 1), (1, 0)])]
where the time goes in v2:
time: 88.6 us; the launch traced here: 86.9 us
  blocking collectives  74.1 us (84%)
  starting transfers between devices  4.59 us (5%)
  Pallas kernels  3.99 us (5%)
  local copies, waits for them, and re-layouts  2.62 us (3%)
  waiting for transfers between devices  0.89 us (1%)
    all_to_all x2, blocking collectives, exchange(): lax.all_to_all(slots.reshape(count // 2, 2, wide), axes, split_axis=0, co...  74.1 us
    ppermute x1, starting transfers between devices, shards(): other = lax.ppermute(mine, 'core', [(0, 1), (1, 0)])  4.59 us
    pallas_call x4, Pallas kernels, call(): pl.pallas_call(kernel, out_shape=shapes, in_specs=[pl.BlockSpec(memory_sp...  3.99 us
  transfers between devices with their start and end apart: 1, of which 1 were waited for; matrix products, arithmetic and copies ran while one was open for 0% of the time, Pallas kernels for 1%

profile of v2, /device:TPU:1, one launch (start us, length us, event | category | flops | bytes accessed | tf_op | source)
XLA Modules:
  0.0 86.9 jit_solution(758782445126718607)
XLA Ops:
  0.6 0.0 copy-start.1
  0.6 0.0 copy-start.2
  0.6 0.6 copy-done.1
  1.3 0.0 copy-done.2
  1.3 0.0 copy-start
  1.3 0.9 %copy-done = bf16[128,768]{1,0:T(8,128)(2,1)S(1)} copy-done((bf16[128,768]{1,0:T(8,128)(2,1)S(1)}, bf16[128,768]{1,0:T(8,128)(2,1)}, u32[]{:S(2)}) %copy-start) | copy-done | bytes 196632
  2.2 1.0 %shard_map.50 = (bf16[512,896]{1,0:T(8,128)(2,1)S(1)}, bf16[128,256]{1,0:T(8,128)(2,1)S(1)}) custom-call(bf16[128,768]{1,0:T(8,128)(2,1)S(1)} %copy-done, bf16[1,128]{1,0:T(2,128)(2,1)S(1)} %bitcast.4, s32[1,128]{1,0:T(1,128)S(1)} %bitcast.5), custom_call_target="tpu_custom_call" | custom-call | flops 100663296 | bytes 1180416 | tf_op jit(solution)/shard_map/pallas_call | solution.py:124
  3.2 0.3 reshape.31
  3.6 48.8 %all_to_all.10 = bf16[256,2,896]{2,1,0:T(2,128)(2,1)S(1)} all-to-all(bf16[256,2,896]{2,1,0:T(2,128)(2,1)S(1)} %reshape.31), channel_id=1, replica_groups=mesh['z'=8,'y'=8,'core'=2,'xhi'=2,'xlo'=2] {'z','y','xhi','xlo'}, dimensions={0} | all-to-all | bytes 1835008 | tf_op jit(solution)/shard_map/all_to_all | solution.py:137
  52.3 0.3 reshape.32.mine_ref
  52.7 4.6 %collective-permute-start = (bf16[512,896]{1,0:T(8,128)(2,1)S(1)}, bf16[512,896]{1,0:T(8,128)(2,1)S(1)}, u32[]{:S(2)}, u32[]{:S(2)}) collective-permute-start(bf16[512,896]{1,0:T(8,128)(2,1)S(1)} %reshape.32.mine_ref), channel_id=1, source_target_pairs={{0,4},{4,0},{1,5},{5,1},{2,6},{6,2},{3,7},{7,3},{8,12},{12,8},{9,1... | collective-permute-start | bytes 2752520 | tf_op jit(solution)/shard_map/ppermute | solution.py:166
  57.3 1.2 %shard_map.51 = (bf16[256,896]{1,0:T(8,128)(2,1)S(1)}, f32[256,128]{1,0:T(8,128)S(1)}, f32[256,768]{1,0:T(8,128)S(1)}) custom-call(s32[1]{0:T(128)} %bitcast.2.xlo_ref, bf16[512,896]{1,0:T(8,128)(2,1)S(1)} %reshape.32.mine_ref), custom_call_target="tpu_custom_call" | custom-call | flops 402653184 | bytes 2293764 | tf_op jit(solution)/shard_map/pallas_call | solution.py:124
  58.5 0.9 %collective-permute-done.key_ref = bf16[512,896]{1,0:T(8,128)(2,1)S(1)} collective-permute-done((bf16[512,896]{1,0:T(8,128)(2,1)S(1)}, bf16[512,896]{1,0:T(8,128)(2,1)S(1)}, u32[]{:S(2)}, u32[]{:S(2)}) %collective-permute-start) | collective-permute-done | bytes 917536 | tf_op jit(solution)/shard_map/ppermute | solution.py:166
  59.4 0.9 %shard_map.52 = bf16[256,896]{1,0:T(8,128)(2,1)S(1)} custom-call(bf16[256,896]{1,0:T(8,128)(2,1)S(1)} %get-tuple-element.11.query_ref, bf16[512,896]{1,0:T(8,128)(2,1)S(1)} %collective-permute-done.key_ref, f32[256,128]{1,0:T(8,128)S(1)} %get-tuple-element.12.mass_ref, f32[256,768]{1,0:T(8,128)S(1)} %get-tuple-element.13.near_ref), custom_call_target="tpu_custom_call" | custom-call | flops 402653184 | bytes 2752512 | tf_op jit(solution)/shard_map/pallas_call | solution.py:124
  60.3 0.2 reshape.33
  60.5 25.3 %all_to_all.11 = bf16[128,2,896]{2,1,0:T(2,128)(2,1)S(1)} all-to-all(bf16[128,2,896]{2,1,0:T(2,128)(2,1)S(1)} %reshape.33), channel_id=1, replica_groups=mesh['z'=8,'y'=8,'core'=2,'xhi'=2,'xlo'=2] {'z','y','xhi'}, dimensions={0} | all-to-all | bytes 917504 | tf_op jit(solution)/shard_map/all_to_all | solution.py:137
  85.7 0.2 reshape.34.back_ref
  85.9 0.9 %shard_map.53 = (bf16[128,768]{1,0:T(8,128)(2,1)}, bf16[1,128]{1,0:T(2,128)(2,1)}) custom-call(bf16[128,256]{1,0:T(8,128)(2,1)S(1)} %get-tuple-element.9.pick_ref, bf16[256,896]{1,0:T(8,128)(2,1)S(1)} %reshape.34.back_ref), custom_call_target="tpu_custom_call" | custom-call | flops 58720256 | bytes 721152 | tf_op jit(solution)/shard_map/pallas_call | solution.py:124
Async XLA Ops:
  0.6 0.7 copy-start.1
  0.6 0.7 copy-start.2
  1.3 0.9 %copy-start = (bf16[128,768]{1,0:T(8,128)(2,1)S(1)}, bf16[128,768]{1,0:T(8,128)(2,1)}, u32[]{:S(2)}) copy-start(bf16[128,768]{1,0:T(8,128)(2,1)} %emb_hbm.1) | copy-start | bytes 589828
  52.7 6.7 %collective-permute-start = (bf16[512,896]{1,0:T(8,128)(2,1)S(1)}, bf16[512,896]{1,0:T(8,128)(2,1)S(1)}, u32[]{:S(2)}, u32[]{:S(2)}) collective-permute-start(bf16[512,896]{1,0:T(8,128)(2,1)S(1)} %reshape.32.mine_ref), channel_id=1, source_target_pairs={{0,4},{4,0},{1,5},{5,1},{2,6},{6,2},{3,7},{7,3},{8,12},{12,8},{9,1... | collective-permute-start | bytes 2752520 | tf_op jit(solution)/shard_map/ppermute | solution.py:166

commit v3 on v1

--- a/solution.py
+++ b/solution.py
@@ -3,6 +3,7 @@
 
 import jax
 import jax.numpy as jnp
+import numpy as np
 from jax import lax
 from jax.experimental import pallas as pl
 from jax.experimental.pallas import tpu as pltpu
@@ -13,8 +14,20 @@
 EXT = 128
 NT = (((1,), (1,)), ((), ()))
 
-AXES = ("z", "y", "core", "xhi", "xlo")
-SPREAD = ("z", "y", "xhi")
+AXES = ("z", "y", "core", "x")
+
+
+class Layout:
+    def __init__(self, dp, grp):
+        side = math.isqrt(dp // 2)
+        ids = np.arange(dp * grp).reshape(side, side, 2, grp)
+        half = [[0, 1], [3, 2]]
+        order = [((a + b) % side, a, h) for h in range(2) for b in range(side) for a in range(side)]
+        self.spread = [
+            [int(ids[z, y, core, half[h][s]]) for z, y, h in order] for core in range(2) for s in range(2)
+        ]
+        self.pairs = [(x, x ^ 1) for x in range(grp)]
+        self.shape = ids.shape
 
 
 def params():
@@ -78,7 +91,13 @@
     near_ref[...] = near
 
 
-def second_kernel(query_ref, key_ref, mass_ref, near_ref, out_ref):
+def next_kernel(query_ref, key_ref, mass_in_ref, near_in_ref, mass_ref, near_ref):
+    mass, near = weigh(query_ref, key_ref, None)
+    mass_ref[...] = jnp.broadcast_to(mass, mass_ref.shape) + mass_in_ref[...]
+    near_ref[...] = near + near_in_ref[...]
+
+
+def last_kernel(query_ref, key_ref, mass_ref, near_ref, out_ref):
     width = near_ref.shape[1]
     mass, near = weigh(query_ref, key_ref, None)
     mass = mass + mass_ref[:, :1]
@@ -112,18 +131,26 @@
     )(*args)
 
 
-def spread(slots, parts):
+def spread(slots, layout):
     count, wide = slots.shape
     moved = lax.all_to_all(
-        slots.reshape(parts, count // parts, wide), SPREAD, split_axis=0, concat_axis=0, tiled=True
+        slots.reshape(count // 2, 2, wide),
+        AXES,
+        split_axis=0,
+        concat_axis=0,
+        axis_index_groups=layout.spread,
+        tiled=True,
     )
     return moved.reshape(count, wide)
 
 
-def shards(embeddings, inv_temp, cluster):
+def both_cores(rows):
+    return lax.all_gather(rows, "core", axis=0, tiled=True)
+
+
+def shards(layout, embeddings, inv_temp, cluster):
     rows, width = embeddings.shape
-    parts = lax.axis_size("z") * lax.axis_size("y") * lax.axis_size("xhi")
-    slots = 2 * parts
+    slots = 2 * len(layout.spread[0])
     wide = width + EXT
     bf16, f32 = jnp.bfloat16, jnp.float32
 
@@ -135,20 +162,24 @@
         inv_temp.reshape(1, rows),
         cluster.reshape(1, rows),
     )
-    query = spread(send, parts)
-
-    pairs = [(0, 1), (1, 0)]
-    far = lax.ppermute(query, "xlo", pairs)
-    near_keys = lax.all_gather(query, "core", axis=0, tiled=True)
+    query = spread(send, layout)
+
+    cut = slots * 3 // 4
+    far_most = lax.ppermute(query[:cut], "x", layout.pairs)
+    far_rest = lax.ppermute(query[cut:], "x", layout.pairs)
+    keys = both_cores(query)
     core = lax.axis_index("core").astype(jnp.int32).reshape(1)
-    work = 4 * slots * 2 * slots * width
-    mass, near = call(
-        first_kernel, [((slots, EXT), f32), ((slots, width), f32)], work, core, query, near_keys, scalars=1
-    )
-    far_keys = lax.all_gather(far, "core", axis=0, tiled=True)
-    (result,) = call(second_kernel, [((slots, wide), bf16)], work, query, far_keys, mass, near)
-
-    back = spread(result, parts)
+    sums = [((slots, EXT), f32), ((slots, width), f32)]
+    work = 4 * slots * width
+    mass, near = call(first_kernel, sums, 2 * slots * work, core, query, keys, scalars=1)
+    keys = both_cores(far_most)
+    mass, near = call(next_kernel, sums, 2 * cut * work, query, keys, mass, near)
+    keys = both_cores(far_rest)
+    (result,) = call(
+        last_kernel, [((slots, wide), bf16)], 2 * (slots - cut) * work, query, keys, mass, near
+    )
+
+    back = spread(result, layout)
     neigh, dup = call(
         unpack_kernel,
         [((rows, width), bf16), ((1, rows), bf16)],
@@ -160,11 +191,10 @@
 
 
 def solution(mesh):
-    dp, grp = mesh.devices.shape
-    z = y = math.isqrt(dp // 2)
-    split = Mesh(mesh.devices.reshape(z, y, 2, grp // 2, 2), AXES)
+    layout = Layout(*mesh.devices.shape)
+    split = Mesh(mesh.devices.reshape(layout.shape), AXES)
     return jax.shard_map(
-        shards,
+        functools.partial(shards, layout),
         mesh=split,
         in_specs=(P(AXES, None), P(AXES), P(AXES, None)),
         out_specs=(P(AXES, None), P(AXES)),

time: 87.4 us -> 89.8 us (1.027); the launches traced: 85.7 us -> 89.2 us
  starting transfers between devices: 2.25 us -> 5.28 us
  waiting for transfers between devices: 0.99 us -> 0.01 us
    ppermute x1 -> x2, starting transfers between devices: 2.25 us -> 5.28 us  [the longest x1 3.36 us: shards(): far_rest = lax.ppermute(query[cut:], 'x', layout.pairs)]
    all_to_all x2, blocking collectives: 63.6 us -> 64.7 us  [spread(): lax.all_to_all(slots.reshape(count // 2, 2, wide), AXES, split_axis=0, co...]
    ppermute x1 -> x2, waiting for transfers between devices: 0.99 us -> 0.01 us  [the longest x1 0.01 us: shards(): far_rest = lax.ppermute(query[cut:], 'x', layout.pairs)]
    all_gather x2 -> x3, blocking collectives: 12.7 us -> 12.2 us  [both_cores(): return lax.all_gather(rows, 'core', axis=0, tiled=True)]
    pallas_call x4 -> x5, Pallas kernels: 3.12 us -> 3.55 us  [call(): pl.pallas_call(kernel, out_shape=shapes, in_specs=specs, out_specs=[pl.Bl...]
  transfers between devices with their start and end apart: 1 -> 2, of which waited for: 1 -> 0; matrix products, arithmetic and copies ran while one was open for 0% -> 0% of each run, Pallas kernels for 1% -> 1%
where the time goes in v3:
time: 89.8 us; the launch traced here: 89.2 us
  blocking collectives  76.8 us (86%)
  starting transfers between devices  5.28 us (6%)
  Pallas kernels  3.55 us (4%)
  local copies, waits for them, and re-layouts  2.77 us (3%)
    all_to_all x2, blocking collectives, spread(): lax.all_to_all(slots.reshape(count // 2, 2, wide), AXES, split_axis=0, co...  64.7 us
    all_gather x3, blocking collectives, both_cores(): return lax.all_gather(rows, 'core', axis=0, tiled=True)  12.2 us
    pallas_call x5, Pallas kernels, call(): pl.pallas_call(kernel, out_shape=shapes, in_specs=specs, out_specs=[pl.Bl...  3.55 us
    ppermute x1, starting transfers between devices, shards(): far_rest = lax.ppermute(query[cut:], 'x', layout.pairs)  3.36 us
    ppermute x1, starting transfers between devices, shards(): far_most = lax.ppermute(query[:cut], 'x', layout.pairs)  1.92 us
  transfers between devices with their start and end apart: 2, of which 0 were waited for; matrix products, arithmetic and copies ran while one was open for 0% of the time, Pallas kernels for 1%

profile of v3, /device:TPU:1, one launch (start us, length us, event | category | flops | bytes accessed | tf_op | source)
XLA Modules:
  0.0 89.2 jit_solution(9991339924514734162)
XLA Ops:
  0.6 0.0 copy-start.1
  0.6 0.0 copy-start.2
  0.6 0.6 copy-done.1
  1.3 0.0 copy-done.2
  1.3 0.0 copy-start
  1.3 0.9 %copy-done = bf16[128,768]{1,0:T(8,128)(2,1)S(1)} copy-done((bf16[128,768]{1,0:T(8,128)(2,1)S(1)}, bf16[128,768]{1,0:T(8,128)(2,1)}, u32[]{:S(2)}) %copy-start) | copy-done | bytes 196632
  2.2 0.4 shard_map.50
  2.6 0.2 reshape.32
  2.8 38.5 %all_to_all.10 = bf16[128,2,896]{2,1,0:T(2,128)(2,1)S(1)} all-to-all(bf16[128,2,896]{2,1,0:T(2,128)(2,1)S(1)} %reshape.32), channel_id=1, replica_groups={{0,72,144,216,288,360,432,504,64,136,208,280,352,424,496,56,128,200,272..., dimensions={0} | all-to-all | bytes 917504 | tf_op jit(solution)/shard_map/all_to_all | solution.py:136
  41.3 0.2 slice.17
  41.5 0.1 slice.15
  41.7 1.9 %collective-permute-start.1 = (bf16[192,896]{1,0:T(8,128)(2,1)S(1)}, bf16[192,896]{1,0:T(8,128)(2,1)S(1)}, u32[]{:S(2)}, u32[]{:S(2)}) collective-permute-start(bf16[192,896]{1,0:T(8,128)(2,1)S(1)} %slice.15), channel_id=1, source_target_pairs={{0,1},{1,0},{2,3},{3,2},{4,5},{5,4},{6,7},{7,6},{8,9},{9,8},{10,11... | collective-permute-start | bytes 1032200 | tf_op jit(solution)/shard_map/ppermute | solution.py:168
  43.6 0.1 slice.16
  43.8 3.4 %collective-permute-start = (bf16[64,896]{1,0:T(8,128)(2,1)S(1)}, bf16[64,896]{1,0:T(8,128)(2,1)S(1)}, u32[]{:S(2)}, u32[]{:S(2)}) collective-permute-start(bf16[64,896]{1,0:T(8,128)(2,1)S(1)} %slice.13), channel_id=1, source_target_pairs={{0,1},{1,0},{2,3},{3,2},{4,5},{5,4},{6,7},{7,6},{8,9},{9,8},{10,11... | collective-permute-start | bytes 344072 | tf_op jit(solution)/shard_map/ppermute | solution.py:169
  47.1 0.2 reshape.33.query_ref
  47.3 5.3 %all_gather.11.key_ref = bf16[512,896]{1,0:T(8,128)(2,1)S(1)} all-gather(bf16[256,896]{1,0:T(8,128)(2,1)S(1)} %reshape.33.query_ref), channel_id=1, replica_groups=mesh['z'=8,'y'=8,'core'=2,'x'=4] {'core'}, dimensions={0}, use_global_device_ids=true | all-gather | bytes 1376256 | tf_op jit(solution)/shard_map/all_gather | solution.py:148
  52.6 0.9 %shard_map.51 = (f32[256,128]{1,0:T(8,128)S(1)}, f32[256,768]{1,0:T(8,128)S(1)}) custom-call(s32[1]{0:T(128)} %bitcast.2.core_ref, bf16[256,896]{1,0:T(8,128)(2,1)S(1)} %reshape.33.query_ref, bf16[512,896]{1,0:T(8,128)(2,1)S(1)} %all_gather.11.key_ref), custom_call_target="tpu_custom_call" | custom-call | flops 402653184 | bytes 2293764 | tf_op jit(solution)/shard_map/pallas_call | solution.py:124
  53.6 0.0 collective-permute-done
  53.6 4.5 %all_gather.9.key_ref = bf16[128,896]{1,0:T(8,128)(2,1)S(1)} all-gather(bf16[64,896]{1,0:T(8,128)(2,1)S(1)} %collective-permute-done), channel_id=1, replica_groups=mesh['z'=8,'y'=8,'core'=2,'x'=4] {'core'}, dimensions={0}, use_global_device_ids=true | all-gather | bytes 344064 | tf_op jit(solution)/shard_map/all_gather | solution.py:148
  58.1 0.0 collective-permute-done.1
  58.1 2.3 %all_gather.10.key_ref = bf16[384,896]{1,0:T(8,128)(2,1)S(1)} all-gather(bf16[192,896]{1,0:T(8,128)(2,1)S(1)} %collective-permute-done.1), channel_id=1, replica_groups=mesh['z'=8,'y'=8,'core'=2,'x'=4] {'core'}, dimensions={0}, use_global_device_ids=true | all-gather | bytes 1032192 | tf_op jit(solution)/shard_map/all_gather | solution.py:148
  60.4 0.8 shard_map.52
  61.2 0.5 shard_map.53
  61.7 0.2 reshape.35
  61.9 26.2 %all_to_all.11 = bf16[128,2,896]{2,1,0:T(2,128)(2,1)S(1)} all-to-all(bf16[128,2,896]{2,1,0:T(2,128)(2,1)S(1)} %reshape.35), channel_id=1, replica_groups={{0,72,144,216,288,360,432,504,64,136,208,280,352,424,496,56,128,200,272..., dimensions={0} | all-to-all | bytes 917504 | tf_op jit(solution)/shard_map/all_to_all | solution.py:136
  88.1 0.2 reshape.36.back_ref
  88.2 0.9 %shard_map.54 = (bf16[128,768]{1,0:T(8,128)(2,1)}, bf16[1,128]{1,0:T(2,128)(2,1)}) custom-call(bf16[128,256]{1,0:T(8,128)(2,1)S(1)} %get-tuple-element.10.pick_ref, bf16[256,896]{1,0:T(8,128)(2,1)S(1)} %reshape.36.back_ref), custom_call_target="tpu_custom_call" | custom-call | flops 58720256 | bytes 721152 | tf_op jit(solution)/shard_map/pallas_call | solution.py:124
  (1 shorter events, 0.0 us)
Async XLA Ops:
  0.6 0.7 copy-start.1
  0.6 0.7 copy-start.2
  1.3 0.9 %copy-start = (bf16[128,768]{1,0:T(8,128)(2,1)S(1)}, bf16[128,768]{1,0:T(8,128)(2,1)}, u32[]{:S(2)}) copy-start(bf16[128,768]{1,0:T(8,128)(2,1)} %emb_ref.1) | copy-start | bytes 589828
  41.7 16.4 %collective-permute-start.1 = (bf16[192,896]{1,0:T(8,128)(2,1)S(1)}, bf16[192,896]{1,0:T(8,128)(2,1)S(1)}, u32[]{:S(2)}, u32[]{:S(2)}) collective-permute-start(bf16[192,896]{1,0:T(8,128)(2,1)S(1)} %slice.15), channel_id=1, source_target_pairs={{0,1},{1,0},{2,3},{3,2},{4,5},{5,4},{6,7},{7,6},{8,9},{9,8},{10,11... | collective-permute-start | bytes 1032200 | tf_op jit(solution)/shard_map/ppermute | solution.py:168
  43.8 9.8 %collective-permute-start = (bf16[64,896]{1,0:T(8,128)(2,1)S(1)}, bf16[64,896]{1,0:T(8,128)(2,1)S(1)}, u32[]{:S(2)}, u32[]{:S(2)}) collective-permute-start(bf16[64,896]{1,0:T(8,128)(2,1)S(1)} %slice.13), channel_id=1, source_target_pairs={{0,1},{1,0},{2,3},{3,2},{4,5},{5,4},{6,7},{7,6},{8,9},{9,8},{10,11... | collective-permute-start | bytes 344072 | tf_op jit(solution)/shard_map/ppermute | solution.py:169

commit v4 on v3

--- a/solution.py
+++ b/solution.py
@@ -22,7 +22,13 @@
         side = math.isqrt(dp // 2)
         ids = np.arange(dp * grp).reshape(side, side, 2, grp)
         half = [[0, 1], [3, 2]]
-        order = [((a + b) % side, a, h) for h in range(2) for b in range(side) for a in range(side)]
+        mid = side // 2
+        order = [
+            ((a + b + mid) % side, (a + mid) % side, h)
+            for h in range(2)
+            for b in range(side)
+            for a in range(side)
+        ]
         self.spread = [
             [int(ids[z, y, core, half[h][s]]) for z, y, h in order] for core in range(2) for s in range(2)
         ]
@@ -89,12 +95,6 @@
     mass, near = weigh(query_ref, key_ref, core_ref[0] * query_ref.shape[0])
     mass_ref[...] = jnp.broadcast_to(mass, mass_ref.shape)
     near_ref[...] = near
-
-
-def next_kernel(query_ref, key_ref, mass_in_ref, near_in_ref, mass_ref, near_ref):
-    mass, near = weigh(query_ref, key_ref, None)
-    mass_ref[...] = jnp.broadcast_to(mass, mass_ref.shape) + mass_in_ref[...]
-    near_ref[...] = near + near_in_ref[...]
 
 
 def last_kernel(query_ref, key_ref, mass_ref, near_ref, out_ref):
@@ -164,20 +164,14 @@
     )
     query = spread(send, layout)
 
-    cut = slots * 3 // 4
-    far_most = lax.ppermute(query[:cut], "x", layout.pairs)
-    far_rest = lax.ppermute(query[cut:], "x", layout.pairs)
+    far = lax.ppermute(query, "x", layout.pairs)
     keys = both_cores(query)
     core = lax.axis_index("core").astype(jnp.int32).reshape(1)
     sums = [((slots, EXT), f32), ((slots, width), f32)]
     work = 4 * slots * width
     mass, near = call(first_kernel, sums, 2 * slots * work, core, query, keys, scalars=1)
-    keys = both_cores(far_most)
-    mass, near = call(next_kernel, sums, 2 * cut * work, query, keys, mass, near)
-    keys = both_cores(far_rest)
-    (result,) = call(
-        last_kernel, [((slots, wide), bf16)], 2 * (slots - cut) * work, query, keys, mass, near
-    )
+    keys = both_cores(far)
+    (result,) = call(last_kernel, [((slots, wide), bf16)], 2 * slots * work, query, keys, mass, near)
 
     back = spread(result, layout)
     neigh, dup = call(

time: 89.8 us -> 84.1 us (0.937)
  blocking collectives: 76.8 us -> 69.2 us
  waiting for transfers between devices: 0.01 us -> 6.56 us
  starting transfers between devices: 5.28 us -> 1.92 us
    ppermute x2 -> x1, waiting for transfers between devices: 0.01 us -> 6.56 us  [shards(): far = lax.ppermute(query, 'x', layout.pairs)]
    all_gather x3 -> x2, blocking collectives: 12.2 us -> 7.49 us  [both_cores(): return lax.all_gather(rows, 'core', axis=0, tiled=True)]
    ppermute x2 -> x1, starting transfers between devices: 5.28 us -> 1.92 us  [shards(): far = lax.ppermute(query, 'x', layout.pairs)]
    all_to_all x2, blocking collectives: 64.7 us -> 61.8 us  [spread(): lax.all_to_all(slots.reshape(count // 2, 2, wide), AXES, split_axis=0, co...]
    pallas_call x5 -> x4, Pallas kernels: 3.55 us -> 3.13 us  [call(): pl.pallas_call(kernel, out_shape=shapes, in_specs=specs, out_specs=[pl.Bl...]
  transfers between devices with their start and end apart: 2 -> 1, of which waited for: 0 -> 1; matrix products, arithmetic and copies ran while one was open for 0% -> 0% of each run, Pallas kernels for 1% -> 1%
where the time goes in v4:
time: 84.1 us; the launch traced here: 83.8 us
  blocking collectives  69.2 us (82%)
  waiting for transfers between devices  6.56 us (8%)
  Pallas kernels  3.13 us (4%)
  local copies, waits for them, and re-layouts  2.27 us (3%)
  starting transfers between devices  1.92 us (2%)
    all_to_all x2, blocking collectives, spread(): lax.all_to_all(slots.reshape(count // 2, 2, wide), AXES, split_axis=0, co...  61.8 us
    all_gather x2, blocking collectives, both_cores(): return lax.all_gather(rows, 'core', axis=0, tiled=True)  7.49 us
    ppermute x1, waiting for transfers between devices, shards(): far = lax.ppermute(query, 'x', layout.pairs)  6.56 us
    pallas_call x4, Pallas kernels, call(): pl.pallas_call(kernel, out_shape=shapes, in_specs=specs, out_specs=[pl.Bl...  3.13 us
    ppermute x1, starting transfers between devices, shards(): far = lax.ppermute(query, 'x', layout.pairs)  1.92 us
  transfers between devices with their start and end apart: 1, of which 1 were waited for; matrix products, arithmetic and copies ran while one was open for 0% of the time, Pallas kernels for 1%

profile of v4, /device:TPU:1, one launch (start us, length us, event | category | flops | bytes accessed | tf_op | source)
XLA Modules:
  0.0 83.8 jit_solution(18364191937842570331)
XLA Ops:
  0.6 0.0 copy-start.1
  0.6 0.0 copy-start.2
  0.6 0.6 copy-done.1
  1.3 0.0 copy-done.2
  1.3 0.0 copy-start
  1.3 0.9 %copy-done = bf16[128,768]{1,0:T(8,128)(2,1)S(1)} copy-done((bf16[128,768]{1,0:T(8,128)(2,1)S(1)}, bf16[128,768]{1,0:T(8,128)(2,1)}, u32[]{:S(2)}) %copy-start) | copy-done | bytes 196632
  2.2 0.4 shard_map.50
  2.6 0.2 reshape.30
  2.8 35.3 %all_to_all.10 = bf16[128,2,896]{2,1,0:T(2,128)(2,1)S(1)} all-to-all(bf16[128,2,896]{2,1,0:T(2,128)(2,1)S(1)} %reshape.30), channel_id=1, replica_groups={{288,360,432,504,0,72,144,216,352,424,496,56,64,136,208,280,416,488,48,..., dimensions={0} | all-to-all | bytes 917504 | tf_op jit(solution)/shard_map/all_to_all | solution.py:136
  38.1 0.2 reshape.31.query_ref
  38.3 1.9 %collective-permute-start = (bf16[256,896]{1,0:T(8,128)(2,1)S(1)}, bf16[256,896]{1,0:T(8,128)(2,1)S(1)}, u32[]{:S(2)}, u32[]{:S(2)}) collective-permute-start(bf16[256,896]{1,0:T(8,128)(2,1)S(1)} %reshape.31.query_ref), channel_id=1, source_target_pairs={{0,1},{1,0},{2,3},{3,2},{4,5},{5,4},{6,7},{7,6},{8,9},{9,8},{10,11... | collective-permute-start | bytes 1376264 | tf_op jit(solution)/shard_map/ppermute | solution.py:167
  40.2 3.3 %all_gather.7.key_ref = bf16[512,896]{1,0:T(8,128)(2,1)S(1)} all-gather(bf16[256,896]{1,0:T(8,128)(2,1)S(1)} %reshape.31.query_ref), channel_id=1, replica_groups=mesh['z'=8,'y'=8,'core'=2,'x'=4] {'core'}, dimensions={0}, use_global_device_ids=true | all-gather | bytes 1376256 | tf_op jit(solution)/shard_map/all_gather | solution.py:148
  43.5 0.9 %shard_map.51 = (f32[256,128]{1,0:T(8,128)S(1)}, f32[256,768]{1,0:T(8,128)S(1)}) custom-call(s32[1]{0:T(128)} %bitcast.2.core_ref, bf16[256,896]{1,0:T(8,128)(2,1)S(1)} %reshape.31.query_ref, bf16[512,896]{1,0:T(8,128)(2,1)S(1)} %all_gather.7.key_ref), custom_call_target="tpu_custom_call" | custom-call | flops 402653184 | bytes 2293764 | tf_op jit(solution)/shard_map/pallas_call | solution.py:124
  44.4 6.6 %collective-permute-done = bf16[256,896]{1,0:T(8,128)(2,1)S(1)} collective-permute-done((bf16[256,896]{1,0:T(8,128)(2,1)S(1)}, bf16[256,896]{1,0:T(8,128)(2,1)S(1)}, u32[]{:S(2)}, u32[]{:S(2)}) %collective-permute-start) | collective-permute-done | bytes 458784 | tf_op jit(solution)/shard_map/ppermute | solution.py:167
  51.0 4.2 %all_gather.6.key_ref = bf16[512,896]{1,0:T(8,128)(2,1)S(1)} all-gather(bf16[256,896]{1,0:T(8,128)(2,1)S(1)} %collective-permute-done), channel_id=1, replica_groups=mesh['z'=8,'y'=8,'core'=2,'x'=4] {'core'}, dimensions={0}, use_global_device_ids=true | all-gather | bytes 1376256 | tf_op jit(solution)/shard_map/all_gather | solution.py:148
  55.2 0.9 %shard_map.52 = bf16[256,896]{1,0:T(8,128)(2,1)S(1)} custom-call(bf16[256,896]{1,0:T(8,128)(2,1)S(1)} %reshape.31.query_ref, bf16[512,896]{1,0:T(8,128)(2,1)S(1)} %all_gather.6.key_ref, f32[256,128]{1,0:T(8,128)S(1)} %get-tuple-element.10.mass_ref, f32[256,768]{1,0:T(8,128)S(1)} %get-tuple-element.11.near_ref), custom_call_target="tpu_custom_call" | custom-call | flops 402653184 | bytes 2752512 | tf_op jit(solution)/shard_map/pallas_call | solution.py:124
  56.1 0.2 reshape.33
  56.3 26.4 %all_to_all.11 = bf16[128,2,896]{2,1,0:T(2,128)(2,1)S(1)} all-to-all(bf16[128,2,896]{2,1,0:T(2,128)(2,1)S(1)} %reshape.33), channel_id=1, replica_groups={{288,360,432,504,0,72,144,216,352,424,496,56,64,136,208,280,416,488,48,..., dimensions={0} | all-to-all | bytes 917504 | tf_op jit(solution)/shard_map/all_to_all | solution.py:136
  82.7 0.2 reshape.34.back_ref
  82.9 0.9 %shard_map.53 = (bf16[128,768]{1,0:T(8,128)(2,1)}, bf16[1,128]{1,0:T(2,128)(2,1)}) custom-call(bf16[128,256]{1,0:T(8,128)(2,1)S(1)} %get-tuple-element.8.pick_ref, bf16[256,896]{1,0:T(8,128)(2,1)S(1)} %reshape.34.back_ref), custom_call_target="tpu_custom_call" | custom-call | flops 58720256 | bytes 721152 | tf_op jit(solution)/shard_map/pallas_call | solution.py:124
Async XLA Ops:
  0.6 0.7 copy-start.1
  0.6 0.7 copy-start.2
  1.3 0.9 %copy-start = (bf16[128,768]{1,0:T(8,128)(2,1)S(1)}, bf16[128,768]{1,0:T(8,128)(2,1)}, u32[]{:S(2)}) copy-start(bf16[128,768]{1,0:T(8,128)(2,1)} %emb_ref.1) | copy-start | bytes 589828
  38.3 12.7 %collective-permute-start = (bf16[256,896]{1,0:T(8,128)(2,1)S(1)}, bf16[256,896]{1,0:T(8,128)(2,1)S(1)}, u32[]{:S(2)}, u32[]{:S(2)}) collective-permute-start(bf16[256,896]{1,0:T(8,128)(2,1)S(1)} %reshape.31.query_ref), channel_id=1, source_target_pairs={{0,1},{1,0},{2,3},{3,2},{4,5},{5,4},{6,7},{7,6},{8,9},{9,8},{10,11... | collective-permute-start | bytes 1376264 | tf_op jit(solution)/shard_map/ppermute | solution.py:167

commit v5 on v4

--- a/solution.py
+++ b/solution.py
@@ -23,21 +23,25 @@
         ids = np.arange(dp * grp).reshape(side, side, 2, grp)
         half = [[0, 1], [3, 2]]
         mid = side // 2
+        steps = sorted(range(side), key=lambda step: (min(step, side - step), step))
         order = [
-            ((a + b + mid) % side, (a + mid) % side, h)
-            for h in range(2)
-            for b in range(side)
-            for a in range(side)
+            ((a + b + mid) % side, (a + mid) % side, h) for h in range(2) for b in steps for a in steps
         ]
-        self.spread = [
-            [int(ids[z, y, core, half[h][s]]) for z, y, h in order] for core in range(2) for s in range(2)
-        ]
+        start = order.index((side - 1, mid, 0))
+        self.count = len(order)
+        self.shift = start
+
+        def groups(order):
+            return [
+                [int(ids[z, y, core, half[h][s]]) for z, y, h in order]
+                for core in range(2)
+                for s in range(2)
+            ]
+
+        self.out = groups(order[start:] + order[:start])
+        self.back = groups(order)
         self.pairs = [(x, x ^ 1) for x in range(grp)]
         self.shape = ids.shape
-
-
-def params():
-    return pltpu.CompilerParams(vmem_limit_bytes=32 * 1024 * 1024)
 
 
 def lane_to_row(ext):
@@ -45,12 +49,17 @@
     return lax.dot_general(first, ext, NT, preferred_element_type=jnp.float32)[:1]
 
 
-def pack_kernel(emb_ref, temp_ref, cluster_ref, send_ref, pick_ref):
+def pack_kernel(
+    shift, emb_hbm, temp_hbm, cluster_hbm, send_ref, pick_ref, emb_ref, temp_ref, cluster_ref, sems
+):
+    pairs = ((cluster_hbm, cluster_ref), (temp_hbm, temp_ref), (emb_hbm, emb_ref))
+    copies = [pltpu.make_async_copy(*pair, sems.at[i]) for i, pair in enumerate(pairs)]
+    for copy in copies:
+        copy.start()
     rows, width = emb_ref.shape
     slots = send_ref.shape[0]
-    values = emb_ref[...].astype(jnp.float32)
-    square_mean = jnp.mean(values * values, axis=1, keepdims=True)
-    unit = (values * lax.rsqrt(square_mean + 1e-06) * (1.0 / math.sqrt(width))).astype(jnp.bfloat16)
+    copies[0].wait()
+    copies[1].wait()
 
     cluster_row = cluster_ref[...].astype(jnp.float32)
     row = lax.broadcasted_iota(jnp.int32, (rows, rows), 0)
@@ -60,17 +69,23 @@
     rank_row = jnp.sum(jnp.where(same & (row < col), 1.0, 0.0), axis=0, keepdims=True)
     rank_col = jnp.sum(jnp.where(same & (col < row), 1.0, 0.0), axis=1, keepdims=True)
     slot_row = (2.0 * cluster_row + rank_row).astype(jnp.int32)
-    slot_col = (2.0 * cluster_col + rank_col).astype(jnp.int32)
+    slot_col = (2.0 * cluster_col + rank_col).astype(jnp.int32) + 2 * shift
+    slot_col = jnp.where(slot_col >= slots, slot_col - slots, slot_col)
+    pick = lax.broadcasted_iota(jnp.int32, (rows, slots), 1) == slot_col
+    pick_ref[...] = jnp.where(pick, 1.0, 0.0).astype(jnp.bfloat16)
 
     put = lax.broadcasted_iota(jnp.int32, (slots, rows), 0) == slot_row
+    temp = jnp.sum(jnp.where(put, temp_ref[...].astype(jnp.float32), 0.0), axis=1, keepdims=True)
+    send_ref[:, width:] = jnp.broadcast_to(temp, (slots, EXT)).astype(jnp.bfloat16)
+
+    copies[2].wait()
+    values = emb_ref[...].astype(jnp.float32)
+    square_mean = jnp.mean(values * values, axis=1, keepdims=True)
+    unit = (values * lax.rsqrt(square_mean + 1e-06) * (1.0 / math.sqrt(width))).astype(jnp.bfloat16)
     placed = jnp.dot(
         jnp.where(put, 1.0, 0.0).astype(jnp.bfloat16), unit, preferred_element_type=jnp.float32
     )
-    temp = jnp.sum(jnp.where(put, temp_ref[...].astype(jnp.float32), 0.0), axis=1, keepdims=True)
     send_ref[:, :width] = placed.astype(jnp.bfloat16)
-    send_ref[:, width:] = jnp.broadcast_to(temp, (slots, EXT)).astype(jnp.bfloat16)
-    pick = lax.broadcasted_iota(jnp.int32, (rows, slots), 1) == slot_col
-    pick_ref[...] = jnp.where(pick, 1.0, 0.0).astype(jnp.bfloat16)
 
 
 def weigh(query_ref, key_ref, own_start):
@@ -97,14 +112,17 @@
     near_ref[...] = near
 
 
-def last_kernel(query_ref, key_ref, mass_ref, near_ref, out_ref):
-    width = near_ref.shape[1]
+def last_kernel(shift, query_ref, key_ref, mass_ref, near_ref, out_ref):
+    slots, width = near_ref.shape
     mass, near = weigh(query_ref, key_ref, None)
     mass = mass + mass_ref[:, :1]
     near = near + near_ref[...]
     neigh = NEIGH_SCALE * math.sqrt(width) * near / (1.0 + mass)
-    out_ref[:, :width] = neigh.astype(jnp.bfloat16)
-    out_ref[:, width:] = jnp.broadcast_to(mass, (mass.shape[0], EXT)).astype(jnp.bfloat16)
+    mass = jnp.broadcast_to(mass, (slots, EXT))
+    moved = 2 * shift
+    for source, target, count in ((0, moved, slots - moved), (slots - moved, 0, moved)):
+        out_ref[target : target + count, :width] = neigh[source : source + count].astype(jnp.bfloat16)
+        out_ref[target : target + count, width:] = mass[source : source + count].astype(jnp.bfloat16)
 
 
 def unpack_kernel(pick_ref, back_ref, neigh_ref, mass_ref):
@@ -115,30 +133,30 @@
     mass_ref[...] = lane_to_row(rows[:, width:]).astype(jnp.bfloat16)
 
 
-def call(kernel, outs, flops, *args, scalars=0):
+def call(kernel, outs, flops, *args, spaces=None, scratch=(), room=32 * 2**20):
     shapes = [jax.ShapeDtypeStruct(shape, dtype) for shape, dtype in outs]
-    specs = [pl.BlockSpec(memory_space=pltpu.SMEM)] * scalars
-    specs += [pl.BlockSpec(memory_space=pltpu.VMEM)] * (len(args) - scalars)
+    spaces = spaces or [pltpu.VMEM] * len(args)
     moved = sum(a.size * a.dtype.itemsize for a in args)
     moved += sum(math.prod(s.shape) * s.dtype.itemsize for s in shapes)
     return pl.pallas_call(
         kernel,
         out_shape=shapes,
-        in_specs=specs,
+        in_specs=[pl.BlockSpec(memory_space=space) for space in spaces],
         out_specs=[pl.BlockSpec(memory_space=pltpu.VMEM)] * len(shapes),
-        compiler_params=params(),
+        scratch_shapes=scratch,
+        compiler_params=pltpu.CompilerParams(vmem_limit_bytes=room),
         cost_estimate=pl.CostEstimate(flops=flops, bytes_accessed=moved, transcendentals=0),
     )(*args)
 
 
-def spread(slots, layout):
+def exchange(slots, groups):
     count, wide = slots.shape
     moved = lax.all_to_all(
         slots.reshape(count // 2, 2, wide),
         AXES,
         split_axis=0,
         concat_axis=0,
-        axis_index_groups=layout.spread,
+        axis_index_groups=groups,
         tiled=True,
     )
     return moved.reshape(count, wide)
@@ -150,30 +168,49 @@
 
 def shards(layout, embeddings, inv_temp, cluster):
     rows, width = embeddings.shape
-    slots = 2 * len(layout.spread[0])
+    slots = 2 * layout.count
     wide = width + EXT
     bf16, f32 = jnp.bfloat16, jnp.float32
 
     send, pick = call(
-        pack_kernel,
+        functools.partial(pack_kernel, layout.shift),
         [((slots, wide), bf16), ((rows, slots), bf16)],
         2 * slots * rows * width,
         embeddings,
         inv_temp.reshape(1, rows),
         cluster.reshape(1, rows),
-    )
-    query = spread(send, layout)
+        spaces=[pltpu.HBM] * 3,
+        scratch=[
+            pltpu.VMEM((rows, width), bf16),
+            pltpu.VMEM((1, rows), bf16),
+            pltpu.VMEM((1, rows), jnp.int32),
+            pltpu.SemaphoreType.DMA((3,)),
+        ],
+        room=60 * 2**20,
+    )
+    query = exchange(send, layout.out)
 
     far = lax.ppermute(query, "x", layout.pairs)
     keys = both_cores(query)
     core = lax.axis_index("core").astype(jnp.int32).reshape(1)
     sums = [((slots, EXT), f32), ((slots, width), f32)]
     work = 4 * slots * width
-    mass, near = call(first_kernel, sums, 2 * slots * work, core, query, keys, scalars=1)
+    mass, near = call(
+        first_kernel, sums, 2 * slots * work, core, query, keys,
+        spaces=[pltpu.SMEM, pltpu.VMEM, pltpu.VMEM],
+    )
     keys = both_cores(far)
-    (result,) = call(last_kernel, [((slots, wide), bf16)], 2 * slots * work, query, keys, mass, near)
-
-    back = spread(result, layout)
+    (result,) = call(
+        functools.partial(last_kernel, layout.shift),
+        [((slots, wide), bf16)],
+        2 * slots * work,
+        query,
+        keys,
+        mass,
+        near,
+    )
+
+    back = exchange(result, layout.back)
     neigh, dup = call(
         unpack_kernel,
         [((rows, width), bf16), ((1, rows), bf16)],

time: 84.1 us -> 84.1 us (level)
  Pallas kernels: 3.13 us -> 4.86 us
  blocking collectives: 69.2 us -> 68.2 us
  waiting for transfers between devices: 6.56 us -> 5.59 us
    all_to_all x2, blocking collectives: 61.8 us -> 59.8 us  [exchange(): lax.all_to_all(slots.reshape(count // 2, 2, wide), AXES, split_axis=0, co...]
    pallas_call x4, Pallas kernels: 3.13 us -> 4.86 us  [call(): pl.pallas_call(kernel, out_shape=shapes, in_specs=[pl.BlockSpec(memory_sp...]
    reshape x4, local copies, waits for them, and re-layouts: 0.69 us -> 1.71 us  [the longest x2 1.37 us: exchange(): slots.reshape(count // 2, 2, wide)]
    all_gather x2, blocking collectives: 7.49 us -> 8.46 us  [both_cores(): return lax.all_gather(rows, 'core', axis=0, tiled=True)]
    ppermute x1, waiting for transfers between devices: 6.56 us -> 5.59 us  [shards(): far = lax.ppermute(query, 'x', layout.pairs)]
    unnamed x6 -> x2, local copies, waits for them, and re-layouts: 1.58 us -> 0.66 us
where the time goes in v5:
time: 84.1 us; the launch traced here: 83.6 us
  blocking collectives  68.2 us (81%)
  waiting for transfers between devices  5.59 us (7%)
  Pallas kernels  4.86 us (6%)
  local copies, waits for them, and re-layouts  2.37 us (3%)
  starting transfers between devices  1.92 us (2%)
    all_to_all x2, blocking collectives, exchange(): lax.all_to_all(slots.reshape(count // 2, 2, wide), AXES, split_axis=0, co...  59.8 us
    all_gather x2, blocking collectives, both_cores(): return lax.all_gather(rows, 'core', axis=0, tiled=True)  8.46 us
    ppermute x1, waiting for transfers between devices, shards(): far = lax.ppermute(query, 'x', layout.pairs)  5.59 us
    pallas_call x4, Pallas kernels, call(): pl.pallas_call(kernel, out_shape=shapes, in_specs=[pl.BlockSpec(memory_sp...  4.86 us
    ppermute x1, starting transfers between devices, shards(): far = lax.ppermute(query, 'x', layout.pairs)  1.92 us
  transfers between devices with their start and end apart: 1, of which 1 were waited for; matrix products, arithmetic and copies ran while one was open for 0% of the time, Pallas kernels for 1%

profile of v5, /device:TPU:1, one launch (start us, length us, event | category | flops | bytes accessed | tf_op | source)
XLA Modules:
  0.0 83.6 jit_solution(8736297604973198854)
XLA Ops:
  0.6 2.1 %shard_map.50 = (bf16[256,896]{1,0:T(8,128)(2,1)}, bf16[128,256]{1,0:T(8,128)(2,1)}) custom-call(bf16[128,768]{1,0:T(8,128)(2,1)} %emb_hbm.1, bf16[1,128]{1,0:T(2,128)(2,1)} %bitcast.4, s32[1,128]{1,0:T(1,128)} %bitcast.5), custom_call_target="tpu_custom_call" | custom-call | flops 50331648 | bytes 721664 | tf_op jit(solution)/shard_map/pallas_call | solution.py:141
  2.7 1.2 %reshape.30 = bf16[128,2,896]{2,1,0:T(2,128)(2,1)S(1)} reshape(bf16[256,896]{1,0:T(8,128)(2,1)} %get-tuple-element.9) | data formatting | bytes 917504 | tf_op jit(solution)/shard_map/reshape | solution.py:155
  3.9 34.4 %all_to_all.10 = bf16[128,2,896]{2,1,0:T(2,128)(2,1)S(1)} all-to-all(bf16[128,2,896]{2,1,0:T(2,128)(2,1)S(1)} %reshape.30), channel_id=1, replica_groups={{480,40,408,112,336,184,264,192,96,168,24,240,464,312,392,320,32,104,47..., dimensions={0} | all-to-all | bytes 917504 | tf_op jit(solution)/shard_map/all_to_all | solution.py:154
  38.4 0.2 reshape.31.query_ref
  38.5 1.9 %collective-permute-start = (bf16[256,896]{1,0:T(8,128)(2,1)S(1)}, bf16[256,896]{1,0:T(8,128)(2,1)S(1)}, u32[]{:S(2)}, u32[]{:S(2)}) collective-permute-start(bf16[256,896]{1,0:T(8,128)(2,1)S(1)} %reshape.31.query_ref), channel_id=1, source_target_pairs={{0,1},{1,0},{2,3},{3,2},{4,5},{5,4},{6,7},{7,6},{8,9},{9,8},{10,11... | collective-permute-start | bytes 1376264 | tf_op jit(solution)/shard_map/ppermute | solution.py:193
  40.5 3.8 %all_gather.7.key_ref = bf16[512,896]{1,0:T(8,128)(2,1)S(1)} all-gather(bf16[256,896]{1,0:T(8,128)(2,1)S(1)} %reshape.31.query_ref), channel_id=1, replica_groups=mesh['z'=8,'y'=8,'core'=2,'x'=4] {'core'}, dimensions={0}, use_global_device_ids=true | all-gather | bytes 1376256 | tf_op jit(solution)/shard_map/all_gather | solution.py:166
  44.2 0.9 %shard_map.51 = (f32[256,128]{1,0:T(8,128)S(1)}, f32[256,768]{1,0:T(8,128)S(1)}) custom-call(s32[1]{0:T(128)} %bitcast.2.core_ref, bf16[256,896]{1,0:T(8,128)(2,1)S(1)} %reshape.31.query_ref, bf16[512,896]{1,0:T(8,128)(2,1)S(1)} %all_gather.7.key_ref), custom_call_target="tpu_custom_call" | custom-call | flops 402653184 | bytes 2293764 | tf_op jit(solution)/shard_map/pallas_call | solution.py:141
  45.2 5.6 %collective-permute-done = bf16[256,896]{1,0:T(8,128)(2,1)S(1)} collective-permute-done((bf16[256,896]{1,0:T(8,128)(2,1)S(1)}, bf16[256,896]{1,0:T(8,128)(2,1)S(1)}, u32[]{:S(2)}, u32[]{:S(2)}) %collective-permute-start) | collective-permute-done | bytes 458784 | tf_op jit(solution)/shard_map/ppermute | solution.py:193
  50.7 4.7 %all_gather.6.key_ref = bf16[512,896]{1,0:T(8,128)(2,1)S(1)} all-gather(bf16[256,896]{1,0:T(8,128)(2,1)S(1)} %collective-permute-done), channel_id=1, replica_groups=mesh['z'=8,'y'=8,'core'=2,'x'=4] {'core'}, dimensions={0}, use_global_device_ids=true | all-gather | bytes 1376256 | tf_op jit(solution)/shard_map/all_gather | solution.py:166
  55.4 0.9 %shard_map.52 = bf16[256,896]{1,0:T(8,128)(2,1)S(1)} custom-call(bf16[256,896]{1,0:T(8,128)(2,1)S(1)} %reshape.31.query_ref, bf16[512,896]{1,0:T(8,128)(2,1)S(1)} %all_gather.6.key_ref, f32[256,128]{1,0:T(8,128)S(1)} %get-tuple-element.10.mass_ref, f32[256,768]{1,0:T(8,128)S(1)} %get-tuple-element.11.near_ref), custom_call_target="tpu_custom_call" | custom-call | flops 402653184 | bytes 2752512 | tf_op jit(solution)/shard_map/pallas_call | solution.py:141
  56.3 0.2 reshape.33
  56.5 25.3 %all_to_all.11 = bf16[128,2,896]{2,1,0:T(2,128)(2,1)S(1)} all-to-all(bf16[128,2,896]{2,1,0:T(2,128)(2,1)S(1)} %reshape.33), channel_id=1, replica_groups={{288,360,216,432,144,504,72,0,352,424,280,496,208,56,136,64,224,296,152..., dimensions={0} | all-to-all | bytes 917504 | tf_op jit(solution)/shard_map/all_to_all | solution.py:154
  81.9 0.0 copy-start
  81.9 0.2 reshape.34.back_ref
  82.0 0.7 copy-done
  82.7 0.9 %shard_map.53 = (bf16[128,768]{1,0:T(8,128)(2,1)}, bf16[1,128]{1,0:T(2,128)(2,1)}) custom-call(bf16[128,256]{1,0:T(8,128)(2,1)S(1)} %copy-done, bf16[256,896]{1,0:T(8,128)(2,1)S(1)} %reshape.34.back_ref), custom_call_target="tpu_custom_call" | custom-call | flops 58720256 | bytes 721152 | tf_op jit(solution)/shard_map/pallas_call | solution.py:141
Async XLA Ops:
  38.5 12.2 %collective-permute-start = (bf16[256,896]{1,0:T(8,128)(2,1)S(1)}, bf16[256,896]{1,0:T(8,128)(2,1)S(1)}, u32[]{:S(2)}, u32[]{:S(2)}) collective-permute-start(bf16[256,896]{1,0:T(8,128)(2,1)S(1)} %reshape.31.query_ref), channel_id=1, source_target_pairs={{0,1},{1,0},{2,3},{3,2},{4,5},{5,4},{6,7},{7,6},{8,9},{9,8},{10,11... | collective-permute-start | bytes 1376264 | tf_op jit(solution)/shard_map/ppermute | solution.py:193
  81.9 0.8 %copy-start = (bf16[128,256]{1,0:T(8,128)(2,1)S(1)}, bf16[128,256]{1,0:T(8,128)(2,1)}, u32[]{:S(2)}) copy-start(bf16[128,256]{1,0:T(8,128)(2,1)} %get-tuple-element.8.pick_ref) | copy-start | bytes 196612

commit v6 on v5

--- a/solution.py
+++ b/solution.py
@@ -21,7 +21,7 @@
     def __init__(self, dp, grp):
         side = math.isqrt(dp // 2)
         ids = np.arange(dp * grp).reshape(side, side, 2, grp)
-        half = [[0, 1], [3, 2]]
+        half = [[0, 3], [1, 2]]
         mid = side // 2
         steps = sorted(range(side), key=lambda step: (min(step, side - step), step))
         order = [
@@ -40,7 +40,7 @@
 
         self.out = groups(order[start:] + order[:start])
         self.back = groups(order)
-        self.pairs = [(x, x ^ 1) for x in range(grp)]
+        self.pairs = [(x, grp - 1 - x) for x in range(grp)]
         self.shape = ids.shape
 
 
@@ -49,17 +49,9 @@
     return lax.dot_general(first, ext, NT, preferred_element_type=jnp.float32)[:1]
 
 
-def pack_kernel(
-    shift, emb_hbm, temp_hbm, cluster_hbm, send_ref, pick_ref, emb_ref, temp_ref, cluster_ref, sems
-):
-    pairs = ((cluster_hbm, cluster_ref), (temp_hbm, temp_ref), (emb_hbm, emb_ref))
-    copies = [pltpu.make_async_copy(*pair, sems.at[i]) for i, pair in enumerate(pairs)]
-    for copy in copies:
-        copy.start()
+def pack_kernel(shift, emb_ref, temp_ref, cluster_ref, send_ref, pick_ref):
     rows, width = emb_ref.shape
     slots = send_ref.shape[0]
-    copies[0].wait()
-    copies[1].wait()
 
     cluster_row = cluster_ref[...].astype(jnp.float32)
     row = lax.broadcasted_iota(jnp.int32, (rows, rows), 0)
@@ -78,7 +70,6 @@
     temp = jnp.sum(jnp.where(put, temp_ref[...].astype(jnp.float32), 0.0), axis=1, keepdims=True)
     send_ref[:, width:] = jnp.broadcast_to(temp, (slots, EXT)).astype(jnp.bfloat16)
 
-    copies[2].wait()
     values = emb_ref[...].astype(jnp.float32)
     square_mean = jnp.mean(values * values, axis=1, keepdims=True)
     unit = (values * lax.rsqrt(square_mean + 1e-06) * (1.0 / math.sqrt(width))).astype(jnp.bfloat16)
@@ -133,7 +124,7 @@
     mass_ref[...] = lane_to_row(rows[:, width:]).astype(jnp.bfloat16)
 
 
-def call(kernel, outs, flops, *args, spaces=None, scratch=(), room=32 * 2**20):
+def call(kernel, outs, flops, *args, spaces=None):
     shapes = [jax.ShapeDtypeStruct(shape, dtype) for shape, dtype in outs]
     spaces = spaces or [pltpu.VMEM] * len(args)
     moved = sum(a.size * a.dtype.itemsize for a in args)
@@ -143,8 +134,7 @@
         out_shape=shapes,
         in_specs=[pl.BlockSpec(memory_space=space) for space in spaces],
         out_specs=[pl.BlockSpec(memory_space=pltpu.VMEM)] * len(shapes),
-        scratch_shapes=scratch,
-        compiler_params=pltpu.CompilerParams(vmem_limit_bytes=room),
+        compiler_params=pltpu.CompilerParams(vmem_limit_bytes=32 * 2**20),
         cost_estimate=pl.CostEstimate(flops=flops, bytes_accessed=moved, transcendentals=0),
     )(*args)
 
@@ -179,14 +169,6 @@
         embeddings,
         inv_temp.reshape(1, rows),
         cluster.reshape(1, rows),
-        spaces=[pltpu.HBM] * 3,
-        scratch=[
-            pltpu.VMEM((rows, width), bf16),
-            pltpu.VMEM((1, rows), bf16),
-            pltpu.VMEM((1, rows), jnp.int32),
-            pltpu.SemaphoreType.DMA((3,)),
-        ],
-        room=60 * 2**20,
     )
     query = exchange(send, layout.out)
 

time: 84.1 us -> 80 us (0.951)
  blocking collectives: 68.2 us -> 65 us
  starting transfers between devices: 1.92 us -> 4.39 us
  Pallas kernels: 4.86 us -> 3.12 us
  waiting for transfers between devices: 5.59 us -> 4.14 us
    all_to_all x2, blocking collectives: 59.8 us -> 56.3 us  [exchange(): lax.all_to_all(slots.reshape(count // 2, 2, wide), AXES, split_axis=0, co...]
    ppermute x1, starting transfers between devices: 1.92 us -> 4.39 us  [shards(): far = lax.ppermute(query, 'x', layout.pairs)]
    pallas_call x4, Pallas kernels: 4.86 us -> 3.12 us  [call(): pl.pallas_call(kernel, out_shape=shapes, in_specs=[pl.BlockSpec(memory_sp...]
    ppermute x1, waiting for transfers between devices: 5.59 us -> 4.14 us  [shards(): far = lax.ppermute(query, 'x', layout.pairs)]
    reshape x2, local copies, waits for them, and re-layouts: 1.37 us -> 0.35 us  [exchange(): slots.reshape(count // 2, 2, wide)]
    unnamed x2 -> x6, local copies, waits for them, and re-layouts: 0.66 us -> 1.58 us
where the time goes in v6:
time: 80 us; the launch traced here: 79.6 us
  blocking collectives  65 us (81%)
  starting transfers between devices  4.39 us (5%)
  waiting for transfers between devices  4.14 us (5%)
  Pallas kernels  3.12 us (4%)
  local copies, waits for them, and re-layouts  2.27 us (3%)
    all_to_all x2, blocking collectives, exchange(): lax.all_to_all(slots.reshape(count // 2, 2, wide), AXES, split_axis=0, co...  56.3 us
    all_gather x2, blocking collectives, both_cores(): return lax.all_gather(rows, 'core', axis=0, tiled=True)  8.67 us
    ppermute x1, starting transfers between devices, shards(): far = lax.ppermute(query, 'x', layout.pairs)  4.39 us
    ppermute x1, waiting for transfers between devices, shards(): far = lax.ppermute(query, 'x', layout.pairs)  4.14 us
    pallas_call x4, Pallas kernels, call(): pl.pallas_call(kernel, out_shape=shapes, in_specs=[pl.BlockSpec(memory_sp...  3.12 us
  transfers between devices with their start and end apart: 1, of which 1 were waited for; matrix products, arithmetic and copies ran while one was open for 0% of the time, Pallas kernels for 1%

profile of v6, /device:TPU:1, one launch (start us, length us, event | category | flops | bytes accessed | tf_op | source)
XLA Modules:
  0.0 79.6 jit_solution(6140481643723820884)
XLA Ops:
  0.6 0.0 copy-start.1
  0.6 0.0 copy-start.2
  0.6 0.6 copy-done.1
  1.3 0.0 copy-done.2
  1.3 0.0 copy-start
  1.3 0.9 %copy-done = bf16[128,768]{1,0:T(8,128)(2,1)S(1)} copy-done((bf16[128,768]{1,0:T(8,128)(2,1)S(1)}, bf16[128,768]{1,0:T(8,128)(2,1)}, u32[]{:S(2)}) %copy-start) | copy-done | bytes 196632
  2.2 0.4 shard_map.50
  2.6 0.2 reshape.30
  2.8 32.7 %all_to_all.10 = bf16[128,2,896]{2,1,0:T(2,128)(2,1)S(1)} all-to-all(bf16[128,2,896]{2,1,0:T(2,128)(2,1)S(1)} %reshape.30), channel_id=1, replica_groups={{480,40,408,112,336,184,264,192,96,168,24,240,464,312,392,320,32,104,47..., dimensions={0} | all-to-all | bytes 917504 | tf_op jit(solution)/shard_map/all_to_all | solution.py:144
  35.5 0.2 reshape.31.query_ref
  35.6 4.4 %collective-permute-start = (bf16[256,896]{1,0:T(8,128)(2,1)S(1)}, bf16[256,896]{1,0:T(8,128)(2,1)S(1)}, u32[]{:S(2)}, u32[]{:S(2)}) collective-permute-start(bf16[256,896]{1,0:T(8,128)(2,1)S(1)} %reshape.31.query_ref), channel_id=1, source_target_pairs={{0,3},{1,2},{2,1},{3,0},{4,7},{5,6},{6,5},{7,4},{8,11},{9,10},{10,... | collective-permute-start | bytes 1376264 | tf_op jit(solution)/shard_map/ppermute | solution.py:175
  40.0 4.0 %all_gather.7.key_ref = bf16[512,896]{1,0:T(8,128)(2,1)S(1)} all-gather(bf16[256,896]{1,0:T(8,128)(2,1)S(1)} %reshape.31.query_ref), channel_id=1, replica_groups=mesh['z'=8,'y'=8,'core'=2,'x'=4] {'core'}, dimensions={0}, use_global_device_ids=true | all-gather | bytes 1376256 | tf_op jit(solution)/shard_map/all_gather | solution.py:156
  44.1 0.9 %shard_map.51 = (f32[256,128]{1,0:T(8,128)S(1)}, f32[256,768]{1,0:T(8,128)S(1)}) custom-call(s32[1]{0:T(128)} %bitcast.2.core_ref, bf16[256,896]{1,0:T(8,128)(2,1)S(1)} %reshape.31.query_ref, bf16[512,896]{1,0:T(8,128)(2,1)S(1)} %all_gather.7.key_ref), custom_call_target="tpu_custom_call" | custom-call | flops 402653184 | bytes 2293764 | tf_op jit(solution)/shard_map/pallas_call | solution.py:132
  45.0 4.1 %collective-permute-done = bf16[256,896]{1,0:T(8,128)(2,1)S(1)} collective-permute-done((bf16[256,896]{1,0:T(8,128)(2,1)S(1)}, bf16[256,896]{1,0:T(8,128)(2,1)S(1)}, u32[]{:S(2)}, u32[]{:S(2)}) %collective-permute-start) | collective-permute-done | bytes 458784 | tf_op jit(solution)/shard_map/ppermute | solution.py:175
  49.1 4.6 %all_gather.6.key_ref = bf16[512,896]{1,0:T(8,128)(2,1)S(1)} all-gather(bf16[256,896]{1,0:T(8,128)(2,1)S(1)} %collective-permute-done), channel_id=1, replica_groups=mesh['z'=8,'y'=8,'core'=2,'x'=4] {'core'}, dimensions={0}, use_global_device_ids=true | all-gather | bytes 1376256 | tf_op jit(solution)/shard_map/all_gather | solution.py:156
  53.8 0.9 %shard_map.52 = bf16[256,896]{1,0:T(8,128)(2,1)S(1)} custom-call(bf16[256,896]{1,0:T(8,128)(2,1)S(1)} %reshape.31.query_ref, bf16[512,896]{1,0:T(8,128)(2,1)S(1)} %all_gather.6.key_ref, f32[256,128]{1,0:T(8,128)S(1)} %get-tuple-element.10.mass_ref, f32[256,768]{1,0:T(8,128)S(1)} %get-tuple-element.11.near_ref), custom_call_target="tpu_custom_call" | custom-call | flops 402653184 | bytes 2752512 | tf_op jit(solution)/shard_map/pallas_call | solution.py:132
  54.7 0.2 reshape.33
  54.8 23.7 %all_to_all.11 = bf16[128,2,896]{2,1,0:T(2,128)(2,1)S(1)} all-to-all(bf16[128,2,896]{2,1,0:T(2,128)(2,1)S(1)} %reshape.33), channel_id=1, replica_groups={{288,360,216,432,144,504,72,0,352,424,280,496,208,56,136,64,224,296,152..., dimensions={0} | all-to-all | bytes 917504 | tf_op jit(solution)/shard_map/all_to_all | solution.py:144
  78.5 0.2 reshape.34.back_ref
  78.7 0.9 %shard_map.53 = (bf16[128,768]{1,0:T(8,128)(2,1)}, bf16[1,128]{1,0:T(2,128)(2,1)}) custom-call(bf16[128,256]{1,0:T(8,128)(2,1)S(1)} %get-tuple-element.8.pick_ref, bf16[256,896]{1,0:T(8,128)(2,1)S(1)} %reshape.34.back_ref), custom_call_target="tpu_custom_call" | custom-call | flops 58720256 | bytes 721152 | tf_op jit(solution)/shard_map/pallas_call | solution.py:132
Async XLA Ops:
  0.6 0.7 copy-start.1
  0.6 0.7 copy-start.2
  1.3 0.9 %copy-start = (bf16[128,768]{1,0:T(8,128)(2,1)S(1)}, bf16[128,768]{1,0:T(8,128)(2,1)}, u32[]{:S(2)}) copy-start(bf16[128,768]{1,0:T(8,128)(2,1)} %emb_ref.1) | copy-start | bytes 589828
  35.6 13.5 %collective-permute-start = (bf16[256,896]{1,0:T(8,128)(2,1)S(1)}, bf16[256,896]{1,0:T(8,128)(2,1)S(1)}, u32[]{:S(2)}, u32[]{:S(2)}) collective-permute-start(bf16[256,896]{1,0:T(8,128)(2,1)S(1)} %reshape.31.query_ref), channel_id=1, source_target_pairs={{0,3},{1,2},{2,1},{3,0},{4,7},{5,6},{6,5},{7,4},{8,11},{9,10},{10,... | collective-permute-start | bytes 1376264 | tf_op jit(solution)/shard_map/ppermute | solution.py:175

commit v7 on v6

--- a/solution.py
+++ b/solution.py
@@ -31,16 +31,12 @@
         self.count = len(order)
         self.shift = start
 
-        def groups(order):
-            return [
-                [int(ids[z, y, core, half[h][s]]) for z, y, h in order]
-                for core in range(2)
-                for s in range(2)
-            ]
-
-        self.out = groups(order[start:] + order[:start])
-        self.back = groups(order)
-        self.pairs = [(x, grp - 1 - x) for x in range(grp)]
+        def group(order, core, s):
+            return [int(ids[z, y, core, half[h][s]]) for z, y, h in order]
+
+        turned = order[start:] + order[:start]
+        self.out = [group(turned, core, 0) + group(turned, core, 1) for core in range(2)]
+        self.back = [group(order, core, s) for core in range(2) for s in range(2)]
         self.shape = ids.shape
 
 
@@ -51,7 +47,7 @@
 
 def pack_kernel(shift, emb_ref, temp_ref, cluster_ref, send_ref, pick_ref):
     rows, width = emb_ref.shape
-    slots = send_ref.shape[0]
+    slots = pick_ref.shape[1]
 
     cluster_row = cluster_ref[...].astype(jnp.float32)
     row = lax.broadcasted_iota(jnp.int32, (rows, rows), 0)
@@ -68,7 +64,7 @@
 
     put = lax.broadcasted_iota(jnp.int32, (slots, rows), 0) == slot_row
     temp = jnp.sum(jnp.where(put, temp_ref[...].astype(jnp.float32), 0.0), axis=1, keepdims=True)
-    send_ref[:, width:] = jnp.broadcast_to(temp, (slots, EXT)).astype(jnp.bfloat16)
+    temp = jnp.broadcast_to(temp, (slots, EXT)).astype(jnp.bfloat16)
 
     values = emb_ref[...].astype(jnp.float32)
     square_mean = jnp.mean(values * values, axis=1, keepdims=True)
@@ -76,17 +72,18 @@
     placed = jnp.dot(
         jnp.where(put, 1.0, 0.0).astype(jnp.bfloat16), unit, preferred_element_type=jnp.float32
     )
-    send_ref[:, :width] = placed.astype(jnp.bfloat16)
-
-
-def weigh(query_ref, key_ref, own_start):
-    width = query_ref.shape[1] - EXT
+    placed = placed.astype(jnp.bfloat16)
+    for side in range(2):
+        send_ref[side * slots : (side + 1) * slots, :width] = placed
+        send_ref[side * slots : (side + 1) * slots, width:] = temp
+
+
+def weigh(query, key_ref, own_start):
+    width = key_ref.shape[1] - EXT
     unit = key_ref[:, :width]
-    cosine = lax.dot_general(
-        query_ref[:, :width], unit, NT, preferred_element_type=jnp.float32
-    )
+    cosine = lax.dot_general(query[:, :width], unit, NT, preferred_element_type=jnp.float32)
     key_temp = lane_to_row(key_ref[:, width:])
-    query_temp = query_ref[:, width : width + 1].astype(jnp.float32)
+    query_temp = query[:, width : width + 1].astype(jnp.float32)
     weight = jnp.exp((cosine - 1.0) * ((query_temp + key_temp) * 0.5))
     allowed = key_temp > 0.0
     if own_start is not None:
@@ -97,15 +94,22 @@
     return jnp.sum(weight, axis=1, keepdims=True), near
 
 
-def first_kernel(core_ref, query_ref, key_ref, mass_ref, near_ref):
-    mass, near = weigh(query_ref, key_ref, core_ref[0] * query_ref.shape[0])
+def query_rows(side_ref, mine_ref, slots):
+    start = pl.multiple_of(side_ref[0] * slots, slots)
+    return start, mine_ref[pl.ds(start, slots), :]
+
+
+def first_kernel(side_ref, mine_ref, mass_ref, near_ref):
+    start, query = query_rows(side_ref, mine_ref, near_ref.shape[0])
+    mass, near = weigh(query, mine_ref, start)
     mass_ref[...] = jnp.broadcast_to(mass, mass_ref.shape)
     near_ref[...] = near
 
 
-def last_kernel(shift, query_ref, key_ref, mass_ref, near_ref, out_ref):
+def last_kernel(shift, side_ref, mine_ref, key_ref, mass_ref, near_ref, out_ref):
     slots, width = near_ref.shape
-    mass, near = weigh(query_ref, key_ref, None)
+    _, query = query_rows(side_ref, mine_ref, slots)
+    mass, near = weigh(query, key_ref, None)
     mass = mass + mass_ref[:, :1]
     near = near + near_ref[...]
     neigh = NEIGH_SCALE * math.sqrt(width) * near / (1.0 + mass)
@@ -152,10 +156,6 @@
     return moved.reshape(count, wide)
 
 
-def both_cores(rows):
-    return lax.all_gather(rows, "core", axis=0, tiled=True)
-
-
 def shards(layout, embeddings, inv_temp, cluster):
     rows, width = embeddings.shape
     slots = 2 * layout.count
@@ -164,34 +164,31 @@
 
     send, pick = call(
         functools.partial(pack_kernel, layout.shift),
-        [((slots, wide), bf16), ((rows, slots), bf16)],
+        [((2 * slots, wide), bf16), ((rows, slots), bf16)],
         2 * slots * rows * width,
         embeddings,
         inv_temp.reshape(1, rows),
         cluster.reshape(1, rows),
     )
-    query = exchange(send, layout.out)
-
-    far = lax.ppermute(query, "x", layout.pairs)
-    keys = both_cores(query)
-    core = lax.axis_index("core").astype(jnp.int32).reshape(1)
-    sums = [((slots, EXT), f32), ((slots, width), f32)]
-    work = 4 * slots * width
+    mine = exchange(send, layout.out)
+    other = lax.ppermute(mine, "core", [(0, 1), (1, 0)])
+    side = (lax.axis_index("x") // 2).astype(jnp.int32).reshape(1)
+    work = 8 * slots * slots * width
+    spaces = [pltpu.SMEM] + [pltpu.VMEM] * 4
     mass, near = call(
-        first_kernel, sums, 2 * slots * work, core, query, keys,
-        spaces=[pltpu.SMEM, pltpu.VMEM, pltpu.VMEM],
-    )
-    keys = both_cores(far)
+        first_kernel, [((slots, EXT), f32), ((slots, width), f32)], work, side, mine, spaces=spaces[:2]
+    )
     (result,) = call(
         functools.partial(last_kernel, layout.shift),
         [((slots, wide), bf16)],
-        2 * slots * work,
-        query,
-        keys,
+        work,
+        side,
+        mine,
+        other,
         mass,
         near,
-    )
-
+        spaces=spaces,
+    )
     back = exchange(result, layout.back)
     neigh, dup = call(
         unpack_kernel,

time: 80 us -> 81.7 us (1.021)
  blocking collectives: 65 us -> 70.2 us
  waiting for transfers between devices: 4.14 us -> 1.17 us
  starting transfers between devices: 4.39 us -> 3.46 us
    all_to_all x2, blocking collectives: 56.3 us -> 70.2 us  [exchange(): lax.all_to_all(slots.reshape(count // 2, 2, wide), AXES, split_axis=0, co...]
    all_gather x2 -> x0, blocking collectives: 8.67 us -> none  [both_cores(): return lax.all_gather(rows, 'core', axis=0, tiled=True)]
    ppermute x1, waiting for transfers between devices: 4.14 us -> 1.17 us  [shards(): other = lax.ppermute(mine, 'core', [(0, 1), (1, 0)])]
    ppermute x1, starting transfers between devices: 4.39 us -> 3.46 us  [shards(): other = lax.ppermute(mine, 'core', [(0, 1), (1, 0)])]
where the time goes in v7:
time: 81.7 us; the launch traced here: 81.3 us
  blocking collectives  70.2 us (86%)
  starting transfers between devices  3.46 us (4%)
  Pallas kernels  3.12 us (4%)
  local copies, waits for them, and re-layouts  2.62 us (3%)
  waiting for transfers between devices  1.17 us (1%)
    all_to_all x2, blocking collectives, exchange(): lax.all_to_all(slots.reshape(count // 2, 2, wide), AXES, split_axis=0, co...  70.2 us
    ppermute x1, starting transfers between devices, shards(): other = lax.ppermute(mine, 'core', [(0, 1), (1, 0)])  3.46 us
    pallas_call x4, Pallas kernels, call(): pl.pallas_call(kernel, out_shape=shapes, in_specs=[pl.BlockSpec(memory_sp...  3.12 us
  transfers between devices with their start and end apart: 1, of which 1 were waited for; matrix products, arithmetic and copies ran while one was open for 0% of the time, Pallas kernels for 1%

profile of v7, /device:TPU:1, one launch (start us, length us, event | category | flops | bytes accessed | tf_op | source)
XLA Modules:
  0.0 81.3 jit_solution(14575098665064259606)
XLA Ops:
  0.6 0.0 copy-start.1
  0.6 0.0 copy-start.2
  0.6 0.6 copy-done.1
  1.3 0.0 copy-done.2
  1.3 0.0 copy-start
  1.3 0.9 %copy-done = bf16[128,768]{1,0:T(8,128)(2,1)S(1)} copy-done((bf16[128,768]{1,0:T(8,128)(2,1)S(1)}, bf16[128,768]{1,0:T(8,128)(2,1)}, u32[]{:S(2)}) %copy-start) | copy-done | bytes 196632
  2.2 0.4 shard_map.50
  2.6 0.3 reshape.31
  3.0 46.0 %all_to_all.10 = bf16[256,2,896]{2,1,0:T(2,128)(2,1)S(1)} all-to-all(bf16[256,2,896]{2,1,0:T(2,128)(2,1)S(1)} %reshape.31), channel_id=1, replica_groups={{480,40,408,112,336,184,264,192,96,168,24,240,464,312,392,320,32,104,47..., dimensions={0} | all-to-all | bytes 1835008 | tf_op jit(solution)/shard_map/all_to_all | solution.py:148
  49.0 0.3 reshape.32.mine_ref
  49.3 3.5 %collective-permute-start = (bf16[512,896]{1,0:T(8,128)(2,1)S(1)}, bf16[512,896]{1,0:T(8,128)(2,1)S(1)}, u32[]{:S(2)}, u32[]{:S(2)}) collective-permute-start(bf16[512,896]{1,0:T(8,128)(2,1)S(1)} %reshape.32.mine_ref), channel_id=1, source_target_pairs={{0,4},{4,0},{1,5},{5,1},{2,6},{6,2},{3,7},{7,3},{8,12},{12,8},{9,1... | collective-permute-start | bytes 2752520 | tf_op jit(solution)/shard_map/ppermute | solution.py:174
  52.8 0.9 %shard_map.51 = (f32[256,128]{1,0:T(8,128)S(1)}, f32[256,768]{1,0:T(8,128)S(1)}) custom-call(s32[1]{0:T(128)} %bitcast.2.side_ref, bf16[512,896]{1,0:T(8,128)(2,1)S(1)} %reshape.32.mine_ref), custom_call_target="tpu_custom_call" | custom-call | flops 402653184 | bytes 1835012 | tf_op jit(solution)/shard_map/pallas_call | solution.py:136
  53.7 1.2 %collective-permute-done.key_ref = bf16[512,896]{1,0:T(8,128)(2,1)S(1)} collective-permute-done((bf16[512,896]{1,0:T(8,128)(2,1)S(1)}, bf16[512,896]{1,0:T(8,128)(2,1)S(1)}, u32[]{:S(2)}, u32[]{:S(2)}) %collective-permute-start) | collective-permute-done | bytes 917536 | tf_op jit(solution)/shard_map/ppermute | solution.py:174
  54.9 0.9 %shard_map.52 = bf16[256,896]{1,0:T(8,128)(2,1)S(1)} custom-call(s32[1]{0:T(128)} %bitcast.2.side_ref, bf16[512,896]{1,0:T(8,128)(2,1)S(1)} %reshape.32.mine_ref, bf16[512,896]{1,0:T(8,128)(2,1)S(1)} %collective-permute-done.key_ref, f32[256,128]{1,0:T(8,128)S(1)} %get-tuple-element.10.mass_ref, f32[256,768]{1,0:T(8,128)S(1)} %get-tuple-element.11.near_ref), custom_call_target="tpu_custom_call" | custom-call | flops 402653184 | bytes 3211268 | tf_op jit(solution)/shard_map/pallas_call | solution.py:136
  55.8 0.2 reshape.33
  56.0 24.2 %all_to_all.11 = bf16[128,2,896]{2,1,0:T(2,128)(2,1)S(1)} all-to-all(bf16[128,2,896]{2,1,0:T(2,128)(2,1)S(1)} %reshape.33), channel_id=1, replica_groups={{288,360,216,432,144,504,72,0,352,424,280,496,208,56,136,64,224,296,152..., dimensions={0} | all-to-all | bytes 917504 | tf_op jit(solution)/shard_map/all_to_all | solution.py:148
  80.2 0.2 reshape.34.back_ref
  80.3 0.9 %shard_map.53 = (bf16[128,768]{1,0:T(8,128)(2,1)}, bf16[1,128]{1,0:T(2,128)(2,1)}) custom-call(bf16[128,256]{1,0:T(8,128)(2,1)S(1)} %get-tuple-element.8.pick_ref, bf16[256,896]{1,0:T(8,128)(2,1)S(1)} %reshape.34.back_ref), custom_call_target="tpu_custom_call" | custom-call | flops 58720256 | bytes 721152 | tf_op jit(solution)/shard_map/pallas_call | solution.py:136
Async XLA Ops:
  0.6 0.7 copy-start.1
  0.6 0.7 copy-start.2
  1.3 0.9 %copy-start = (bf16[128,768]{1,0:T(8,128)(2,1)S(1)}, bf16[128,768]{1,0:T(8,128)(2,1)}, u32[]{:S(2)}) copy-start(bf16[128,768]{1,0:T(8,128)(2,1)} %emb_ref.1) | copy-start | bytes 589828
  49.3 5.5 %collective-permute-start = (bf16[512,896]{1,0:T(8,128)(2,1)S(1)}, bf16[512,896]{1,0:T(8,128)(2,1)S(1)}, u32[]{:S(2)}, u32[]{:S(2)}) collective-permute-start(bf16[512,896]{1,0:T(8,128)(2,1)S(1)} %reshape.32.mine_ref), channel_id=1, source_target_pairs={{0,4},{4,0},{1,5},{5,1},{2,6},{6,2},{3,7},{7,3},{8,12},{12,8},{9,1... | collective-permute-start | bytes 2752520 | tf_op jit(solution)/shard_map/ppermute | solution.py:174

commit v8 on v6

--- a/solution.py
+++ b/solution.py
@@ -79,13 +79,11 @@
     send_ref[:, :width] = placed.astype(jnp.bfloat16)
 
 
-def weigh(query_ref, key_ref, own_start):
-    width = query_ref.shape[1] - EXT
-    unit = key_ref[:, :width]
+def weigh(query_ref, unit, key_temp, own_start):
+    width = unit.shape[1]
     cosine = lax.dot_general(
         query_ref[:, :width], unit, NT, preferred_element_type=jnp.float32
     )
-    key_temp = lane_to_row(key_ref[:, width:])
     query_temp = query_ref[:, width : width + 1].astype(jnp.float32)
     weight = jnp.exp((cosine - 1.0) * ((query_temp + key_temp) * 0.5))
     allowed = key_temp > 0.0
@@ -97,15 +95,18 @@
     return jnp.sum(weight, axis=1, keepdims=True), near
 
 
-def first_kernel(core_ref, query_ref, key_ref, mass_ref, near_ref):
-    mass, near = weigh(query_ref, key_ref, core_ref[0] * query_ref.shape[0])
+def first_kernel(core_ref, query_ref, key_ref, mass_ref, near_ref, temp_ref):
+    slots, width = near_ref.shape
+    temp = lane_to_row(key_ref[:, width:])
+    temp_ref[...] = jnp.broadcast_to(temp, temp_ref.shape).astype(jnp.bfloat16)
+    mass, near = weigh(query_ref, key_ref[:, :width], temp, core_ref[0] * slots)
     mass_ref[...] = jnp.broadcast_to(mass, mass_ref.shape)
     near_ref[...] = near
 
 
-def last_kernel(shift, query_ref, key_ref, mass_ref, near_ref, out_ref):
+def last_kernel(shift, query_ref, unit_ref, temp_ref, mass_ref, near_ref, out_ref):
     slots, width = near_ref.shape
-    mass, near = weigh(query_ref, key_ref, None)
+    mass, near = weigh(query_ref, unit_ref[...], temp_ref[:1].astype(jnp.float32), None)
     mass = mass + mass_ref[:, :1]
     near = near + near_ref[...]
     neigh = NEIGH_SCALE * math.sqrt(width) * near / (1.0 + mass)
@@ -141,7 +142,7 @@
 
 def exchange(slots, groups):
     count, wide = slots.shape
-    moved = lax.all_to_all(
+    return lax.all_to_all(
         slots.reshape(count // 2, 2, wide),
         AXES,
         split_axis=0,
@@ -149,7 +150,6 @@
         axis_index_groups=groups,
         tiled=True,
     )
-    return moved.reshape(count, wide)
 
 
 def both_cores(rows):
@@ -170,29 +170,35 @@
         inv_temp.reshape(1, rows),
         cluster.reshape(1, rows),
     )
-    query = exchange(send, layout.out)
-
-    far = lax.ppermute(query, "x", layout.pairs)
+    mine = exchange(send, layout.out)
+    far = lax.ppermute(mine[:, :, :width].reshape(slots, width), "x", layout.pairs)
+    query = mine.reshape(slots, wide)
     keys = both_cores(query)
     core = lax.axis_index("core").astype(jnp.int32).reshape(1)
-    sums = [((slots, EXT), f32), ((slots, width), f32)]
-    work = 4 * slots * width
-    mass, near = call(
-        first_kernel, sums, 2 * slots * work, core, query, keys,
+    work = 8 * slots * slots * width
+    mass, near, temps = call(
+        first_kernel,
+        [((slots, EXT), f32), ((slots, width), f32), ((16, 2 * slots), bf16)],
+        work,
+        core,
+        query,
+        keys,
         spaces=[pltpu.SMEM, pltpu.VMEM, pltpu.VMEM],
     )
-    keys = both_cores(far)
+    far_temps = lax.ppermute(temps, "x", layout.pairs)
+    far_keys = both_cores(far)
     (result,) = call(
         functools.partial(last_kernel, layout.shift),
         [((slots, wide), bf16)],
-        2 * slots * work,
+        work,
         query,
-        keys,
+        far_keys,
+        far_temps,
         mass,
         near,
     )
 
-    back = exchange(result, layout.back)
+    back = exchange(result, layout.back).reshape(slots, wide)
     neigh, dup = call(
         unpack_kernel,
         [((rows, width), bf16), ((1, rows), bf16)],

time: 80 us -> 78.8 us (0.985)
  waiting for transfers between devices: 4.14 us -> 0.54 us
  starting transfers between devices: 4.39 us -> 6.49 us
    ppermute x1 -> x2, waiting for transfers between devices: 4.14 us -> 0.54 us  [the longest x1 0.54 us: shards(): lax.ppermute(mine[:, :, :width].reshape(slots, width), 'x', layout.pairs)]
    ppermute x1 -> x2, starting transfers between devices: 4.39 us -> 6.49 us  [the longest x1 4.39 us: shards(): lax.ppermute(mine[:, :, :width].reshape(slots, width), 'x', layout.pairs)]
  transfers between devices with their start and end apart: 1 -> 2, of which waited for: 1 -> 1; matrix products, arithmetic and copies ran while one was open for 0% -> 0% of each run, Pallas kernels for 1% -> 1%
where the time goes in v8:
time: 78.8 us; the launch traced here: 78.3 us
  blocking collectives  64.9 us (82%)
  starting transfers between devices  6.49 us (8%)
  Pallas kernels  2.89 us (4%)
  local copies, waits for them, and re-layouts  2.7 us (3%)
    all_to_all x2, blocking collectives, exchange(): lax.all_to_all(slots.reshape(count // 2, 2, wide), AXES, split_axis=0, co...  56.3 us
    all_gather x2, blocking collectives, both_cores(): return lax.all_gather(rows, 'core', axis=0, tiled=True)  8.57 us
    ppermute x1, starting transfers between devices, shards(): lax.ppermute(mine[:, :, :width].reshape(slots, width), 'x', layout.pairs)  4.39 us
    pallas_call x4, Pallas kernels, call(): pl.pallas_call(kernel, out_shape=shapes, in_specs=[pl.BlockSpec(memory_sp...  2.89 us
    ppermute x1, starting transfers between devices, shards(): far_temps = lax.ppermute(temps, 'x', layout.pairs)  2.11 us
    unnamed x6, local copies, waits for them, and re-layouts  1.58 us
  transfers between devices with their start and end apart: 2, of which 1 were waited for; matrix products, arithmetic and copies ran while one was open for 0% of the time, Pallas kernels for 1%

profile of v8, /device:TPU:1, one launch (start us, length us, event | category | flops | bytes accessed | tf_op | source)
XLA Modules:
  0.0 78.3 jit_solution(15556796894573552548)
XLA Ops:
  0.6 0.0 copy-start.1
  0.6 0.0 copy-start.2
  0.6 0.6 copy-done.1
  1.3 0.0 copy-done.2
  1.3 0.0 copy-start
  1.3 0.9 %copy-done = bf16[128,768]{1,0:T(8,128)(2,1)S(1)} copy-done((bf16[128,768]{1,0:T(8,128)(2,1)S(1)}, bf16[128,768]{1,0:T(8,128)(2,1)}, u32[]{:S(2)}) %copy-start) | copy-done | bytes 196632
  2.2 0.4 shard_map.50
  2.6 0.2 reshape.33
  2.8 32.7 %all_to_all.10 = bf16[128,2,896]{2,1,0:T(2,128)(2,1)S(1)} all-to-all(bf16[128,2,896]{2,1,0:T(2,128)(2,1)S(1)} %reshape.33), channel_id=1, replica_groups={{480,40,408,112,336,184,264,192,96,168,24,240,464,312,392,320,32,104,47..., dimensions={0} | all-to-all | bytes 917504 | tf_op jit(solution)/shard_map/all_to_all | solution.py:145
  35.5 0.3 slice.4
  35.7 0.1 reshape.35
  35.9 4.4 %collective-permute-start = (bf16[256,768]{1,0:T(8,128)(2,1)S(1)}, bf16[256,768]{1,0:T(8,128)(2,1)S(1)}, u32[]{:S(2)}, u32[]{:S(2)}) collective-permute-start(bf16[256,768]{1,0:T(8,128)(2,1)S(1)} %reshape.35), channel_id=1, source_target_pairs={{0,3},{1,2},{2,1},{3,0},{4,7},{5,6},{6,5},{7,4},{8,11},{9,10},{10,... | collective-permute-start | bytes 1179656 | tf_op jit(solution)/shard_map/ppermute | solution.py:174
  40.3 0.2 reshape.34.query_ref
  40.5 4.0 %all_gather.7.key_ref = bf16[512,896]{1,0:T(8,128)(2,1)S(1)} all-gather(bf16[256,896]{1,0:T(8,128)(2,1)S(1)} %reshape.34.query_ref), channel_id=1, replica_groups=mesh['z'=8,'y'=8,'core'=2,'x'=4] {'core'}, dimensions={0}, use_global_device_ids=true | all-gather | bytes 1376256 | tf_op jit(solution)/shard_map/all_gather | solution.py:156
  44.5 0.8 %shard_map.51 = (f32[256,128]{1,0:T(8,128)S(1)}, f32[256,768]{1,0:T(8,128)S(1)}, bf16[16,512]{1,0:T(8,128)(2,1)S(1)}) custom-call(s32[1]{0:T(128)} %bitcast.2.core_ref, bf16[256,896]{1,0:T(8,128)(2,1)S(1)} %reshape.34.query_ref, bf16[512,896]{1,0:T(8,128)(2,1)S(1)} %all_gather.7.key_ref), custom_call_target="tpu_custom_call" | custom-call | flops 402653184 | bytes 2310148 | tf_op jit(solution)/shard_map/pallas_call | solution.py:133
  45.3 2.1 %collective-permute-start.1 = (bf16[16,512]{1,0:T(8,128)(2,1)S(1)}, bf16[16,512]{1,0:T(8,128)(2,1)S(1)}, u32[]{:S(2)}, u32[]{:S(2)}) collective-permute-start(bf16[16,512]{1,0:T(8,128)(2,1)S(1)} %get-tuple-element.11), channel_id=1, source_target_pairs={{0,3},{1,2},{2,1},{3,0},{4,7},{5,6},{6,5},{7,4},{8,11},{9,10},{10,... | collective-permute-start | bytes 49160 | tf_op jit(solution)/shard_map/ppermute | solution.py:188
  47.4 0.5 collective-permute-done
  48.0 4.6 %all_gather.6.unit_ref = bf16[512,768]{1,0:T(8,128)(2,1)S(1)} all-gather(bf16[256,768]{1,0:T(8,128)(2,1)S(1)} %collective-permute-done), channel_id=1, replica_groups=mesh['z'=8,'y'=8,'core'=2,'x'=4] {'core'}, dimensions={0}, use_global_device_ids=true | all-gather | bytes 1179648 | tf_op jit(solution)/shard_map/all_gather | solution.py:156
  52.5 0.0 collective-permute-done.1.temp_ref
  52.5 0.8 shard_map.52
  53.3 0.2 reshape.37
  53.5 23.7 %all_to_all.11 = bf16[128,2,896]{2,1,0:T(2,128)(2,1)S(1)} all-to-all(bf16[128,2,896]{2,1,0:T(2,128)(2,1)S(1)} %reshape.37), channel_id=1, replica_groups={{288,360,216,432,144,504,72,0,352,424,280,496,208,56,136,64,224,296,152..., dimensions={0} | all-to-all | bytes 917504 | tf_op jit(solution)/shard_map/all_to_all | solution.py:145
  77.1 0.2 reshape.38.back_ref
  77.3 0.9 %shard_map.53 = (bf16[128,768]{1,0:T(8,128)(2,1)}, bf16[1,128]{1,0:T(2,128)(2,1)}) custom-call(bf16[128,256]{1,0:T(8,128)(2,1)S(1)} %get-tuple-element.9.pick_ref, bf16[256,896]{1,0:T(8,128)(2,1)S(1)} %reshape.38.back_ref), custom_call_target="tpu_custom_call" | custom-call | flops 58720256 | bytes 721152 | tf_op jit(solution)/shard_map/pallas_call | solution.py:133
Async XLA Ops:
  0.6 0.7 copy-start.1
  0.6 0.7 copy-start.2
  1.3 0.9 %copy-start = (bf16[128,768]{1,0:T(8,128)(2,1)S(1)}, bf16[128,768]{1,0:T(8,128)(2,1)}, u32[]{:S(2)}) copy-start(bf16[128,768]{1,0:T(8,128)(2,1)} %emb_ref.1) | copy-start | bytes 589828
  35.9 12.1 %collective-permute-start = (bf16[256,768]{1,0:T(8,128)(2,1)S(1)}, bf16[256,768]{1,0:T(8,128)(2,1)S(1)}, u32[]{:S(2)}, u32[]{:S(2)}) collective-permute-start(bf16[256,768]{1,0:T(8,128)(2,1)S(1)} %reshape.35), channel_id=1, source_target_pairs={{0,3},{1,2},{2,1},{3,0},{4,7},{5,6},{6,5},{7,4},{8,11},{9,10},{10,... | collective-permute-start | bytes 1179656 | tf_op jit(solution)/shard_map/ppermute | solution.py:174
  45.3 7.2 %collective-permute-start.1 = (bf16[16,512]{1,0:T(8,128)(2,1)S(1)}, bf16[16,512]{1,0:T(8,128)(2,1)S(1)}, u32[]{:S(2)}, u32[]{:S(2)}) collective-permute-start(bf16[16,512]{1,0:T(8,128)(2,1)S(1)} %get-tuple-element.11), channel_id=1, source_target_pairs={{0,3},{1,2},{2,1},{3,0},{4,7},{5,6},{6,5},{7,4},{8,11},{9,10},{10,... | collective-permute-start | bytes 49160 | tf_op jit(solution)/shard_map/ppermute | solution.py:188

commit v9 on v8

--- a/solution.py
+++ b/solution.py
@@ -21,7 +21,7 @@
     def __init__(self, dp, grp):
         side = math.isqrt(dp // 2)
         ids = np.arange(dp * grp).reshape(side, side, 2, grp)
-        half = [[0, 3], [1, 2]]
+        half = [[1, 2], [0, 3]]
         mid = side // 2
         steps = sorted(range(side), key=lambda step: (min(step, side - step), step))
         order = [
@@ -49,10 +49,8 @@
     return lax.dot_general(first, ext, NT, preferred_element_type=jnp.float32)[:1]
 
 
-def pack_kernel(shift, emb_ref, temp_ref, cluster_ref, send_ref, pick_ref):
-    rows, width = emb_ref.shape
-    slots = send_ref.shape[0]
-
+def place_kernel(shift, temp_ref, cluster_ref, put_ref, temps_ref, pick_ref):
+    slots, rows = put_ref.shape
     cluster_row = cluster_ref[...].astype(jnp.float32)
     row = lax.broadcasted_iota(jnp.int32, (rows, rows), 0)
     col = lax.broadcasted_iota(jnp.int32, (rows, rows), 1)
@@ -65,18 +63,20 @@
     slot_col = jnp.where(slot_col >= slots, slot_col - slots, slot_col)
     pick = lax.broadcasted_iota(jnp.int32, (rows, slots), 1) == slot_col
     pick_ref[...] = jnp.where(pick, 1.0, 0.0).astype(jnp.bfloat16)
-
     put = lax.broadcasted_iota(jnp.int32, (slots, rows), 0) == slot_row
+    put_ref[...] = jnp.where(put, 1.0, 0.0).astype(jnp.bfloat16)
     temp = jnp.sum(jnp.where(put, temp_ref[...].astype(jnp.float32), 0.0), axis=1, keepdims=True)
-    send_ref[:, width:] = jnp.broadcast_to(temp, (slots, EXT)).astype(jnp.bfloat16)
-
+    temps_ref[...] = jnp.broadcast_to(temp, (slots, EXT)).astype(jnp.bfloat16)
+
+
+def pack_kernel(emb_ref, put_ref, temps_ref, send_ref):
+    width = emb_ref.shape[1]
     values = emb_ref[...].astype(jnp.float32)
     square_mean = jnp.mean(values * values, axis=1, keepdims=True)
     unit = (values * lax.rsqrt(square_mean + 1e-06) * (1.0 / math.sqrt(width))).astype(jnp.bfloat16)
-    placed = jnp.dot(
-        jnp.where(put, 1.0, 0.0).astype(jnp.bfloat16), unit, preferred_element_type=jnp.float32
-    )
+    placed = jnp.dot(put_ref[...], unit, preferred_element_type=jnp.float32)
     send_ref[:, :width] = placed.astype(jnp.bfloat16)
+    send_ref[:, width:] = temps_ref[...]
 
 
 def weigh(query_ref, unit, key_temp, own_start):
@@ -162,13 +162,15 @@
     wide = width + EXT
     bf16, f32 = jnp.bfloat16, jnp.float32
 
-    send, pick = call(
-        functools.partial(pack_kernel, layout.shift),
-        [((slots, wide), bf16), ((rows, slots), bf16)],
-        2 * slots * rows * width,
-        embeddings,
+    put, temps, pick = call(
+        functools.partial(place_kernel, layout.shift),
+        [((slots, rows), bf16), ((slots, EXT), bf16), ((rows, slots), bf16)],
+        2 * slots * rows * rows * rows,
         inv_temp.reshape(1, rows),
         cluster.reshape(1, rows),
+    )
+    (send,) = call(
+        pack_kernel, [((slots, wide), bf16)], 2 * slots * rows * width, embeddings, put, temps
     )
     mine = exchange(send, layout.out)
     far = lax.ppermute(mine[:, :, :width].reshape(slots, width), "x", layout.pairs)

time: 78.8 us -> 79.7 us (1.011)
  blocking collectives: 64.9 us -> 66.1 us
    all_to_all x2, blocking collectives: 56.3 us -> 57.6 us  [exchange(): lax.all_to_all(slots.reshape(count // 2, 2, wide), AXES, split_axis=0, co...]
    pallas_call x4 -> x5, Pallas kernels: 2.89 us -> 3.08 us  [call(): pl.pallas_call(kernel, out_shape=shapes, in_specs=[pl.BlockSpec(memory_sp...]
where the time goes in v9:
time: 79.7 us; the launch traced here: 79.4 us
  blocking collectives  66.1 us (83%)
  starting transfers between devices  6.49 us (8%)
  Pallas kernels  3.08 us (4%)
  local copies, waits for them, and re-layouts  2.48 us (3%)
    all_to_all x2, blocking collectives, exchange(): lax.all_to_all(slots.reshape(count // 2, 2, wide), AXES, split_axis=0, co...  57.6 us
    all_gather x2, blocking collectives, both_cores(): return lax.all_gather(rows, 'core', axis=0, tiled=True)  8.57 us
    ppermute x1, starting transfers between devices, shards(): lax.ppermute(mine[:, :, :width].reshape(slots, width), 'x', layout.pairs)  3.73 us
    pallas_call x5, Pallas kernels, call(): pl.pallas_call(kernel, out_shape=shapes, in_specs=[pl.BlockSpec(memory_sp...  3.08 us
    ppermute x1, starting transfers between devices, shards(): far_temps = lax.ppermute(temps, 'x', layout.pairs)  2.76 us
  transfers between devices with their start and end apart: 2, of which 1 were waited for; matrix products, arithmetic and copies ran while one was open for 0% of the time, Pallas kernels for 1%

profile of v9, /device:TPU:1, one launch (start us, length us, event | category | flops | bytes accessed | tf_op | source)
XLA Modules:
  0.0 79.4 jit_solution(4565709504068151350)
XLA Ops:
  0.6 0.0 copy-start.1
  0.6 0.0 copy-start.2
  0.6 0.6 copy-done.1
  1.3 0.0 copy-done.2
  1.3 0.0 copy-start
  1.3 0.2 shard_map.50
  1.5 0.7 copy-done
  2.2 0.3 shard_map.51
  2.6 0.2 reshape.33
  2.8 33.0 %all_to_all.10 = bf16[128,2,896]{2,1,0:T(2,128)(2,1)S(1)} all-to-all(bf16[128,2,896]{2,1,0:T(2,128)(2,1)S(1)} %reshape.33), channel_id=1, replica_groups={{481,41,409,113,337,185,265,193,97,169,25,241,465,313,393,321,33,105,47..., dimensions={0} | all-to-all | bytes 917504 | tf_op jit(solution)/shard_map/all_to_all | solution.py:145
  35.8 0.3 slice.4
  36.0 0.1 reshape.35
  36.2 3.7 %collective-permute-start = (bf16[256,768]{1,0:T(8,128)(2,1)S(1)}, bf16[256,768]{1,0:T(8,128)(2,1)S(1)}, u32[]{:S(2)}, u32[]{:S(2)}) collective-permute-start(bf16[256,768]{1,0:T(8,128)(2,1)S(1)} %reshape.35), channel_id=1, source_target_pairs={{0,3},{1,2},{2,1},{3,0},{4,7},{5,6},{6,5},{7,4},{8,11},{9,10},{10,... | collective-permute-start | bytes 1179656 | tf_op jit(solution)/shard_map/ppermute | solution.py:176
  39.9 0.2 reshape.34.query_ref
  40.1 4.0 %all_gather.7.key_ref = bf16[512,896]{1,0:T(8,128)(2,1)S(1)} all-gather(bf16[256,896]{1,0:T(8,128)(2,1)S(1)} %reshape.34.query_ref), channel_id=1, replica_groups=mesh['z'=8,'y'=8,'core'=2,'x'=4] {'core'}, dimensions={0}, use_global_device_ids=true | all-gather | bytes 1376256 | tf_op jit(solution)/shard_map/all_gather | solution.py:156
  44.1 0.8 %shard_map.52 = (f32[256,128]{1,0:T(8,128)S(1)}, f32[256,768]{1,0:T(8,128)S(1)}, bf16[16,512]{1,0:T(8,128)(2,1)S(1)}) custom-call(s32[1]{0:T(128)} %bitcast.2.core_ref, bf16[256,896]{1,0:T(8,128)(2,1)S(1)} %reshape.34.query_ref, bf16[512,896]{1,0:T(8,128)(2,1)S(1)} %all_gather.7.key_ref), custom_call_target="tpu_custom_call" | custom-call | flops 402653184 | bytes 2310148 | tf_op jit(solution)/shard_map/pallas_call | solution.py:133
  45.0 2.8 %collective-permute-start.1 = (bf16[16,512]{1,0:T(8,128)(2,1)S(1)}, bf16[16,512]{1,0:T(8,128)(2,1)S(1)}, u32[]{:S(2)}, u32[]{:S(2)}) collective-permute-start(bf16[16,512]{1,0:T(8,128)(2,1)S(1)} %get-tuple-element.13), channel_id=1, source_target_pairs={{0,3},{1,2},{2,1},{3,0},{4,7},{5,6},{6,5},{7,4},{8,11},{9,10},{10,... | collective-permute-start | bytes 49160 | tf_op jit(solution)/shard_map/ppermute | solution.py:190
  47.7 0.5 collective-permute-done
  48.3 4.6 %all_gather.6.unit_ref = bf16[512,768]{1,0:T(8,128)(2,1)S(1)} all-gather(bf16[256,768]{1,0:T(8,128)(2,1)S(1)} %collective-permute-done), channel_id=1, replica_groups=mesh['z'=8,'y'=8,'core'=2,'x'=4] {'core'}, dimensions={0}, use_global_device_ids=true | all-gather | bytes 1179648 | tf_op jit(solution)/shard_map/all_gather | solution.py:156
  52.8 0.0 collective-permute-done.1.temp_ref
  52.8 0.8 shard_map.53
  53.6 0.2 reshape.37
  53.8 24.6 %all_to_all.11 = bf16[128,2,896]{2,1,0:T(2,128)(2,1)S(1)} all-to-all(bf16[128,2,896]{2,1,0:T(2,128)(2,1)S(1)} %reshape.37), channel_id=1, replica_groups={{289,361,217,433,145,505,73,1,353,425,281,497,209,57,137,65,225,297,153..., dimensions={0} | all-to-all | bytes 917504 | tf_op jit(solution)/shard_map/all_to_all | solution.py:145
  78.3 0.2 reshape.38.back_ref
  78.5 0.9 %shard_map.54 = (bf16[128,768]{1,0:T(8,128)(2,1)}, bf16[1,128]{1,0:T(2,128)(2,1)}) custom-call(bf16[128,256]{1,0:T(8,128)(2,1)S(1)} %get-tuple-element.10.pick_ref, bf16[256,896]{1,0:T(8,128)(2,1)S(1)} %reshape.38.back_ref), custom_call_target="tpu_custom_call" | custom-call | flops 58720256 | bytes 721152 | tf_op jit(solution)/shard_map/pallas_call | solution.py:133
Async XLA Ops:
  0.6 0.7 copy-start.1
  0.6 0.7 copy-start.2
  1.3 0.9 %copy-start = (bf16[128,768]{1,0:T(8,128)(2,1)S(1)}, bf16[128,768]{1,0:T(8,128)(2,1)}, u32[]{:S(2)}) copy-start(bf16[128,768]{1,0:T(8,128)(2,1)} %emb_ref.1) | copy-start | bytes 589828
  36.2 12.1 %collective-permute-start = (bf16[256,768]{1,0:T(8,128)(2,1)S(1)}, bf16[256,768]{1,0:T(8,128)(2,1)S(1)}, u32[]{:S(2)}, u32[]{:S(2)}) collective-permute-start(bf16[256,768]{1,0:T(8,128)(2,1)S(1)} %reshape.35), channel_id=1, source_target_pairs={{0,3},{1,2},{2,1},{3,0},{4,7},{5,6},{6,5},{7,4},{8,11},{9,10},{10,... | collective-permute-start | bytes 1179656 | tf_op jit(solution)/shard_map/ppermute | solution.py:176
  45.0 7.9 %collective-permute-start.1 = (bf16[16,512]{1,0:T(8,128)(2,1)S(1)}, bf16[16,512]{1,0:T(8,128)(2,1)S(1)}, u32[]{:S(2)}, u32[]{:S(2)}) collective-permute-start(bf16[16,512]{1,0:T(8,128)(2,1)S(1)} %get-tuple-element.13), channel_id=1, source_target_pairs={{0,3},{1,2},{2,1},{3,0},{4,7},{5,6},{6,5},{7,4},{8,11},{9,10},{10,... | collective-permute-start | bytes 49160 | tf_op jit(solution)/shard_map/ppermute | solution.py:190

commit v10 on v8

--- a/solution.py
+++ b/solution.py
@@ -98,7 +98,7 @@
 def first_kernel(core_ref, query_ref, key_ref, mass_ref, near_ref, temp_ref):
     slots, width = near_ref.shape
     temp = lane_to_row(key_ref[:, width:])
-    temp_ref[...] = jnp.broadcast_to(temp, temp_ref.shape).astype(jnp.bfloat16)
+    temp_ref[...] = jnp.broadcast_to(temp, temp_ref.shape)
     mass, near = weigh(query_ref, key_ref[:, :width], temp, core_ref[0] * slots)
     mass_ref[...] = jnp.broadcast_to(mass, mass_ref.shape)
     near_ref[...] = near
@@ -106,7 +106,7 @@
 
 def last_kernel(shift, query_ref, unit_ref, temp_ref, mass_ref, near_ref, out_ref):
     slots, width = near_ref.shape
-    mass, near = weigh(query_ref, unit_ref[...], temp_ref[:1].astype(jnp.float32), None)
+    mass, near = weigh(query_ref, unit_ref[...], temp_ref[:1], None)
     mass = mass + mass_ref[:, :1]
     near = near + near_ref[...]
     neigh = NEIGH_SCALE * math.sqrt(width) * near / (1.0 + mass)
@@ -171,14 +171,14 @@
         cluster.reshape(1, rows),
     )
     mine = exchange(send, layout.out)
-    far = lax.ppermute(mine[:, :, :width].reshape(slots, width), "x", layout.pairs)
-    query = mine.reshape(slots, wide)
+    query = lax.optimization_barrier(mine.reshape(slots, wide))
+    far = lax.ppermute(query[:, :width], "x", layout.pairs)
     keys = both_cores(query)
     core = lax.axis_index("core").astype(jnp.int32).reshape(1)
     work = 8 * slots * slots * width
     mass, near, temps = call(
         first_kernel,
-        [((slots, EXT), f32), ((slots, width), f32), ((16, 2 * slots), bf16)],
+        [((slots, EXT), f32), ((slots, width), f32), ((8, 2 * slots), f32)],
         work,
         core,
         query,

time: 78.8 us -> 78.6 us (level)
  no operation moved by 1% of the time
where the time goes in v10:
time: 78.6 us; the launch traced here: 78 us
  blocking collectives  64.9 us (83%)
  starting transfers between devices  6.49 us (8%)
  Pallas kernels  2.89 us (4%)
  local copies, waits for them, and re-layouts  2.3 us (3%)
    all_to_all x2, blocking collectives, exchange(): lax.all_to_all(slots.reshape(count // 2, 2, wide), AXES, split_axis=0, co...  56.3 us
    all_gather x2, blocking collectives, both_cores(): return lax.all_gather(rows, 'core', axis=0, tiled=True)  8.57 us
    ppermute x1, starting transfers between devices, shards(): far = lax.ppermute(query[:, :width], 'x', layout.pairs)  4.39 us
    pallas_call x4, Pallas kernels, call(): pl.pallas_call(kernel, out_shape=shapes, in_specs=[pl.BlockSpec(memory_sp...  2.89 us
    ppermute x1, starting transfers between devices, shards(): far_temps = lax.ppermute(temps, 'x', layout.pairs)  2.11 us
    unnamed x6, local copies, waits for them, and re-layouts  1.58 us
  transfers between devices with their start and end apart: 2, of which 1 were waited for; matrix products, arithmetic and copies ran while one was open for 0% of the time, Pallas kernels for 1%

profile of v10, /device:TPU:1, one launch (start us, length us, event | category | flops | bytes accessed | tf_op | source)
XLA Modules:
  0.0 78.0 jit_solution(13450974629812954714)
XLA Ops:
  0.6 0.0 copy-start.1
  0.6 0.0 copy-start.2
  0.6 0.6 copy-done.1
  1.3 0.0 copy-done.2
  1.3 0.0 copy-start
  1.3 0.9 %copy-done = bf16[128,768]{1,0:T(8,128)(2,1)S(1)} copy-done((bf16[128,768]{1,0:T(8,128)(2,1)S(1)}, bf16[128,768]{1,0:T(8,128)(2,1)}, u32[]{:S(2)}) %copy-start) | copy-done | bytes 196632
  2.2 0.4 shard_map.50
  2.6 0.2 reshape.30
  2.8 32.7 %all_to_all.10 = bf16[128,2,896]{2,1,0:T(2,128)(2,1)S(1)} all-to-all(bf16[128,2,896]{2,1,0:T(2,128)(2,1)S(1)} %reshape.30), channel_id=1, replica_groups={{480,40,408,112,336,184,264,192,96,168,24,240,464,312,392,320,32,104,47..., dimensions={0} | all-to-all | bytes 917504 | tf_op jit(solution)/shard_map/all_to_all | solution.py:145
  35.5 0.2 reshape.31.query_ref
  35.7 4.4 %collective-permute-start = (bf16[256,768]{1,0:T(8,128)(2,1)S(1)}, bf16[256,768]{1,0:T(8,128)(2,1)S(1)}, u32[]{:S(2)}, u32[]{:S(2)}) collective-permute-start(bf16[256,768]{1,0:T(8,128)(2,1)S(1)} %slice.4), channel_id=1, source_target_pairs={{0,3},{1,2},{2,1},{3,0},{4,7},{5,6},{6,5},{7,4},{8,11},{9,10},{10,... | collective-permute-start | bytes 1179656 | tf_op jit(solution)/shard_map/ppermute | solution.py:175
  40.1 4.0 %all_gather.7.key_ref = bf16[512,896]{1,0:T(8,128)(2,1)S(1)} all-gather(bf16[256,896]{1,0:T(8,128)(2,1)S(1)} %reshape.31.query_ref), channel_id=1, replica_groups=mesh['z'=8,'y'=8,'core'=2,'x'=4] {'core'}, dimensions={0}, use_global_device_ids=true | all-gather | bytes 1376256 | tf_op jit(solution)/shard_map/all_gather | solution.py:156
  44.1 0.8 %shard_map.51 = (f32[256,128]{1,0:T(8,128)S(1)}, f32[256,768]{1,0:T(8,128)S(1)}, f32[8,512]{1,0:T(8,128)S(1)}) custom-call(s32[1]{0:T(128)} %bitcast.2.core_ref, bf16[256,896]{1,0:T(8,128)(2,1)S(1)} %reshape.31.query_ref, bf16[512,896]{1,0:T(8,128)(2,1)S(1)} %all_gather.7.key_ref), custom_call_target="tpu_custom_call" | custom-call | flops 402653184 | bytes 2310148 | tf_op jit(solution)/shard_map/pallas_call | solution.py:133
  44.9 2.1 %collective-permute-start.1 = (f32[8,512]{1,0:T(8,128)S(1)}, f32[8,512]{1,0:T(8,128)S(1)}, u32[]{:S(2)}, u32[]{:S(2)}) collective-permute-start(f32[8,512]{1,0:T(8,128)S(1)} %get-tuple-element.11), channel_id=1, source_target_pairs={{0,3},{1,2},{2,1},{3,0},{4,7},{5,6},{6,5},{7,4},{8,11},{9,10},{10,... | collective-permute-start | bytes 49160 | tf_op jit(solution)/shard_map/ppermute | solution.py:188
  47.0 0.7 collective-permute-done
  47.7 4.6 %all_gather.6.unit_ref = bf16[512,768]{1,0:T(8,128)(2,1)S(1)} all-gather(bf16[256,768]{1,0:T(8,128)(2,1)S(1)} %collective-permute-done), channel_id=1, replica_groups=mesh['z'=8,'y'=8,'core'=2,'x'=4] {'core'}, dimensions={0}, use_global_device_ids=true | all-gather | bytes 1179648 | tf_op jit(solution)/shard_map/all_gather | solution.py:156
  52.3 0.0 collective-permute-done.1.temp_ref
  52.3 0.8 shard_map.52
  53.1 0.2 reshape.33
  53.2 23.6 %all_to_all.11 = bf16[128,2,896]{2,1,0:T(2,128)(2,1)S(1)} all-to-all(bf16[128,2,896]{2,1,0:T(2,128)(2,1)S(1)} %reshape.33), channel_id=1, replica_groups={{288,360,216,432,144,504,72,0,352,424,280,496,208,56,136,64,224,296,152..., dimensions={0} | all-to-all | bytes 917504 | tf_op jit(solution)/shard_map/all_to_all | solution.py:145
  76.9 0.2 reshape.34.back_ref
  77.1 0.9 %shard_map.53 = (bf16[128,768]{1,0:T(8,128)(2,1)}, bf16[1,128]{1,0:T(2,128)(2,1)}) custom-call(bf16[128,256]{1,0:T(8,128)(2,1)S(1)} %get-tuple-element.9.pick_ref, bf16[256,896]{1,0:T(8,128)(2,1)S(1)} %reshape.34.back_ref), custom_call_target="tpu_custom_call" | custom-call | flops 58720256 | bytes 721152 | tf_op jit(solution)/shard_map/pallas_call | solution.py:133
  (1 shorter events, 0.0 us)
Async XLA Ops:
  0.6 0.7 copy-start.1
  0.6 0.7 copy-start.2
  1.3 0.9 %copy-start = (bf16[128,768]{1,0:T(8,128)(2,1)S(1)}, bf16[128,768]{1,0:T(8,128)(2,1)}, u32[]{:S(2)}) copy-start(bf16[128,768]{1,0:T(8,128)(2,1)} %emb_ref.1) | copy-start | bytes 589828
  35.7 12.1 %collective-permute-start = (bf16[256,768]{1,0:T(8,128)(2,1)S(1)}, bf16[256,768]{1,0:T(8,128)(2,1)S(1)}, u32[]{:S(2)}, u32[]{:S(2)}) collective-permute-start(bf16[256,768]{1,0:T(8,128)(2,1)S(1)} %slice.4), channel_id=1, source_target_pairs={{0,3},{1,2},{2,1},{3,0},{4,7},{5,6},{6,5},{7,4},{8,11},{9,10},{10,... | collective-permute-start | bytes 1179656 | tf_op jit(solution)/shard_map/ppermute | solution.py:175
  44.9 7.4 %collective-permute-start.1 = (f32[8,512]{1,0:T(8,128)S(1)}, f32[8,512]{1,0:T(8,128)S(1)}, u32[]{:S(2)}, u32[]{:S(2)}) collective-permute-start(f32[8,512]{1,0:T(8,128)S(1)} %get-tuple-element.11), channel_id=1, source_target_pairs={{0,3},{1,2},{2,1},{3,0},{4,7},{5,6},{6,5},{7,4},{8,11},{9,10},{10,... | collective-permute-start | bytes 49160 | tf_op jit(solution)/shard_map/ppermute | solution.py:188

commit v11 on v10

--- a/solution.py
+++ b/solution.py
@@ -49,17 +49,26 @@
     return lax.dot_general(first, ext, NT, preferred_element_type=jnp.float32)[:1]
 
 
-def pack_kernel(shift, emb_ref, temp_ref, cluster_ref, send_ref, pick_ref):
+def order_kernel(same_ref, before_ref):
+    row = lax.broadcasted_iota(jnp.int32, same_ref.shape, 0)
+    col = lax.broadcasted_iota(jnp.int32, same_ref.shape, 1)
+    same_ref[...] = jnp.where(row == col, 1.0, 0.0)
+    before_ref[...] = jnp.where(row < col, 1.0, 0.0)
+
+
+def pack_kernel(
+    shift, emb_ref, temp_ref, cluster_ref, same_ref, before_ref, send_ref, pick_ref
+):
     rows, width = emb_ref.shape
     slots = send_ref.shape[0]
 
     cluster_row = cluster_ref[...].astype(jnp.float32)
-    row = lax.broadcasted_iota(jnp.int32, (rows, rows), 0)
-    col = lax.broadcasted_iota(jnp.int32, (rows, rows), 1)
-    cluster_col = jnp.sum(jnp.where(row == col, cluster_row, 0.0), axis=1, keepdims=True)
-    same = cluster_row == cluster_col
-    rank_row = jnp.sum(jnp.where(same & (row < col), 1.0, 0.0), axis=0, keepdims=True)
-    rank_col = jnp.sum(jnp.where(same & (col < row), 1.0, 0.0), axis=1, keepdims=True)
+    before = before_ref[...]
+    after = 1.0 - before - same_ref[...]
+    cluster_col = jnp.sum(same_ref[...] * cluster_row, axis=1, keepdims=True)
+    alike = cluster_row == cluster_col
+    rank_row = jnp.sum(jnp.where(alike, before, 0.0), axis=0, keepdims=True)
+    rank_col = jnp.sum(jnp.where(alike, after, 0.0), axis=1, keepdims=True)
     slot_row = (2.0 * cluster_row + rank_row).astype(jnp.int32)
     slot_col = (2.0 * cluster_col + rank_col).astype(jnp.int32) + 2 * shift
     slot_col = jnp.where(slot_col >= slots, slot_col - slots, slot_col)
@@ -162,6 +171,7 @@
     wide = width + EXT
     bf16, f32 = jnp.bfloat16, jnp.float32
 
+    same, before = call(order_kernel, [((rows, rows), f32)] * 2, 8 * rows * rows * rows * rows)
     send, pick = call(
         functools.partial(pack_kernel, layout.shift),
         [((slots, wide), bf16), ((rows, slots), bf16)],
@@ -169,6 +179,8 @@
         embeddings,
         inv_temp.reshape(1, rows),
         cluster.reshape(1, rows),
+        same,
+        before,
     )
     mine = exchange(send, layout.out)
     query = lax.optimization_barrier(mine.reshape(slots, wide))

time: 78.6 us -> 77.9 us (level)
    pallas_call x4 -> x5, Pallas kernels: 2.89 us -> 2.92 us  [call(): pl.pallas_call(kernel, out_shape=shapes, in_specs=[pl.BlockSpec(memory_sp...]
where the time goes in v11:
time: 77.9 us; the launch traced here: 77.4 us
  blocking collectives  64.9 us (83%)
  starting transfers between devices  6.49 us (8%)
  Pallas kernels  2.92 us (4%)
  local copies, waits for them, and re-layouts  1.61 us (2%)
    all_to_all x2, blocking collectives, exchange(): lax.all_to_all(slots.reshape(count // 2, 2, wide), AXES, split_axis=0, co...  56.3 us
    all_gather x2, blocking collectives, both_cores(): return lax.all_gather(rows, 'core', axis=0, tiled=True)  8.57 us
    ppermute x1, starting transfers between devices, shards(): far = lax.ppermute(query[:, :width], 'x', layout.pairs)  4.4 us
    pallas_call x5, Pallas kernels, call(): pl.pallas_call(kernel, out_shape=shapes, in_specs=[pl.BlockSpec(memory_sp...  2.92 us
    ppermute x1, starting transfers between devices, shards(): far_temps = lax.ppermute(temps, 'x', layout.pairs)  2.1 us
  transfers between devices with their start and end apart: 2, of which 1 were waited for; matrix products, arithmetic and copies ran while one was open for 0% of the time, Pallas kernels for 1%

profile of v11, /device:TPU:1, one launch (start us, length us, event | category | flops | bytes accessed | tf_op | source)
XLA Modules:
  0.0 77.4 jit_solution(17145505524059477019)
XLA Ops:
  0.6 0.0 copy-start
  0.7 0.0 copy-start.1
  0.7 0.0 copy-start.2
  0.7 0.9 %copy-done = bf16[128,768]{1,0:T(8,128)(2,1)S(1)} copy-done((bf16[128,768]{1,0:T(8,128)(2,1)S(1)}, bf16[128,768]{1,0:T(8,128)(2,1)}, u32[]{:S(2)}) %copy-start) | copy-done | bytes 196632
  1.6 0.0 copy-done.1
  1.6 0.0 copy-done.2
  1.6 0.4 shard_map.51
  2.0 0.2 reshape.30
  2.1 32.7 %all_to_all.10 = bf16[128,2,896]{2,1,0:T(2,128)(2,1)S(1)} all-to-all(bf16[128,2,896]{2,1,0:T(2,128)(2,1)S(1)} %reshape.30), channel_id=1, replica_groups={{480,40,408,112,336,184,264,192,96,168,24,240,464,312,392,320,32,104,47..., dimensions={0} | all-to-all | bytes 917504 | tf_op jit(solution)/shard_map/all_to_all | solution.py:154
  34.8 0.2 reshape.31.query_ref
  35.0 4.4 %collective-permute-start = (bf16[256,768]{1,0:T(8,128)(2,1)S(1)}, bf16[256,768]{1,0:T(8,128)(2,1)S(1)}, u32[]{:S(2)}, u32[]{:S(2)}) collective-permute-start(bf16[256,768]{1,0:T(8,128)(2,1)S(1)} %slice.4), channel_id=1, source_target_pairs={{0,3},{1,2},{2,1},{3,0},{4,7},{5,6},{6,5},{7,4},{8,11},{9,10},{10,... | collective-permute-start | bytes 1179656 | tf_op jit(solution)/shard_map/ppermute | solution.py:187
  39.4 4.0 %all_gather.7.key_ref = bf16[512,896]{1,0:T(8,128)(2,1)S(1)} all-gather(bf16[256,896]{1,0:T(8,128)(2,1)S(1)} %reshape.31.query_ref), channel_id=1, replica_groups=mesh['z'=8,'y'=8,'core'=2,'x'=4] {'core'}, dimensions={0}, use_global_device_ids=true | all-gather | bytes 1376256 | tf_op jit(solution)/shard_map/all_gather | solution.py:165
  43.4 0.8 %shard_map.52 = (f32[256,128]{1,0:T(8,128)S(1)}, f32[256,768]{1,0:T(8,128)S(1)}, f32[8,512]{1,0:T(8,128)S(1)}) custom-call(s32[1]{0:T(128)} %bitcast.2.core_ref, bf16[256,896]{1,0:T(8,128)(2,1)S(1)} %reshape.31.query_ref, bf16[512,896]{1,0:T(8,128)(2,1)S(1)} %all_gather.7.key_ref), custom_call_target="tpu_custom_call" | custom-call | flops 402653184 | bytes 2310148 | tf_op jit(solution)/shard_map/pallas_call | solution.py:142
  44.3 2.1 %collective-permute-start.1 = (f32[8,512]{1,0:T(8,128)S(1)}, f32[8,512]{1,0:T(8,128)S(1)}, u32[]{:S(2)}, u32[]{:S(2)}) collective-permute-start(f32[8,512]{1,0:T(8,128)S(1)} %get-tuple-element.15), channel_id=1, source_target_pairs={{0,3},{1,2},{2,1},{3,0},{4,7},{5,6},{6,5},{7,4},{8,11},{9,10},{10,... | collective-permute-start | bytes 49160 | tf_op jit(solution)/shard_map/ppermute | solution.py:200
  46.4 0.7 collective-permute-done
  47.1 4.6 %all_gather.6.unit_ref = bf16[512,768]{1,0:T(8,128)(2,1)S(1)} all-gather(bf16[256,768]{1,0:T(8,128)(2,1)S(1)} %collective-permute-done), channel_id=1, replica_groups=mesh['z'=8,'y'=8,'core'=2,'x'=4] {'core'}, dimensions={0}, use_global_device_ids=true | all-gather | bytes 1179648 | tf_op jit(solution)/shard_map/all_gather | solution.py:165
  51.6 0.0 collective-permute-done.1.temp_ref
  51.6 0.8 shard_map.53
  52.4 0.2 reshape.33
  52.6 23.7 %all_to_all.11 = bf16[128,2,896]{2,1,0:T(2,128)(2,1)S(1)} all-to-all(bf16[128,2,896]{2,1,0:T(2,128)(2,1)S(1)} %reshape.33), channel_id=1, replica_groups={{288,360,216,432,144,504,72,0,352,424,280,496,208,56,136,64,224,296,152..., dimensions={0} | all-to-all | bytes 917504 | tf_op jit(solution)/shard_map/all_to_all | solution.py:154
  76.3 0.2 reshape.34.back_ref
  76.4 0.9 %shard_map.54 = (bf16[128,768]{1,0:T(8,128)(2,1)}, bf16[1,128]{1,0:T(2,128)(2,1)}) custom-call(bf16[128,256]{1,0:T(8,128)(2,1)S(1)} %get-tuple-element.13.pick_ref, bf16[256,896]{1,0:T(8,128)(2,1)S(1)} %reshape.34.back_ref), custom_call_target="tpu_custom_call" | custom-call | flops 58720256 | bytes 721152 | tf_op jit(solution)/shard_map/pallas_call | solution.py:142
  (2 shorter events, 0.0 us)
Async XLA Ops:
  0.6 0.9 %copy-start = (bf16[128,768]{1,0:T(8,128)(2,1)S(1)}, bf16[128,768]{1,0:T(8,128)(2,1)}, u32[]{:S(2)}) copy-start(bf16[128,768]{1,0:T(8,128)(2,1)} %emb_ref.1) | copy-start | bytes 589828
  0.7 0.9 %copy-start.1 = (bf16[128]{0:T(256)(128)(2,1)S(1)}, bf16[128]{0:T(256)(128)(2,1)}, u32[]{:S(2)}) copy-start(bf16[128]{0:T(256)(128)(2,1)} %param.4) | copy-start | bytes 772
  0.7 0.9 %copy-start.2 = (s32[128,1]{0,1:T(1,128)S(1)}, s32[128,1]{0,1:T(1,128)}, u32[]{:S(2)}) copy-start(s32[128,1]{0,1:T(1,128)} %param.5) | copy-start | bytes 1540
  35.0 12.1 %collective-permute-start = (bf16[256,768]{1,0:T(8,128)(2,1)S(1)}, bf16[256,768]{1,0:T(8,128)(2,1)S(1)}, u32[]{:S(2)}, u32[]{:S(2)}) collective-permute-start(bf16[256,768]{1,0:T(8,128)(2,1)S(1)} %slice.4), channel_id=1, source_target_pairs={{0,3},{1,2},{2,1},{3,0},{4,7},{5,6},{6,5},{7,4},{8,11},{9,10},{10,... | collective-permute-start | bytes 1179656 | tf_op jit(solution)/shard_map/ppermute | solution.py:187
  44.3 7.4 %collective-permute-start.1 = (f32[8,512]{1,0:T(8,128)S(1)}, f32[8,512]{1,0:T(8,128)S(1)}, u32[]{:S(2)}, u32[]{:S(2)}) collective-permute-start(f32[8,512]{1,0:T(8,128)S(1)} %get-tuple-element.15), channel_id=1, source_target_pairs={{0,3},{1,2},{2,1},{3,0},{4,7},{5,6},{6,5},{7,4},{8,11},{9,10},{10,... | collective-permute-start | bytes 49160 | tf_op jit(solution)/shard_map/ppermute | solution.py:200

commit v12 on v11

--- a/solution.py
+++ b/solution.py
@@ -27,19 +27,20 @@
         order = [
             ((a + b + mid) % side, (a + mid) % side, h) for h in range(2) for b in steps for a in steps
         ]
-        start = order.index((side - 1, mid, 0))
+        first_out = order.index((side - 1, mid + 1, 0))
+        first_back = order.index((mid, mid + 1, 0))
         self.count = len(order)
-        self.shift = start
-
-        def groups(order):
+        self.shift = (first_out - first_back) % self.count
+
+        def groups(start):
             return [
-                [int(ids[z, y, core, half[h][s]]) for z, y, h in order]
+                [int(ids[z, y, core, half[h][s]]) for z, y, h in order[start:] + order[:start]]
                 for core in range(2)
                 for s in range(2)
             ]
 
-        self.out = groups(order[start:] + order[:start])
-        self.back = groups(order)
+        self.out = groups(first_out)
+        self.back = groups(first_back)
         self.pairs = [(x, grp - 1 - x) for x in range(grp)]
         self.shape = ids.shape
 

time: 77.9 us -> 77.6 us (level)
  transfers between devices with their start and end apart: 2 -> 2, of which waited for: 1 -> 0; matrix products, arithmetic and copies ran while one was open for 0% -> 0% of each run, Pallas kernels for 1% -> 1%
where the time goes in v12:
time: 77.6 us; the launch traced here: 76.9 us
  blocking collectives  64.9 us (84%)
  starting transfers between devices  6.74 us (9%)
  Pallas kernels  2.91 us (4%)
  local copies, waits for them, and re-layouts  1.61 us (2%)
    all_to_all x2, blocking collectives, exchange(): lax.all_to_all(slots.reshape(count // 2, 2, wide), AXES, split_axis=0, co...  55.8 us
    all_gather x2, blocking collectives, both_cores(): return lax.all_gather(rows, 'core', axis=0, tiled=True)  9.09 us
    ppermute x1, starting transfers between devices, shards(): far = lax.ppermute(query[:, :width], 'x', layout.pairs)  4.64 us
    pallas_call x5, Pallas kernels, call(): pl.pallas_call(kernel, out_shape=shapes, in_specs=[pl.BlockSpec(memory_sp...  2.91 us
    ppermute x1, starting transfers between devices, shards(): far_temps = lax.ppermute(temps, 'x', layout.pairs)  2.11 us
  transfers between devices with their start and end apart: 2, of which 0 were waited for; matrix products, arithmetic and copies ran while one was open for 0% of the time, Pallas kernels for 1%

profile of v12, /device:TPU:1, one launch (start us, length us, event | category | flops | bytes accessed | tf_op | source)
XLA Modules:
  0.0 76.9 jit_solution(15131732956553118313)
XLA Ops:
  0.6 0.0 copy-start
  0.7 0.0 copy-start.1
  0.7 0.0 copy-start.2
  0.7 0.9 %copy-done = bf16[128,768]{1,0:T(8,128)(2,1)S(1)} copy-done((bf16[128,768]{1,0:T(8,128)(2,1)S(1)}, bf16[128,768]{1,0:T(8,128)(2,1)}, u32[]{:S(2)}) %copy-start) | copy-done | bytes 196632
  1.6 0.0 copy-done.1
  1.6 0.0 copy-done.2
  1.6 0.4 shard_map.51
  2.0 0.2 reshape.30
  2.1 32.2 %all_to_all.10 = bf16[128,2,896]{2,1,0:T(2,128)(2,1)S(1)} all-to-all(bf16[128,2,896]{2,1,0:T(2,128)(2,1)S(1)} %reshape.30), channel_id=1, replica_groups={{488,344,48,272,120,200,128,160,232,88,304,16,376,456,384,480,40,408,11..., dimensions={0} | all-to-all | bytes 917504 | tf_op jit(solution)/shard_map/all_to_all | solution.py:155
  34.3 0.2 reshape.31.query_ref
  34.5 4.6 %collective-permute-start = (bf16[256,768]{1,0:T(8,128)(2,1)S(1)}, bf16[256,768]{1,0:T(8,128)(2,1)S(1)}, u32[]{:S(2)}, u32[]{:S(2)}) collective-permute-start(bf16[256,768]{1,0:T(8,128)(2,1)S(1)} %slice.4), channel_id=1, source_target_pairs={{0,3},{1,2},{2,1},{3,0},{4,7},{5,6},{6,5},{7,4},{8,11},{9,10},{10,... | collective-permute-start | bytes 1179656 | tf_op jit(solution)/shard_map/ppermute | solution.py:188
  39.2 4.3 %all_gather.7.key_ref = bf16[512,896]{1,0:T(8,128)(2,1)S(1)} all-gather(bf16[256,896]{1,0:T(8,128)(2,1)S(1)} %reshape.31.query_ref), channel_id=1, replica_groups=mesh['z'=8,'y'=8,'core'=2,'x'=4] {'core'}, dimensions={0}, use_global_device_ids=true | all-gather | bytes 1376256 | tf_op jit(solution)/shard_map/all_gather | solution.py:166
  43.4 0.8 %shard_map.52 = (f32[256,128]{1,0:T(8,128)S(1)}, f32[256,768]{1,0:T(8,128)S(1)}, f32[8,512]{1,0:T(8,128)S(1)}) custom-call(s32[1]{0:T(128)} %bitcast.2.core_ref, bf16[256,896]{1,0:T(8,128)(2,1)S(1)} %reshape.31.query_ref, bf16[512,896]{1,0:T(8,128)(2,1)S(1)} %all_gather.7.key_ref), custom_call_target="tpu_custom_call" | custom-call | flops 402653184 | bytes 2310148 | tf_op jit(solution)/shard_map/pallas_call | solution.py:143
  44.2 2.1 %collective-permute-start.1 = (f32[8,512]{1,0:T(8,128)S(1)}, f32[8,512]{1,0:T(8,128)S(1)}, u32[]{:S(2)}, u32[]{:S(2)}) collective-permute-start(f32[8,512]{1,0:T(8,128)S(1)} %get-tuple-element.15), channel_id=1, source_target_pairs={{0,3},{1,2},{2,1},{3,0},{4,7},{5,6},{6,5},{7,4},{8,11},{9,10},{10,... | collective-permute-start | bytes 49160 | tf_op jit(solution)/shard_map/ppermute | solution.py:201
  46.4 0.0 collective-permute-done
  46.4 4.8 %all_gather.6.unit_ref = bf16[512,768]{1,0:T(8,128)(2,1)S(1)} all-gather(bf16[256,768]{1,0:T(8,128)(2,1)S(1)} %collective-permute-done), channel_id=1, replica_groups=mesh['z'=8,'y'=8,'core'=2,'x'=4] {'core'}, dimensions={0}, use_global_device_ids=true | all-gather | bytes 1179648 | tf_op jit(solution)/shard_map/all_gather | solution.py:166
  51.2 0.0 collective-permute-done.1.temp_ref
  51.2 0.8 shard_map.53
  52.0 0.2 reshape.33
  52.1 23.7 %all_to_all.11 = bf16[128,2,896]{2,1,0:T(2,128)(2,1)S(1)} all-to-all(bf16[128,2,896]{2,1,0:T(2,128)(2,1)S(1)} %reshape.33), channel_id=1, replica_groups={{296,152,368,80,440,8,448,416,488,344,48,272,120,200,128,160,232,88,304..., dimensions={0} | all-to-all | bytes 917504 | tf_op jit(solution)/shard_map/all_to_all | solution.py:155
  75.8 0.2 reshape.34.back_ref
  76.0 0.9 %shard_map.54 = (bf16[128,768]{1,0:T(8,128)(2,1)}, bf16[1,128]{1,0:T(2,128)(2,1)}) custom-call(bf16[128,256]{1,0:T(8,128)(2,1)S(1)} %get-tuple-element.13.pick_ref, bf16[256,896]{1,0:T(8,128)(2,1)S(1)} %reshape.34.back_ref), custom_call_target="tpu_custom_call" | custom-call | flops 58720256 | bytes 721152 | tf_op jit(solution)/shard_map/pallas_call | solution.py:143
  (2 shorter events, 0.0 us)
Async XLA Ops:
  0.6 0.9 %copy-start = (bf16[128,768]{1,0:T(8,128)(2,1)S(1)}, bf16[128,768]{1,0:T(8,128)(2,1)}, u32[]{:S(2)}) copy-start(bf16[128,768]{1,0:T(8,128)(2,1)} %emb_ref.1) | copy-start | bytes 589828
  0.7 0.9 %copy-start.1 = (bf16[128]{0:T(256)(128)(2,1)S(1)}, bf16[128]{0:T(256)(128)(2,1)}, u32[]{:S(2)}) copy-start(bf16[128]{0:T(256)(128)(2,1)} %param.4) | copy-start | bytes 772
  0.7 0.9 %copy-start.2 = (s32[128,1]{0,1:T(1,128)S(1)}, s32[128,1]{0,1:T(1,128)}, u32[]{:S(2)}) copy-start(s32[128,1]{0,1:T(1,128)} %param.5) | copy-start | bytes 1540
  34.5 11.9 %collective-permute-start = (bf16[256,768]{1,0:T(8,128)(2,1)S(1)}, bf16[256,768]{1,0:T(8,128)(2,1)S(1)}, u32[]{:S(2)}, u32[]{:S(2)}) collective-permute-start(bf16[256,768]{1,0:T(8,128)(2,1)S(1)} %slice.4), channel_id=1, source_target_pairs={{0,3},{1,2},{2,1},{3,0},{4,7},{5,6},{6,5},{7,4},{8,11},{9,10},{10,... | collective-permute-start | bytes 1179656 | tf_op jit(solution)/shard_map/ppermute | solution.py:188
  44.2 6.9 %collective-permute-start.1 = (f32[8,512]{1,0:T(8,128)S(1)}, f32[8,512]{1,0:T(8,128)S(1)}, u32[]{:S(2)}, u32[]{:S(2)}) collective-permute-start(f32[8,512]{1,0:T(8,128)S(1)} %get-tuple-element.15), channel_id=1, source_target_pairs={{0,3},{1,2},{2,1},{3,0},{4,7},{5,6},{6,5},{7,4},{8,11},{9,10},{10,... | collective-permute-start | bytes 49160 | tf_op jit(solution)/shard_map/ppermute | solution.py:201

commit v13 on v12

--- a/solution.py
+++ b/solution.py
@@ -25,10 +25,10 @@
         mid = side // 2
         steps = sorted(range(side), key=lambda step: (min(step, side - step), step))
         order = [
-            ((a + b + mid) % side, (a + mid) % side, h) for h in range(2) for b in steps for a in steps
+            ((a + b + mid) % side, (a + mid) % side, h) for b in steps for a in steps for h in (1, 0)
         ]
-        first_out = order.index((side - 1, mid + 1, 0))
-        first_back = order.index((mid, mid + 1, 0))
+        first_out = order.index((side - 1, mid + 1, 1))
+        first_back = order.index((mid, mid + 1, 1))
         self.count = len(order)
         self.shift = (first_out - first_back) % self.count
 

time: 77.6 us -> 77.9 us (level)
    ppermute x1, starting transfers between devices: 4.64 us -> 3.73 us  [shards(): far = lax.ppermute(query[:, :width], 'x', layout.pairs)]
  transfers between devices with their start and end apart: 2 -> 2, of which waited for: 0 -> 1; matrix products, arithmetic and copies ran while one was open for 0% -> 0% of each run, Pallas kernels for 1% -> 1%
where the time goes in v13:
time: 77.9 us; the launch traced here: 77.7 us
  blocking collectives  65.4 us (84%)
  starting transfers between devices  6.49 us (8%)
  Pallas kernels  2.92 us (4%)
  local copies, waits for them, and re-layouts  1.61 us (2%)
    all_to_all x2, blocking collectives, exchange(): lax.all_to_all(slots.reshape(count // 2, 2, wide), AXES, split_axis=0, co...  56.6 us
    all_gather x2, blocking collectives, both_cores(): return lax.all_gather(rows, 'core', axis=0, tiled=True)  8.75 us
    ppermute x1, starting transfers between devices, shards(): far = lax.ppermute(query[:, :width], 'x', layout.pairs)  3.73 us
    pallas_call x5, Pallas kernels, call(): pl.pallas_call(kernel, out_shape=shapes, in_specs=[pl.BlockSpec(memory_sp...  2.92 us
    ppermute x1, starting transfers between devices, shards(): far_temps = lax.ppermute(temps, 'x', layout.pairs)  2.76 us
  transfers between devices with their start and end apart: 2, of which 1 were waited for; matrix products, arithmetic and copies ran while one was open for 0% of the time, Pallas kernels for 1%

profile of v13, /device:TPU:1, one launch (start us, length us, event | category | flops | bytes accessed | tf_op | source)
XLA Modules:
  0.0 77.7 jit_solution(5081516629971735786)
XLA Ops:
  0.6 0.0 copy-start
  0.7 0.0 copy-start.1
  0.7 0.0 copy-start.2
  0.7 0.9 %copy-done = bf16[128,768]{1,0:T(8,128)(2,1)S(1)} copy-done((bf16[128,768]{1,0:T(8,128)(2,1)S(1)}, bf16[128,768]{1,0:T(8,128)(2,1)}, u32[]{:S(2)}) %copy-start) | copy-done | bytes 196632
  1.6 0.0 copy-done.1
  1.6 0.0 copy-done.2
  1.6 0.4 shard_map.51
  2.0 0.2 reshape.30
  2.1 32.9 %all_to_all.10 = bf16[128,2,896]{2,1,0:T(2,128)(2,1)S(1)} all-to-all(bf16[128,2,896]{2,1,0:T(2,128)(2,1)S(1)} %reshape.30), channel_id=1, replica_groups={{489,488,345,344,49,48,273,272,121,120,201,200,129,128,161,160,233,232,..., dimensions={0} | all-to-all | bytes 917504 | tf_op jit(solution)/shard_map/all_to_all | solution.py:155
  35.1 0.2 reshape.31.query_ref
  35.3 3.7 %collective-permute-start = (bf16[256,768]{1,0:T(8,128)(2,1)S(1)}, bf16[256,768]{1,0:T(8,128)(2,1)S(1)}, u32[]{:S(2)}, u32[]{:S(2)}) collective-permute-start(bf16[256,768]{1,0:T(8,128)(2,1)S(1)} %slice.4), channel_id=1, source_target_pairs={{0,3},{1,2},{2,1},{3,0},{4,7},{5,6},{6,5},{7,4},{8,11},{9,10},{10,... | collective-permute-start | bytes 1179656 | tf_op jit(solution)/shard_map/ppermute | solution.py:188
  39.0 4.1 %all_gather.7.key_ref = bf16[512,896]{1,0:T(8,128)(2,1)S(1)} all-gather(bf16[256,896]{1,0:T(8,128)(2,1)S(1)} %reshape.31.query_ref), channel_id=1, replica_groups=mesh['z'=8,'y'=8,'core'=2,'x'=4] {'core'}, dimensions={0}, use_global_device_ids=true | all-gather | bytes 1376256 | tf_op jit(solution)/shard_map/all_gather | solution.py:166
  43.1 0.8 %shard_map.52 = (f32[256,128]{1,0:T(8,128)S(1)}, f32[256,768]{1,0:T(8,128)S(1)}, f32[8,512]{1,0:T(8,128)S(1)}) custom-call(s32[1]{0:T(128)} %bitcast.2.core_ref, bf16[256,896]{1,0:T(8,128)(2,1)S(1)} %reshape.31.query_ref, bf16[512,896]{1,0:T(8,128)(2,1)S(1)} %all_gather.7.key_ref), custom_call_target="tpu_custom_call" | custom-call | flops 402653184 | bytes 2310148 | tf_op jit(solution)/shard_map/pallas_call | solution.py:143
  44.0 2.8 %collective-permute-start.1 = (f32[8,512]{1,0:T(8,128)S(1)}, f32[8,512]{1,0:T(8,128)S(1)}, u32[]{:S(2)}, u32[]{:S(2)}) collective-permute-start(f32[8,512]{1,0:T(8,128)S(1)} %get-tuple-element.15), channel_id=1, source_target_pairs={{0,3},{1,2},{2,1},{3,0},{4,7},{5,6},{6,5},{7,4},{8,11},{9,10},{10,... | collective-permute-start | bytes 49160 | tf_op jit(solution)/shard_map/ppermute | solution.py:201
  46.7 0.5 collective-permute-done
  47.3 4.6 %all_gather.6.unit_ref = bf16[512,768]{1,0:T(8,128)(2,1)S(1)} all-gather(bf16[256,768]{1,0:T(8,128)(2,1)S(1)} %collective-permute-done), channel_id=1, replica_groups=mesh['z'=8,'y'=8,'core'=2,'x'=4] {'core'}, dimensions={0}, use_global_device_ids=true | all-gather | bytes 1179648 | tf_op jit(solution)/shard_map/all_gather | solution.py:166
  51.9 0.0 collective-permute-done.1.temp_ref
  51.9 0.8 shard_map.53
  52.7 0.2 reshape.33
  52.9 23.7 %all_to_all.11 = bf16[128,2,896]{2,1,0:T(2,128)(2,1)S(1)} all-to-all(bf16[128,2,896]{2,1,0:T(2,128)(2,1)S(1)} %reshape.33), channel_id=1, replica_groups={{297,296,153,152,369,368,81,80,441,440,9,8,449,448,417,416,489,488,345,..., dimensions={0} | all-to-all | bytes 917504 | tf_op jit(solution)/shard_map/all_to_all | solution.py:155
  76.5 0.2 reshape.34.back_ref
  76.7 0.9 %shard_map.54 = (bf16[128,768]{1,0:T(8,128)(2,1)}, bf16[1,128]{1,0:T(2,128)(2,1)}) custom-call(bf16[128,256]{1,0:T(8,128)(2,1)S(1)} %get-tuple-element.13.pick_ref, bf16[256,896]{1,0:T(8,128)(2,1)S(1)} %reshape.34.back_ref), custom_call_target="tpu_custom_call" | custom-call | flops 58720256 | bytes 721152 | tf_op jit(solution)/shard_map/pallas_call | solution.py:143
  (2 shorter events, 0.0 us)
Async XLA Ops:
  0.6 0.9 %copy-start = (bf16[128,768]{1,0:T(8,128)(2,1)S(1)}, bf16[128,768]{1,0:T(8,128)(2,1)}, u32[]{:S(2)}) copy-start(bf16[128,768]{1,0:T(8,128)(2,1)} %emb_ref.1) | copy-start | bytes 589828
  0.7 0.9 %copy-start.1 = (bf16[128]{0:T(256)(128)(2,1)S(1)}, bf16[128]{0:T(256)(128)(2,1)}, u32[]{:S(2)}) copy-start(bf16[128]{0:T(256)(128)(2,1)} %param.4) | copy-start | bytes 772
  0.7 0.9 %copy-start.2 = (s32[128,1]{0,1:T(1,128)S(1)}, s32[128,1]{0,1:T(1,128)}, u32[]{:S(2)}) copy-start(s32[128,1]{0,1:T(1,128)} %param.5) | copy-start | bytes 1540
  35.3 12.0 %collective-permute-start = (bf16[256,768]{1,0:T(8,128)(2,1)S(1)}, bf16[256,768]{1,0:T(8,128)(2,1)S(1)}, u32[]{:S(2)}, u32[]{:S(2)}) collective-permute-start(bf16[256,768]{1,0:T(8,128)(2,1)S(1)} %slice.4), channel_id=1, source_target_pairs={{0,3},{1,2},{2,1},{3,0},{4,7},{5,6},{6,5},{7,4},{8,11},{9,10},{10,... | collective-permute-start | bytes 1179656 | tf_op jit(solution)/shard_map/ppermute | solution.py:188
  44.0 8.0 %collective-permute-start.1 = (f32[8,512]{1,0:T(8,128)S(1)}, f32[8,512]{1,0:T(8,128)S(1)}, u32[]{:S(2)}, u32[]{:S(2)}) collective-permute-start(f32[8,512]{1,0:T(8,128)S(1)} %get-tuple-element.15), channel_id=1, source_target_pairs={{0,3},{1,2},{2,1},{3,0},{4,7},{5,6},{6,5},{7,4},{8,11},{9,10},{10,... | collective-permute-start | bytes 49160 | tf_op jit(solution)/shard_map/ppermute | solution.py:201

commit v14 on v12

--- a/solution.py
+++ b/solution.py
@@ -61,7 +61,7 @@
     shift, emb_ref, temp_ref, cluster_ref, same_ref, before_ref, send_ref, pick_ref
 ):
     rows, width = emb_ref.shape
-    slots = send_ref.shape[0]
+    slots = pick_ref.shape[1]
 
     cluster_row = cluster_ref[...].astype(jnp.float32)
     before = before_ref[...]
@@ -78,7 +78,8 @@
 
     put = lax.broadcasted_iota(jnp.int32, (slots, rows), 0) == slot_row
     temp = jnp.sum(jnp.where(put, temp_ref[...].astype(jnp.float32), 0.0), axis=1, keepdims=True)
-    send_ref[:, width:] = jnp.broadcast_to(temp, (slots, EXT)).astype(jnp.bfloat16)
+    temp = jnp.broadcast_to(temp, (slots, EXT)).astype(jnp.bfloat16)
+    send_ref[:, :, width:] = temp.reshape(slots // 2, 2, EXT)
 
     values = emb_ref[...].astype(jnp.float32)
     square_mean = jnp.mean(values * values, axis=1, keepdims=True)
@@ -86,7 +87,7 @@
     placed = jnp.dot(
         jnp.where(put, 1.0, 0.0).astype(jnp.bfloat16), unit, preferred_element_type=jnp.float32
     )
-    send_ref[:, :width] = placed.astype(jnp.bfloat16)
+    send_ref[:, :, :width] = placed.astype(jnp.bfloat16).reshape(slots // 2, 2, width)
 
 
 def weigh(query_ref, unit, key_temp, own_start):
@@ -123,13 +124,16 @@
     mass = jnp.broadcast_to(mass, (slots, EXT))
     moved = 2 * shift
     for source, target, count in ((0, moved, slots - moved), (slots - moved, 0, moved)):
-        out_ref[target : target + count, :width] = neigh[source : source + count].astype(jnp.bfloat16)
-        out_ref[target : target + count, width:] = mass[source : source + count].astype(jnp.bfloat16)
+        pairs = pl.ds(target // 2, count // 2)
+        for values, columns in ((neigh, slice(0, width)), (mass, slice(width, width + EXT))):
+            part = values[source : source + count].astype(jnp.bfloat16)
+            out_ref[pairs, :, columns] = part.reshape(count // 2, 2, part.shape[1])
 
 
 def unpack_kernel(pick_ref, back_ref, neigh_ref, mass_ref):
     width = neigh_ref.shape[1]
-    rows = jnp.dot(pick_ref[...], back_ref[...], preferred_element_type=jnp.float32)
+    back = back_ref[...].reshape(pick_ref.shape[1], back_ref.shape[2])
+    rows = jnp.dot(pick_ref[...], back, preferred_element_type=jnp.float32)
     rows = rows.astype(jnp.bfloat16)
     neigh_ref[...] = rows[:, :width]
     mass_ref[...] = lane_to_row(rows[:, width:]).astype(jnp.bfloat16)
@@ -150,15 +154,9 @@
     )(*args)
 
 
-def exchange(slots, groups):
-    count, wide = slots.shape
+def exchange(pairs, groups):
     return lax.all_to_all(
-        slots.reshape(count // 2, 2, wide),
-        AXES,
-        split_axis=0,
-        concat_axis=0,
-        axis_index_groups=groups,
-        tiled=True,
+        pairs, AXES, split_axis=0, concat_axis=0, axis_index_groups=groups, tiled=True
     )
 
 
@@ -175,7 +173,7 @@
     same, before = call(order_kernel, [((rows, rows), f32)] * 2, 8 * rows * rows * rows * rows)
     send, pick = call(
         functools.partial(pack_kernel, layout.shift),
-        [((slots, wide), bf16), ((rows, slots), bf16)],
+        [((slots // 2, 2, wide), bf16), ((rows, slots), bf16)],
         2 * slots * rows * width,
         embeddings,
         inv_temp.reshape(1, rows),
@@ -202,7 +200,7 @@
     far_keys = both_cores(far)
     (result,) = call(
         functools.partial(last_kernel, layout.shift),
-        [((slots, wide), bf16)],
+        [((slots // 2, 2, wide), bf16)],
         work,
         query,
         far_keys,
@@ -211,7 +209,7 @@
         near,
     )
 
-    back = exchange(result, layout.back).reshape(slots, wide)
+    back = exchange(result, layout.back)
     neigh, dup = call(
         unpack_kernel,
         [((rows, width), bf16), ((1, rows), bf16)],

time: 77.6 us -> 77.1 us (level)
  no operation moved by 1% of the time
where the time goes in v14:
time: 77.1 us; the launch traced here: 76.5 us
  blocking collectives  64.9 us (84%)
  starting transfers between devices  6.75 us (9%)
  Pallas kernels  2.97 us (4%)
  local copies, waits for them, and re-layouts  1.09 us (1%)
    all_to_all x2, blocking collectives, exchange(): lax.all_to_all(pairs, AXES, split_axis=0, concat_axis=0, axis_index_group...  55.8 us
    all_gather x2, blocking collectives, both_cores(): return lax.all_gather(rows, 'core', axis=0, tiled=True)  9.08 us
    ppermute x1, starting transfers between devices, shards(): far = lax.ppermute(query[:, :width], 'x', layout.pairs)  4.64 us
    pallas_call x5, Pallas kernels, call(): pl.pallas_call(kernel, out_shape=shapes, in_specs=[pl.BlockSpec(memory_sp...  2.97 us
    ppermute x1, starting transfers between devices, shards(): far_temps = lax.ppermute(temps, 'x', layout.pairs)  2.12 us
  transfers between devices with their start and end apart: 2, of which 0 were waited for; matrix products, arithmetic and copies ran while one was open for 0% of the time, Pallas kernels for 1%

profile of v14, /device:TPU:1, one launch (start us, length us, event | category | flops | bytes accessed | tf_op | source)
XLA Modules:
  0.0 76.5 jit_solution(11948852759777245869)
XLA Ops:
  0.6 0.0 copy-start
  0.7 0.0 copy-start.1
  0.7 0.0 copy-start.2
  0.7 0.9 %copy-done = bf16[128,768]{1,0:T(8,128)(2,1)S(1)} copy-done((bf16[128,768]{1,0:T(8,128)(2,1)S(1)}, bf16[128,768]{1,0:T(8,128)(2,1)}, u32[]{:S(2)}) %copy-start) | copy-done | bytes 196632
  1.6 0.0 copy-done.1
  1.6 0.0 copy-done.2
  1.6 0.4 shard_map.51
  2.0 32.2 %all_to_all.10 = bf16[128,2,896]{2,1,0:T(2,128)(2,1)S(1)} all-to-all(bf16[128,2,896]{2,1,0:T(2,128)(2,1)S(1)} %get-tuple-element.14), channel_id=1, replica_groups={{488,344,48,272,120,200,128,160,232,88,304,16,376,456,384,480,40,408,11..., dimensions={0} | all-to-all | bytes 917504 | tf_op jit(solution)/shard_map/all_to_all | solution.py:158
  34.1 0.2 reshape.21.query_ref
  34.3 4.6 %collective-permute-start = (bf16[256,768]{1,0:T(8,128)(2,1)S(1)}, bf16[256,768]{1,0:T(8,128)(2,1)S(1)}, u32[]{:S(2)}, u32[]{:S(2)}) collective-permute-start(bf16[256,768]{1,0:T(8,128)(2,1)S(1)} %slice.4), channel_id=1, source_target_pairs={{0,3},{1,2},{2,1},{3,0},{4,7},{5,6},{6,5},{7,4},{8,11},{9,10},{10,... | collective-permute-start | bytes 1179656 | tf_op jit(solution)/shard_map/ppermute | solution.py:186
  39.0 4.3 %all_gather.7.key_ref = bf16[512,896]{1,0:T(8,128)(2,1)S(1)} all-gather(bf16[256,896]{1,0:T(8,128)(2,1)S(1)} %reshape.21.query_ref), channel_id=1, replica_groups=mesh['z'=8,'y'=8,'core'=2,'x'=4] {'core'}, dimensions={0}, use_global_device_ids=true | all-gather | bytes 1376256 | tf_op jit(solution)/shard_map/all_gather | solution.py:164
  43.3 0.8 %shard_map.52 = (f32[256,128]{1,0:T(8,128)S(1)}, f32[256,768]{1,0:T(8,128)S(1)}, f32[8,512]{1,0:T(8,128)S(1)}) custom-call(s32[1]{0:T(128)} %bitcast.2.core_ref, bf16[256,896]{1,0:T(8,128)(2,1)S(1)} %reshape.21.query_ref, bf16[512,896]{1,0:T(8,128)(2,1)S(1)} %all_gather.7.key_ref), custom_call_target="tpu_custom_call" | custom-call | flops 402653184 | bytes 2310148 | tf_op jit(solution)/shard_map/pallas_call | solution.py:147
  44.1 2.1 %collective-permute-start.1 = (f32[8,512]{1,0:T(8,128)S(1)}, f32[8,512]{1,0:T(8,128)S(1)}, u32[]{:S(2)}, u32[]{:S(2)}) collective-permute-start(f32[8,512]{1,0:T(8,128)S(1)} %get-tuple-element.15), channel_id=1, source_target_pairs={{0,3},{1,2},{2,1},{3,0},{4,7},{5,6},{6,5},{7,4},{8,11},{9,10},{10,... | collective-permute-start | bytes 49160 | tf_op jit(solution)/shard_map/ppermute | solution.py:199
  46.2 0.0 collective-permute-done
  46.2 4.8 %all_gather.6.unit_ref = bf16[512,768]{1,0:T(8,128)(2,1)S(1)} all-gather(bf16[256,768]{1,0:T(8,128)(2,1)S(1)} %collective-permute-done), channel_id=1, replica_groups=mesh['z'=8,'y'=8,'core'=2,'x'=4] {'core'}, dimensions={0}, use_global_device_ids=true | all-gather | bytes 1179648 | tf_op jit(solution)/shard_map/all_gather | solution.py:164
  51.0 0.0 collective-permute-done.1.temp_ref
  51.0 0.8 %shard_map.53 = bf16[128,2,896]{2,1,0:T(2,128)(2,1)S(1)} custom-call(bf16[256,896]{1,0:T(8,128)(2,1)S(1)} %reshape.21.query_ref, bf16[512,768]{1,0:T(8,128)(2,1)S(1)} %all_gather.6.unit_ref, f32[8,512]{1,0:T(8,128)S(1)} %collective-permute-done.1.temp_ref, f32[256,128]{1,0:T(8,128)S(1)} %get-tuple-element.16.mass_ref, f32[256,768]{1,0:T(8,128)S(1)} %get-tuple-element.17.near_ref), custom_call_target="tpu_custom_call" | custom-call | flops 402653184 | bytes 2637824 | tf_op jit(solution)/shard_map/pallas_call | solution.py:147
  51.8 23.7 %all_to_all.11.back_ref = bf16[128,2,896]{2,1,0:T(2,128)(2,1)S(1)} all-to-all(bf16[128,2,896]{2,1,0:T(2,128)(2,1)S(1)} %shard_map.53), channel_id=1, replica_groups={{296,152,368,80,440,8,448,416,488,344,48,272,120,200,128,160,232,88,304..., dimensions={0} | all-to-all | bytes 917504 | tf_op jit(solution)/shard_map/all_to_all | solution.py:158
  75.5 1.0 %shard_map.54 = (bf16[128,768]{1,0:T(8,128)(2,1)}, bf16[1,128]{1,0:T(2,128)(2,1)}) custom-call(bf16[128,256]{1,0:T(8,128)(2,1)S(1)} %get-tuple-element.13.pick_ref, bf16[128,2,896]{2,1,0:T(2,128)(2,1)S(1)} %all_to_all.11.back_ref), custom_call_target="tpu_custom_call" | custom-call | flops 58720256 | bytes 721152 | tf_op jit(solution)/shard_map/pallas_call | solution.py:147
  (2 shorter events, 0.0 us)
Async XLA Ops:
  0.6 0.9 %copy-start = (bf16[128,768]{1,0:T(8,128)(2,1)S(1)}, bf16[128,768]{1,0:T(8,128)(2,1)}, u32[]{:S(2)}) copy-start(bf16[128,768]{1,0:T(8,128)(2,1)} %emb_ref.1) | copy-start | bytes 589828
  0.7 0.9 %copy-start.1 = (bf16[128]{0:T(256)(128)(2,1)S(1)}, bf16[128]{0:T(256)(128)(2,1)}, u32[]{:S(2)}) copy-start(bf16[128]{0:T(256)(128)(2,1)} %param.4) | copy-start | bytes 772
  0.7 0.9 %copy-start.2 = (s32[128,1]{0,1:T(1,128)S(1)}, s32[128,1]{0,1:T(1,128)}, u32[]{:S(2)}) copy-start(s32[128,1]{0,1:T(1,128)} %param.5) | copy-start | bytes 1540
  34.3 11.9 %collective-permute-start = (bf16[256,768]{1,0:T(8,128)(2,1)S(1)}, bf16[256,768]{1,0:T(8,128)(2,1)S(1)}, u32[]{:S(2)}, u32[]{:S(2)}) collective-permute-start(bf16[256,768]{1,0:T(8,128)(2,1)S(1)} %slice.4), channel_id=1, source_target_pairs={{0,3},{1,2},{2,1},{3,0},{4,7},{5,6},{6,5},{7,4},{8,11},{9,10},{10,... | collective-permute-start | bytes 1179656 | tf_op jit(solution)/shard_map/ppermute | solution.py:186
  44.1 7.0 %collective-permute-start.1 = (f32[8,512]{1,0:T(8,128)S(1)}, f32[8,512]{1,0:T(8,128)S(1)}, u32[]{:S(2)}, u32[]{:S(2)}) collective-permute-start(f32[8,512]{1,0:T(8,128)S(1)} %get-tuple-element.15), channel_id=1, source_target_pairs={{0,3},{1,2},{2,1},{3,0},{4,7},{5,6},{6,5},{7,4},{8,11},{9,10},{10,... | collective-permute-start | bytes 49160 | tf_op jit(solution)/shard_map/ppermute | solution.py:199

commit v15 on v14

--- a/solution.py
+++ b/solution.py
@@ -27,8 +27,11 @@
         order = [
             ((a + b + mid) % side, (a + mid) % side, h) for h in range(2) for b in steps for a in steps
         ]
-        first_out = order.index((side - 1, mid + 1, 0))
+        first_out = order.index((side - 1, mid, 0))
         first_back = order.index((mid, mid + 1, 0))
+        apart = (first_back - first_out) % 8
+        order[first_out], order[first_out + apart] = order[first_out + apart], order[first_out]
+        first_out += apart
         self.count = len(order)
         self.shift = (first_out - first_back) % self.count
 

time: 77.1 us -> 77.9 us (1.010)
    all_to_all x2, blocking collectives: 55.8 us -> 56.7 us  [exchange(): lax.all_to_all(pairs, AXES, split_axis=0, concat_axis=0, axis_index_group...]
  transfers between devices with their start and end apart: 2 -> 2, of which waited for: 0 -> 1; matrix products, arithmetic and copies ran while one was open for 0% -> 0% of each run, Pallas kernels for 1% -> 1%
where the time goes in v15:
time: 77.9 us; the launch traced here: 77.3 us
  blocking collectives  65.3 us (84%)
  starting transfers between devices  6.48 us (8%)
  Pallas kernels  2.98 us (4%)
  local copies, waits for them, and re-layouts  1.09 us (1%)
    all_to_all x2, blocking collectives, exchange(): lax.all_to_all(pairs, AXES, split_axis=0, concat_axis=0, axis_index_group...  56.7 us
    all_gather x2, blocking collectives, both_cores(): return lax.all_gather(rows, 'core', axis=0, tiled=True)  8.58 us
    ppermute x1, starting transfers between devices, shards(): far = lax.ppermute(query[:, :width], 'x', layout.pairs)  4.38 us
    pallas_call x5, Pallas kernels, call(): pl.pallas_call(kernel, out_shape=shapes, in_specs=[pl.BlockSpec(memory_sp...  2.98 us
    ppermute x1, starting transfers between devices, shards(): far_temps = lax.ppermute(temps, 'x', layout.pairs)  2.1 us
  transfers between devices with their start and end apart: 2, of which 1 were waited for; matrix products, arithmetic and copies ran while one was open for 0% of the time, Pallas kernels for 1%

profile of v15, /device:TPU:1, one launch (start us, length us, event | category | flops | bytes accessed | tf_op | source)
XLA Modules:
  0.0 77.3 jit_solution(499040172174884787)
XLA Ops:
  0.6 0.0 copy-start
  0.7 0.0 copy-start.1
  0.7 0.0 copy-start.2
  0.7 0.9 %copy-done = bf16[128,768]{1,0:T(8,128)(2,1)S(1)} copy-done((bf16[128,768]{1,0:T(8,128)(2,1)S(1)}, bf16[128,768]{1,0:T(8,128)(2,1)}, u32[]{:S(2)}) %copy-start) | copy-done | bytes 196632
  1.6 0.0 copy-done.1
  1.6 0.0 copy-done.2
  1.6 0.4 shard_map.51
  2.0 32.7 %all_to_all.10 = bf16[128,2,896]{2,1,0:T(2,128)(2,1)S(1)} all-to-all(bf16[128,2,896]{2,1,0:T(2,128)(2,1)S(1)} %get-tuple-element.14), channel_id=1, replica_groups={{480,408,112,336,184,264,192,96,168,24,240,464,312,392,320,32,104,472,1..., dimensions={0} | all-to-all | bytes 917504 | tf_op jit(solution)/shard_map/all_to_all | solution.py:161
  34.6 0.2 reshape.21.query_ref
  34.8 4.4 %collective-permute-start = (bf16[256,768]{1,0:T(8,128)(2,1)S(1)}, bf16[256,768]{1,0:T(8,128)(2,1)S(1)}, u32[]{:S(2)}, u32[]{:S(2)}) collective-permute-start(bf16[256,768]{1,0:T(8,128)(2,1)S(1)} %slice.4), channel_id=1, source_target_pairs={{0,3},{1,2},{2,1},{3,0},{4,7},{5,6},{6,5},{7,4},{8,11},{9,10},{10,... | collective-permute-start | bytes 1179656 | tf_op jit(solution)/shard_map/ppermute | solution.py:189
  39.2 4.0 %all_gather.7.key_ref = bf16[512,896]{1,0:T(8,128)(2,1)S(1)} all-gather(bf16[256,896]{1,0:T(8,128)(2,1)S(1)} %reshape.21.query_ref), channel_id=1, replica_groups=mesh['z'=8,'y'=8,'core'=2,'x'=4] {'core'}, dimensions={0}, use_global_device_ids=true | all-gather | bytes 1376256 | tf_op jit(solution)/shard_map/all_gather | solution.py:167
  43.3 0.8 %shard_map.52 = (f32[256,128]{1,0:T(8,128)S(1)}, f32[256,768]{1,0:T(8,128)S(1)}, f32[8,512]{1,0:T(8,128)S(1)}) custom-call(s32[1]{0:T(128)} %bitcast.2.core_ref, bf16[256,896]{1,0:T(8,128)(2,1)S(1)} %reshape.21.query_ref, bf16[512,896]{1,0:T(8,128)(2,1)S(1)} %all_gather.7.key_ref), custom_call_target="tpu_custom_call" | custom-call | flops 402653184 | bytes 2310148 | tf_op jit(solution)/shard_map/pallas_call | solution.py:150
  44.1 2.1 %collective-permute-start.1 = (f32[8,512]{1,0:T(8,128)S(1)}, f32[8,512]{1,0:T(8,128)S(1)}, u32[]{:S(2)}, u32[]{:S(2)}) collective-permute-start(f32[8,512]{1,0:T(8,128)S(1)} %get-tuple-element.15), channel_id=1, source_target_pairs={{0,3},{1,2},{2,1},{3,0},{4,7},{5,6},{6,5},{7,4},{8,11},{9,10},{10,... | collective-permute-start | bytes 49160 | tf_op jit(solution)/shard_map/ppermute | solution.py:202
  46.2 0.7 collective-permute-done
  46.9 4.6 %all_gather.6.unit_ref = bf16[512,768]{1,0:T(8,128)(2,1)S(1)} all-gather(bf16[256,768]{1,0:T(8,128)(2,1)S(1)} %collective-permute-done), channel_id=1, replica_groups=mesh['z'=8,'y'=8,'core'=2,'x'=4] {'core'}, dimensions={0}, use_global_device_ids=true | all-gather | bytes 1179648 | tf_op jit(solution)/shard_map/all_gather | solution.py:167
  51.5 0.0 collective-permute-done.1.temp_ref
  51.5 0.8 %shard_map.53 = bf16[128,2,896]{2,1,0:T(2,128)(2,1)S(1)} custom-call(bf16[256,896]{1,0:T(8,128)(2,1)S(1)} %reshape.21.query_ref, bf16[512,768]{1,0:T(8,128)(2,1)S(1)} %all_gather.6.unit_ref, f32[8,512]{1,0:T(8,128)S(1)} %collective-permute-done.1.temp_ref, f32[256,128]{1,0:T(8,128)S(1)} %get-tuple-element.16.mass_ref, f32[256,768]{1,0:T(8,128)S(1)} %get-tuple-element.17.near_ref), custom_call_target="tpu_custom_call" | custom-call | flops 402653184 | bytes 2637824 | tf_op jit(solution)/shard_map/pallas_call | solution.py:150
  52.3 24.1 %all_to_all.11.back_ref = bf16[128,2,896]{2,1,0:T(2,128)(2,1)S(1)} all-to-all(bf16[128,2,896]{2,1,0:T(2,128)(2,1)S(1)} %shard_map.53), channel_id=1, replica_groups={{296,152,368,80,440,8,448,416,488,344,48,272,120,200,128,160,232,88,304..., dimensions={0} | all-to-all | bytes 917504 | tf_op jit(solution)/shard_map/all_to_all | solution.py:161
  76.3 1.0 %shard_map.54 = (bf16[128,768]{1,0:T(8,128)(2,1)}, bf16[1,128]{1,0:T(2,128)(2,1)}) custom-call(bf16[128,256]{1,0:T(8,128)(2,1)S(1)} %get-tuple-element.13.pick_ref, bf16[128,2,896]{2,1,0:T(2,128)(2,1)S(1)} %all_to_all.11.back_ref), custom_call_target="tpu_custom_call" | custom-call | flops 58720256 | bytes 721152 | tf_op jit(solution)/shard_map/pallas_call | solution.py:150
  (2 shorter events, 0.0 us)
Async XLA Ops:
  0.6 0.9 %copy-start = (bf16[128,768]{1,0:T(8,128)(2,1)S(1)}, bf16[128,768]{1,0:T(8,128)(2,1)}, u32[]{:S(2)}) copy-start(bf16[128,768]{1,0:T(8,128)(2,1)} %emb_ref.1) | copy-start | bytes 589828
  0.7 0.9 %copy-start.1 = (bf16[128]{0:T(256)(128)(2,1)S(1)}, bf16[128]{0:T(256)(128)(2,1)}, u32[]{:S(2)}) copy-start(bf16[128]{0:T(256)(128)(2,1)} %param.4) | copy-start | bytes 772
  0.7 0.9 %copy-start.2 = (s32[128,1]{0,1:T(1,128)S(1)}, s32[128,1]{0,1:T(1,128)}, u32[]{:S(2)}) copy-start(s32[128,1]{0,1:T(1,128)} %param.5) | copy-start | bytes 1540
  34.8 12.1 %collective-permute-start = (bf16[256,768]{1,0:T(8,128)(2,1)S(1)}, bf16[256,768]{1,0:T(8,128)(2,1)S(1)}, u32[]{:S(2)}, u32[]{:S(2)}) collective-permute-start(bf16[256,768]{1,0:T(8,128)(2,1)S(1)} %slice.4), channel_id=1, source_target_pairs={{0,3},{1,2},{2,1},{3,0},{4,7},{5,6},{6,5},{7,4},{8,11},{9,10},{10,... | collective-permute-start | bytes 1179656 | tf_op jit(solution)/shard_map/ppermute | solution.py:189
  44.1 7.4 %collective-permute-start.1 = (f32[8,512]{1,0:T(8,128)S(1)}, f32[8,512]{1,0:T(8,128)S(1)}, u32[]{:S(2)}, u32[]{:S(2)}) collective-permute-start(f32[8,512]{1,0:T(8,128)S(1)} %get-tuple-element.15), channel_id=1, source_target_pairs={{0,3},{1,2},{2,1},{3,0},{4,7},{5,6},{6,5},{7,4},{8,11},{9,10},{10,... | collective-permute-start | bytes 49160 | tf_op jit(solution)/shard_map/ppermute | solution.py:202

commit v16 on v14

--- a/solution.py
+++ b/solution.py
@@ -27,8 +27,8 @@
         order = [
             ((a + b + mid) % side, (a + mid) % side, h) for h in range(2) for b in steps for a in steps
         ]
-        first_out = order.index((side - 1, mid + 1, 0))
-        first_back = order.index((mid, mid + 1, 0))
+        first_out = order.index((side - 1, mid + 2, 0))
+        first_back = order.index((mid, mid + 2, 0))
         self.count = len(order)
         self.shift = (first_out - first_back) % self.count
 

time: 77.1 us -> 78 us (1.012)
  blocking collectives: 64.9 us -> 66.4 us
    all_to_all x2, blocking collectives: 55.8 us -> 57.2 us  [exchange(): lax.all_to_all(pairs, AXES, split_axis=0, concat_axis=0, axis_index_group...]
    ppermute x1, starting transfers between devices: 4.64 us -> 3.84 us  [shards(): far = lax.ppermute(query[:, :width], 'x', layout.pairs)]
where the time goes in v16:
time: 78 us; the launch traced here: 77.8 us
  blocking collectives  66.4 us (85%)
  starting transfers between devices  6.52 us (8%)
  Pallas kernels  2.98 us (4%)
  local copies, waits for them, and re-layouts  1.09 us (1%)
    all_to_all x2, blocking collectives, exchange(): lax.all_to_all(pairs, AXES, split_axis=0, concat_axis=0, axis_index_group...  57.2 us
    all_gather x2, blocking collectives, both_cores(): return lax.all_gather(rows, 'core', axis=0, tiled=True)  9.25 us
    ppermute x1, starting transfers between devices, shards(): far = lax.ppermute(query[:, :width], 'x', layout.pairs)  3.84 us
    pallas_call x5, Pallas kernels, call(): pl.pallas_call(kernel, out_shape=shapes, in_specs=[pl.BlockSpec(memory_sp...  2.98 us
    ppermute x1, starting transfers between devices, shards(): far_temps = lax.ppermute(temps, 'x', layout.pairs)  2.68 us
  transfers between devices with their start and end apart: 2, of which 0 were waited for; matrix products, arithmetic and copies ran while one was open for 0% of the time, Pallas kernels for 1%

profile of v16, /device:TPU:1, one launch (start us, length us, event | category | flops | bytes accessed | tf_op | source)
XLA Modules:
  0.0 77.8 jit_solution(6453041665232925642)
XLA Ops:
  0.6 0.0 copy-start
  0.7 0.0 copy-start.1
  0.7 0.0 copy-start.2
  0.7 0.9 %copy-done = bf16[128,768]{1,0:T(8,128)(2,1)S(1)} copy-done((bf16[128,768]{1,0:T(8,128)(2,1)S(1)}, bf16[128,768]{1,0:T(8,128)(2,1)}, u32[]{:S(2)}) %copy-start) | copy-done | bytes 196632
  1.6 0.0 copy-done.1
  1.6 0.0 copy-done.2
  1.6 0.4 shard_map.51
  2.0 32.2 %all_to_all.10 = bf16[128,2,896]{2,1,0:T(2,128)(2,1)S(1)} all-to-all(bf16[128,2,896]{2,1,0:T(2,128)(2,1)S(1)} %get-tuple-element.14), channel_id=1, replica_groups={{496,208,56,136,64,224,296,152,368,80,440,8,448,416,488,344,48,272,120,..., dimensions={0} | all-to-all | bytes 917504 | tf_op jit(solution)/shard_map/all_to_all | solution.py:158
  34.1 0.2 reshape.21.query_ref
  34.4 3.8 %collective-permute-start = (bf16[256,768]{1,0:T(8,128)(2,1)S(1)}, bf16[256,768]{1,0:T(8,128)(2,1)S(1)}, u32[]{:S(2)}, u32[]{:S(2)}) collective-permute-start(bf16[256,768]{1,0:T(8,128)(2,1)S(1)} %slice.4), channel_id=1, source_target_pairs={{0,3},{1,2},{2,1},{3,0},{4,7},{5,6},{6,5},{7,4},{8,11},{9,10},{10,... | collective-permute-start | bytes 1179656 | tf_op jit(solution)/shard_map/ppermute | solution.py:186
  38.2 4.4 %all_gather.7.key_ref = bf16[512,896]{1,0:T(8,128)(2,1)S(1)} all-gather(bf16[256,896]{1,0:T(8,128)(2,1)S(1)} %reshape.21.query_ref), channel_id=1, replica_groups=mesh['z'=8,'y'=8,'core'=2,'x'=4] {'core'}, dimensions={0}, use_global_device_ids=true | all-gather | bytes 1376256 | tf_op jit(solution)/shard_map/all_gather | solution.py:164
  42.6 0.8 %shard_map.52 = (f32[256,128]{1,0:T(8,128)S(1)}, f32[256,768]{1,0:T(8,128)S(1)}, f32[8,512]{1,0:T(8,128)S(1)}) custom-call(s32[1]{0:T(128)} %bitcast.2.core_ref, bf16[256,896]{1,0:T(8,128)(2,1)S(1)} %reshape.21.query_ref, bf16[512,896]{1,0:T(8,128)(2,1)S(1)} %all_gather.7.key_ref), custom_call_target="tpu_custom_call" | custom-call | flops 402653184 | bytes 2310148 | tf_op jit(solution)/shard_map/pallas_call | solution.py:147
  43.4 2.7 %collective-permute-start.1 = (f32[8,512]{1,0:T(8,128)S(1)}, f32[8,512]{1,0:T(8,128)S(1)}, u32[]{:S(2)}, u32[]{:S(2)}) collective-permute-start(f32[8,512]{1,0:T(8,128)S(1)} %get-tuple-element.15), channel_id=1, source_target_pairs={{0,3},{1,2},{2,1},{3,0},{4,7},{5,6},{6,5},{7,4},{8,11},{9,10},{10,... | collective-permute-start | bytes 49160 | tf_op jit(solution)/shard_map/ppermute | solution.py:199
  46.1 0.0 collective-permute-done
  46.1 4.9 %all_gather.6.unit_ref = bf16[512,768]{1,0:T(8,128)(2,1)S(1)} all-gather(bf16[256,768]{1,0:T(8,128)(2,1)S(1)} %collective-permute-done), channel_id=1, replica_groups=mesh['z'=8,'y'=8,'core'=2,'x'=4] {'core'}, dimensions={0}, use_global_device_ids=true | all-gather | bytes 1179648 | tf_op jit(solution)/shard_map/all_gather | solution.py:164
  51.0 0.0 collective-permute-done.1.temp_ref
  51.0 0.8 %shard_map.53 = bf16[128,2,896]{2,1,0:T(2,128)(2,1)S(1)} custom-call(bf16[256,896]{1,0:T(8,128)(2,1)S(1)} %reshape.21.query_ref, bf16[512,768]{1,0:T(8,128)(2,1)S(1)} %all_gather.6.unit_ref, f32[8,512]{1,0:T(8,128)S(1)} %collective-permute-done.1.temp_ref, f32[256,128]{1,0:T(8,128)S(1)} %get-tuple-element.16.mass_ref, f32[256,768]{1,0:T(8,128)S(1)} %get-tuple-element.17.near_ref), custom_call_target="tpu_custom_call" | custom-call | flops 402653184 | bytes 2637824 | tf_op jit(solution)/shard_map/pallas_call | solution.py:147
  51.8 25.0 %all_to_all.11.back_ref = bf16[128,2,896]{2,1,0:T(2,128)(2,1)S(1)} all-to-all(bf16[128,2,896]{2,1,0:T(2,128)(2,1)S(1)} %shard_map.53), channel_id=1, replica_groups={{304,16,376,456,384,480,40,408,112,336,184,264,192,96,168,24,240,464,31..., dimensions={0} | all-to-all | bytes 917504 | tf_op jit(solution)/shard_map/all_to_all | solution.py:158
  76.8 1.0 %shard_map.54 = (bf16[128,768]{1,0:T(8,128)(2,1)}, bf16[1,128]{1,0:T(2,128)(2,1)}) custom-call(bf16[128,256]{1,0:T(8,128)(2,1)S(1)} %get-tuple-element.13.pick_ref, bf16[128,2,896]{2,1,0:T(2,128)(2,1)S(1)} %all_to_all.11.back_ref), custom_call_target="tpu_custom_call" | custom-call | flops 58720256 | bytes 721152 | tf_op jit(solution)/shard_map/pallas_call | solution.py:147
  (2 shorter events, 0.0 us)
Async XLA Ops:
  0.6 0.9 %copy-start = (bf16[128,768]{1,0:T(8,128)(2,1)S(1)}, bf16[128,768]{1,0:T(8,128)(2,1)}, u32[]{:S(2)}) copy-start(bf16[128,768]{1,0:T(8,128)(2,1)} %emb_ref.1) | copy-start | bytes 589828
  0.7 0.9 %copy-start.1 = (bf16[128]{0:T(256)(128)(2,1)S(1)}, bf16[128]{0:T(256)(128)(2,1)}, u32[]{:S(2)}) copy-start(bf16[128]{0:T(256)(128)(2,1)} %param.4) | copy-start | bytes 772
  0.7 0.9 %copy-start.2 = (s32[128,1]{0,1:T(1,128)S(1)}, s32[128,1]{0,1:T(1,128)}, u32[]{:S(2)}) copy-start(s32[128,1]{0,1:T(1,128)} %param.5) | copy-start | bytes 1540
  34.4 11.7 %collective-permute-start = (bf16[256,768]{1,0:T(8,128)(2,1)S(1)}, bf16[256,768]{1,0:T(8,128)(2,1)S(1)}, u32[]{:S(2)}, u32[]{:S(2)}) collective-permute-start(bf16[256,768]{1,0:T(8,128)(2,1)S(1)} %slice.4), channel_id=1, source_target_pairs={{0,3},{1,2},{2,1},{3,0},{4,7},{5,6},{6,5},{7,4},{8,11},{9,10},{10,... | collective-permute-start | bytes 1179656 | tf_op jit(solution)/shard_map/ppermute | solution.py:186
  43.4 7.6 %collective-permute-start.1 = (f32[8,512]{1,0:T(8,128)S(1)}, f32[8,512]{1,0:T(8,128)S(1)}, u32[]{:S(2)}, u32[]{:S(2)}) collective-permute-start(f32[8,512]{1,0:T(8,128)S(1)} %get-tuple-element.15), channel_id=1, source_target_pairs={{0,3},{1,2},{2,1},{3,0},{4,7},{5,6},{6,5},{7,4},{8,11},{9,10},{10,... | collective-permute-start | bytes 49160 | tf_op jit(solution)/shard_map/ppermute | solution.py:199
